TPU v7x, 128 devices: a whole 4x4x4 slice. The times are simulated.
128 devices in a mesh: wide: 16 (over x, y), narrow: 8 (over z, core).
Axes of the slice: x: 4, y: 4, z: 4, core: 2. Of those that a mesh axis runs over, the one named last changes fastest.
Arguments:
- potential: float32 [8, 256, 256, 128], P(None, 'wide', 'narrow'), may hold values from -6 to 6
- source_current: float32 [3, 256, 256, 128], P(None, 'wide', 'narrow'), may hold values from -6 to 6
- cell_label: int32 [256, 256, 128], P('wide', 'narrow'), may hold values from 0 to 47
- region_kappa: float32 [16], replicated, may hold values from 0.5 to 4
- send_lines: int32 [128, 128, 4], P(('wide', 'narrow')), may hold values from 0 to 511, as said below
- recv_slot: int32 [128, 256], P(('wide', 'narrow')), may hold values from 0 to 511, as said below
- velocity: float32 [3, 128, 256, 128], P(None, 'wide', 'narrow'), may hold values from -6 to 6
Outputs:
- potential_next: float32 [8, 256, 256, 128], P(None, 'wide', 'narrow')
- les_force: bfloat16 [3, 128, 256, 128], P(None, 'wide', 'narrow')
- velocity_next: float32 [3, 128, 256, 128], P(None, 'wide', 'narrow')
Inputs may be any that keep to these rules, and one draw needn't show every extreme that they name: send_lines[e, l, c] is a line of device e's EM block; over the pairs that recv_slot uses, each line of device e is named at most once. `recv_slot`: each device l reads all 4 slots of each of 64 source devices, each slot for exactly one of its LES lines.
All inputs are finite; a program needn't handle non-finite values.
Results may differ from a plain program's by a relative error of at most 0.001.
Values may be sent and summed in bfloat16 or wider, within the bound.
No kernel may reach another device: no remote copies, remote signals or barrier semaphores. Data moves between devices by JAX's collectives and lax.ppermute only.
A program may use at most 64 MiB of HBM per device.

v0:
```python
import jax
import jax.numpy as jnp
from jax import lax
from jax.sharding import PartitionSpec as P

DT = 0.25
VISC = 0.5


def extended(block, sides, width):
    for axis, dim in sides:
        count = lax.axis_size(axis)
        forward = [(i, i + 1) for i in range(count - 1)]
        backward = [(target, source) for source, target in forward]
        low = lax.ppermute(
            lax.slice_in_dim(block, block.shape[dim] - width, None, axis=dim), axis, forward
        )
        high = lax.ppermute(lax.slice_in_dim(block, 0, width, axis=dim), axis, backward)
        block = jnp.concatenate([low, block, high], axis=dim)
    return block


def beside_all(q):
    ends = jnp.pad(q[1:-1, 1:-1], ((0, 0), (0, 0), (1, 1)))
    return (
        q[2:, 1:-1] + q[:-2, 1:-1] + q[1:-1, 2:] + q[1:-1, :-2] + ends[:, :, 2:] + ends[:, :, :-2]
    )


def slope(q, axis):
    if axis == 0:
        return 0.5 * (q[2:, 1:-1] - q[:-2, 1:-1])
    if axis == 1:
        return 0.5 * (q[1:-1, 2:] - q[1:-1, :-2])
    ends = jnp.pad(q[1:-1, 1:-1], ((0, 0), (0, 0), (1, 1)))
    return 0.5 * (ends[:, :, 2:] - ends[:, :, :-2])


def sweep(padded, kappa, drive):
    scale = 1.0 / (36.0 + kappa * kappa)
    div_re = slope(padded[0], 0) + slope(padded[1], 1) + slope(padded[2], 2)
    div_im = slope(padded[4], 0) + slope(padded[5], 1) + slope(padded[6], 2)
    real_parts = []
    imag_parts = []
    for comp in range(3):
        first = drive[comp] + beside_all(padded[comp]) + kappa * slope(padded[7], comp)
        second = beside_all(padded[4 + comp]) - kappa * slope(padded[3], comp)
        real_parts.append((6.0 * first + kappa * second) * scale)
        imag_parts.append((6.0 * second - kappa * first) * scale)
    first = beside_all(padded[3]) + kappa * div_im
    second = beside_all(padded[7]) - kappa * div_re
    real_parts.append((6.0 * first + kappa * second) * scale)
    imag_parts.append((6.0 * second - kappa * first) * scale)
    return jnp.stack(real_parts + imag_parts)


def curl(padded, base):
    ax_f, ay_f, az_f = (padded[base], padded[base + 1], padded[base + 2])
    return [
        slope(az_f, 1) - slope(ay_f, 2),
        slope(ax_f, 2) - slope(az_f, 0),
        slope(ay_f, 0) - slope(ax_f, 1),
    ]


def lorentz_force(padded, kappa, drive, melt):
    real_b = curl(padded, 0)
    imag_b = curl(padded, 4)
    cur_re = []
    cur_im = []
    for comp in range(3):
        field_re = padded[comp, 1:-1, 1:-1] + slope(padded[3], comp)
        field_im = padded[4 + comp, 1:-1, 1:-1] + slope(padded[7], comp)
        cur_re.append(drive[comp] + kappa * field_im)
        cur_im.append(-kappa * field_re)
    parts = []
    for comp in range(3):
        nxt = (comp + 1) % 3
        far = (comp + 2) % 3
        value = (
            cur_re[nxt] * real_b[far]
            + cur_im[nxt] * imag_b[far]
            - cur_re[far] * real_b[nxt]
            - cur_im[far] * imag_b[nxt]
        )
        parts.append(0.5 * value * melt)
    return jnp.stack(parts).astype(jnp.bfloat16)


def predict(padded, push):
    rows_out = []
    for comp in range(3):
        middle = padded[comp, 1:-1, 1:-1]
        carried = padded[0, 1:-1, 1:-1] * slope(padded[comp], 0)
        carried = carried + padded[1, 1:-1, 1:-1] * slope(padded[comp], 1)
        carried = carried + padded[2, 1:-1, 1:-1] * slope(padded[comp], 2)
        spread = beside_all(padded[comp]) - 6.0 * middle
        rows_out.append(middle + DT * (-carried + VISC * spread + push[comp].astype(jnp.float32)))
    return jnp.stack(rows_out)


def kappa_field(material, region, region_kappa):
    labels = jnp.arange(region_kappa.shape[0], dtype=jnp.int32)
    hits = region[None] == labels[:, None, None, None]
    looked = jnp.sum(jnp.where(hits, region_kappa[:, None, None, None], 0.0), axis=0)
    return jnp.where(material == 2, looked, 0.0)


def faces(field):
    return extended(field, (("wide", 1), ("narrow", 2)), 1)


def body(potential, source_current, cell_label, region_kappa, send_lines, recv_slot, velocity):
    span_x = potential.shape[1]
    span_y = potential.shape[2]
    depth = potential.shape[3]
    count_regions = region_kappa.shape[0]
    material = cell_label // count_regions
    region = cell_label % count_regions
    kappa = kappa_field(material, region, region_kappa)
    drive = jnp.where((material == 0)[None], source_current, 0.0)
    melt = (material == 2).astype(jnp.float32)
    potential_half = sweep(faces(potential), kappa, drive)
    potential_next = sweep(faces(potential_half), kappa, drive)
    lorentz = lorentz_force(faces(potential_next), kappa, drive, melt)
    peers = send_lines.shape[1]
    slots = send_lines.shape[2]
    flat = lorentz.reshape(3, span_x * span_y, depth)
    outgoing = jnp.take(flat, send_lines.reshape(-1), axis=1)
    incoming = lax.all_to_all(
        outgoing.reshape(3, peers, slots, depth),
        ("wide", "narrow"),
        split_axis=1,
        concat_axis=1,
        tiled=True,
    )
    incoming = incoming.reshape(3, peers * slots, depth)
    les_force = jnp.take(incoming, recv_slot[0], axis=1).reshape(
        3, velocity.shape[1], velocity.shape[2], depth
    )
    flow = extended(velocity, (("wide", 1), ("narrow", 2)), 1)
    velocity_next = predict(flow, les_force)
    return (potential_next, les_force, velocity_next)


def solution(mesh):
    in_specs = (
        P(None, "wide", "narrow", None),
        P(None, "wide", "narrow", None),
        P("wide", "narrow", None),
        P(),
        P(("wide", "narrow"), None, None),
        P(("wide", "narrow"), None),
        P(None, "wide", "narrow", None),
    )
    out_specs = (
        P(None, "wide", "narrow", None),
        P(None, "wide", "narrow", None),
        P(None, "wide", "narrow", None),
    )
    return jax.shard_map(body, mesh=mesh, in_specs=in_specs, out_specs=out_specs, check_vma=False)
```

profile of v0, /device:TPU:1, one launch (start us, length us, event | category | flops | bytes accessed | tf_op | source)
XLA Modules:
  0.0 125.5 jit_solution(14705535467382254480)
XLA Ops:
  0.7 1.8 %fusion.153 = (f32[8,1,32,128]{3,2,1,0:T(8,128)}, f32[8,1,32,128]{3,2,1,0:T(8,128)}) fusion(f32[8,16,32,128]{3,2,1,0:T(8,128)} %param.7), kind=kLoop, calls=%fused_computation.336 | loop fusion | bytes 524288 | tf_op jit(solution)/shard_map/slice | solution.py:18
  2.5 4.0 %collective-permute-start = (f32[8,1,32,128]{3,2,1,0:T(8,128)}, f32[8,1,32,128]{3,2,1,0:T(8,128)S(1)}, u32[]{:S(2)}, u32[]{:S(2)}) collective-permute-start(f32[8,1,32,128]{3,2,1,0:T(8,128)} %get-tuple-element.78), channel_id=1, source_target_pairs={{0,8},{8,16},{16,24},{24,32},{32,40},{40,48},{48,56},{56,64},{64,7... | collective-permute-start | bytes 393224 | tf_op jit(solution)/shard_map/ppermute | solution.py:15
  6.5 1.3 %collective-permute-start.1 = (f32[8,1,32,128]{3,2,1,0:T(8,128)}, f32[8,1,32,128]{3,2,1,0:T(8,128)S(1)}, u32[]{:S(2)}, u32[]{:S(2)}) collective-permute-start(f32[8,1,32,128]{3,2,1,0:T(8,128)} %get-tuple-element.77), channel_id=1, source_target_pairs={{8,0},{16,8},{24,16},{32,24},{40,32},{48,40},{56,48},{64,56},{72,6... | collective-permute-start | bytes 393224 | tf_op jit(solution)/shard_map/ppermute | solution.py:18
  7.8 1.5 %fusion.155 = (f32[3,1,32,128]{3,2,1,0:T(8,128)}, f32[3,1,32,128]{3,2,1,0:T(8,128)}) fusion(f32[3,8,32,128]{3,2,1,0:T(8,128)} %param.13), kind=kLoop, calls=%fused_computation.338 | loop fusion | bytes 196608 | tf_op jit(solution)/shard_map/slice | solution.py:18
  9.3 4.6 %collective-permute-start.12 = (f32[3,1,32,128]{3,2,1,0:T(8,128)}, f32[3,1,32,128]{3,2,1,0:T(8,128)}, u32[]{:S(2)}, u32[]{:S(2)}) collective-permute-start(f32[3,1,32,128]{3,2,1,0:T(8,128)} %get-tuple-element.87), channel_id=1, source_target_pairs={{0,8},{8,16},{16,24},{24,32},{32,40},{40,48},{48,56},{56,64},{64,7... | collective-permute-start | bytes 147464 | tf_op jit(solution)/shard_map/ppermute | solution.py:15
  13.9 1.3 %collective-permute-start.13 = (f32[3,1,32,128]{3,2,1,0:T(8,128)}, f32[3,1,32,128]{3,2,1,0:T(8,128)}, u32[]{:S(2)}, u32[]{:S(2)}) collective-permute-start(f32[3,1,32,128]{3,2,1,0:T(8,128)} %get-tuple-element.86), channel_id=1, source_target_pairs={{8,0},{16,8},{24,16},{32,24},{40,32},{48,40},{56,48},{64,56},{72,6... | collective-permute-start | bytes 147464 | tf_op jit(solution)/shard_map/ppermute | solution.py:18
  15.2 1.1 broadcast_compare_fusion.1
  16.3 1.0 add_select_fusion
  17.4 0.8 copy.32
  18.2 1.2 compare_and_fusion.2
  20.5 1.3 reduce.3
  22.4 1.2 broadcast_select_fusion
  24.6 4.9 %collective-permute-start.2 = (f32[8,18,1,128]{3,2,1,0:T(1,128)S(1)}, f32[8,18,1,128]{3,2,1,0:T(1,128)S(1)}, u32[]{:S(2)}, u32[]{:S(2)}) collective-permute-start(f32[8,18,1,128]{3,2,1,0:T(1,128)S(1)} %get-tuple-element.71), channel_id=1, source_target_pairs={{0,1},{1,2},{2,3},{3,4},{4,5},{5,6},{6,7},{8,9},{9,10},{10,11},{11... | collective-permute-start | bytes 221192 | tf_op jit(solution)/shard_map/ppermute | solution.py:15
  29.6 1.9 %collective-permute-start.3 = (f32[8,18,1,128]{3,2,1,0:T(1,128)S(1)}, f32[8,18,1,128]{3,2,1,0:T(1,128)S(1)}, u32[]{:S(2)}, u32[]{:S(2)}) collective-permute-start(f32[8,18,1,128]{3,2,1,0:T(1,128)S(1)} %get-tuple-element.72), channel_id=1, source_target_pairs={{1,0},{2,1},{3,2},{4,3},{5,4},{6,5},{7,6},{9,8},{10,9},{11,10},{12... | collective-permute-start | bytes 221192 | tf_op jit(solution)/shard_map/ppermute | solution.py:18
  32.0 3.2 %collective-permute-done.3 = f32[8,18,1,128]{3,2,1,0:T(1,128)S(1)} collective-permute-done((f32[8,18,1,128]{3,2,1,0:T(1,128)S(1)}, f32[8,18,1,128]{3,2,1,0:T(1,128)S(1)}, u32[]{:S(2)}, u32[]{:S(2)}) %collective-permute-start.3) | collective-permute-done | bytes 73760 | tf_op jit(solution)/shard_map/ppermute | solution.py:18
  36.2 0.7 copy-done.3
  36.9 1.2 bitcast_dynamic-update-slice_fusion.15
  38.6 0.6 bitcast_dynamic-update-slice_fusion.13
  39.2 0.7 bitcast_dynamic-update-slice_fusion.12
  40.3 0.7 fusion.152
  40.9 4.3 %collective-permute-start.4 = (f32[8,1,32,128]{3,2,1,0:T(8,128)}, f32[8,1,32,128]{3,2,1,0:T(8,128)S(1)}, u32[]{:S(2)}, u32[]{:S(2)}) collective-permute-start(f32[8,1,32,128]{3,2,1,0:T(8,128)} %get-tuple-element.75), channel_id=1, source_target_pairs={{0,8},{8,16},{16,24},{24,32},{32,40},{40,48},{48,56},{56,64},{64,7... | collective-permute-start | bytes 393224 | tf_op jit(solution)/shard_map/ppermute | solution.py:15
  45.2 1.3 %collective-permute-start.5 = (f32[8,1,32,128]{3,2,1,0:T(8,128)S(1)}, f32[8,1,32,128]{3,2,1,0:T(8,128)S(1)}, u32[]{:S(2)}, u32[]{:S(2)}) collective-permute-start(f32[8,1,32,128]{3,2,1,0:T(8,128)S(1)} %get-tuple-element.76), channel_id=1, source_target_pairs={{8,0},{16,8},{24,16},{32,24},{40,32},{48,40},{56,48},{64,56},{72,6... | collective-permute-start | bytes 393224 | tf_op jit(solution)/shard_map/ppermute | solution.py:18
  47.1 0.7 copy.28
  47.8 1.3 %pad_clamp_fusion.1 = s32[1024]{0:T(1024)} fusion(s32[512]{0:T(512)} %bitcast.253), kind=kLoop, calls=%fused_computation.328 | loop fusion | flops 1024 | bytes 6144 | tf_op jit(solution)/shard_map/jit(_take)/gather | solution.py:129
  49.0 1.9 %collective-permute-done.5 = f32[8,1,32,128]{3,2,1,0:T(8,128)S(1)} collective-permute-done((f32[8,1,32,128]{3,2,1,0:T(8,128)S(1)}, f32[8,1,32,128]{3,2,1,0:T(8,128)S(1)}, u32[]{:S(2)}, u32[]{:S(2)}) %collective-permute-start.5) | collective-permute-done | bytes 131104 | tf_op jit(solution)/shard_map/ppermute | solution.py:18
  51.0 3.9 %collective-permute-start.6 = (f32[8,18,1,128]{3,2,1,0:T(1,128)S(1)}, f32[8,18,1,128]{3,2,1,0:T(1,128)S(1)}, u32[]{:S(2)}, u32[]{:S(2)}) collective-permute-start(f32[8,18,1,128]{3,2,1,0:T(1,128)S(1)} %get-tuple-element.69), channel_id=1, source_target_pairs={{0,1},{1,2},{2,3},{3,4},{4,5},{5,6},{6,7},{8,9},{9,10},{10,11},{11... | collective-permute-start | bytes 221192 | tf_op jit(solution)/shard_map/ppermute | solution.py:15
  54.9 1.9 %collective-permute-start.7 = (f32[8,18,1,128]{3,2,1,0:T(1,128)S(1)}, f32[8,18,1,128]{3,2,1,0:T(1,128)S(1)}, u32[]{:S(2)}, u32[]{:S(2)}) collective-permute-start(f32[8,18,1,128]{3,2,1,0:T(1,128)S(1)} %get-tuple-element.70), channel_id=1, source_target_pairs={{1,0},{2,1},{3,2},{4,3},{5,4},{6,5},{7,6},{9,8},{10,9},{11,10},{12... | collective-permute-start | bytes 221192 | tf_op jit(solution)/shard_map/ppermute | solution.py:18
  56.9 0.8 constant_dynamic-update-slice_fusion.5
  57.7 2.9 %collective-permute-done.7 = f32[8,18,1,128]{3,2,1,0:T(1,128)S(1)} collective-permute-done((f32[8,18,1,128]{3,2,1,0:T(1,128)S(1)}, f32[8,18,1,128]{3,2,1,0:T(1,128)S(1)}, u32[]{:S(2)}, u32[]{:S(2)}) %collective-permute-start.7) | collective-permute-done | bytes 73760 | tf_op jit(solution)/shard_map/ppermute | solution.py:18
  63.1 0.7 bitcast_dynamic-update-slice_fusion.4
  64.1 2.8 %collective-permute-start.8 = (f32[8,1,32,128]{3,2,1,0:T(8,128)S(1)}, f32[8,1,32,128]{3,2,1,0:T(8,128)S(1)}, u32[]{:S(2)}, u32[]{:S(2)}) collective-permute-start(f32[8,1,32,128]{3,2,1,0:T(8,128)S(1)} %get-tuple-element.73), channel_id=1, source_target_pairs={{0,8},{8,16},{16,24},{24,32},{32,40},{40,48},{48,56},{56,64},{64,7... | collective-permute-start | bytes 393224 | tf_op jit(solution)/shard_map/ppermute | solution.py:15
  67.0 1.3 %collective-permute-start.9 = (f32[8,1,32,128]{3,2,1,0:T(8,128)S(1)}, f32[8,1,32,128]{3,2,1,0:T(8,128)S(1)}, u32[]{:S(2)}, u32[]{:S(2)}) collective-permute-start(f32[8,1,32,128]{3,2,1,0:T(8,128)S(1)} %get-tuple-element.74), channel_id=1, source_target_pairs={{8,0},{16,8},{24,16},{32,24},{40,32},{48,40},{56,48},{64,56},{72,6... | collective-permute-start | bytes 393224 | tf_op jit(solution)/shard_map/ppermute | solution.py:18
  68.3 0.8 constant_dynamic-update-slice_fusion.3
  69.1 5.9 %collective-permute-done.9 = f32[8,1,32,128]{3,2,1,0:T(8,128)S(1)} collective-permute-done((f32[8,1,32,128]{3,2,1,0:T(8,128)S(1)}, f32[8,1,32,128]{3,2,1,0:T(8,128)S(1)}, u32[]{:S(2)}, u32[]{:S(2)}) %collective-permute-start.9) | collective-permute-done | bytes 131104 | tf_op jit(solution)/shard_map/ppermute | solution.py:18
  75.2 3.0 %collective-permute-start.10 = (f32[8,18,1,128]{3,2,1,0:T(1,128)S(1)}, f32[8,18,1,128]{3,2,1,0:T(1,128)S(1)}, u32[]{:S(2)}, u32[]{:S(2)}) collective-permute-start(f32[8,18,1,128]{3,2,1,0:T(1,128)S(1)} %get-tuple-element.67), channel_id=1, source_target_pairs={{0,1},{1,2},{2,3},{3,4},{4,5},{5,6},{6,7},{8,9},{9,10},{10,11},{11... | collective-permute-start | bytes 221192 | tf_op jit(solution)/shard_map/ppermute | solution.py:15
  78.2 1.9 %collective-permute-start.11 = (f32[8,18,1,128]{3,2,1,0:T(1,128)S(1)}, f32[8,18,1,128]{3,2,1,0:T(1,128)S(1)}, u32[]{:S(2)}, u32[]{:S(2)}) collective-permute-start(f32[8,18,1,128]{3,2,1,0:T(1,128)S(1)} %get-tuple-element.68), channel_id=1, source_target_pairs={{1,0},{2,1},{3,2},{4,3},{5,4},{6,5},{7,6},{9,8},{10,9},{11,10},{12... | collective-permute-start | bytes 221192 | tf_op jit(solution)/shard_map/ppermute | solution.py:18
  80.1 3.6 %collective-permute-start.14 = (f32[3,10,1,128]{3,2,1,0:T(1,128)S(1)}, f32[3,10,1,128]{3,2,1,0:T(1,128)S(1)}, u32[]{:S(2)}, u32[]{:S(2)}) collective-permute-start(f32[3,10,1,128]{3,2,1,0:T(1,128)S(1)} %get-tuple-element.82), channel_id=1, source_target_pairs={{0,1},{1,2},{2,3},{3,4},{4,5},{5,6},{6,7},{8,9},{9,10},{10,11},{11... | collective-permute-start | bytes 46088 | tf_op jit(solution)/shard_map/ppermute | solution.py:15
  83.8 2.1 %collective-permute-start.15 = (f32[3,10,1,128]{3,2,1,0:T(1,128)S(1)}, f32[3,10,1,128]{3,2,1,0:T(1,128)S(1)}, u32[]{:S(2)}, u32[]{:S(2)}) collective-permute-start(f32[3,10,1,128]{3,2,1,0:T(1,128)S(1)} %get-tuple-element.83), channel_id=1, source_target_pairs={{1,0},{2,1},{3,2},{4,3},{5,4},{6,5},{7,6},{9,8},{10,9},{11,10},{12... | collective-permute-start | bytes 46088 | tf_op jit(solution)/shard_map/ppermute | solution.py:18
  86.8 0.6 copy-done.4
  87.4 1.0 select_convert_fusion.2
  89.9 0.9 pad_maximum_fusion.4
  90.9 2.1 %gather_fusion = bf16[512,3,128]{2,1,0:T(4,128)(2,1)S(1)} fusion(bf16[3,512,128]{2,0,1:T(4,128)(2,1)S(1)} %pad_maximum_fusion.4, s32[1024]{0:T(1024)S(1)} %copy-done.7), kind=kCustom, calls=%fused_computation | custom fusion | bytes 788480 | tf_op jit(solution)/shard_map/jit(_take)/gather | solution.py:129
  92.9 1.1 copy_select_fusion
  94.0 15.3 %all-to-all-start = ((bf16[3,128,4,128]{3,2,0,1:T(4,128)(2,1)}), bf16[3,128,4,128]{3,2,0,1:T(4,128)(2,1)S(1)}, u32[]{:S(2)}, u32[]{:S(2)}) async-start(bf16[3,128,4,128]{3,2,0,1:T(4,128)(2,1)} %copy_select_fusion), calls=%async_computation | async-start | bytes 786432 | tf_op jit(solution)/shard_map/all_to_all | solution.py:130
  109.6 12.0 %all-to-all-done = bf16[3,128,4,128]{3,2,0,1:T(4,128)(2,1)S(1)} async-done(((bf16[3,128,4,128]{3,2,0,1:T(4,128)(2,1)}), bf16[3,128,4,128]{3,2,0,1:T(4,128)(2,1)S(1)}, u32[]{:S(2)}, u32[]{:S(2)}) %all-to-all-start) | async-done | bytes 393248 | tf_op jit(solution)/shard_map/all_to_all | solution.py:130
  121.8 1.0 gather_fusion.1
  123.6 0.8 copy_select_fusion.1
  124.7 0.8 pad_maximum_fusion.5
  (111 shorter events, 12.2 us)
Async XLA Ops:
  0.6 23.7 %copy-start.2 = (f32[8,16,32,128]{3,2,1,0:T(8,128)S(1)}, f32[8,16,32,128]{3,2,1,0:T(8,128)}, u32[]{:S(2)}) copy-start(f32[8,16,32,128]{3,2,1,0:T(8,128)} %param.7) | copy-start | bytes 6291460
  0.6 23.0 %copy-start.10 = (s32[1,256]{1,0:T(1,128)S(1)}, s32[1,256]{1,0:T(1,128)}, u32[]{:S(2)}) copy-start(s32[1,256]{1,0:T(1,128)} %param.12) | copy-start | bytes 3076
  2.5 21.8 %collective-permute-start = (f32[8,1,32,128]{3,2,1,0:T(8,128)}, f32[8,1,32,128]{3,2,1,0:T(8,128)S(1)}, u32[]{:S(2)}, u32[]{:S(2)}) collective-permute-start(f32[8,1,32,128]{3,2,1,0:T(8,128)} %get-tuple-element.78), channel_id=1, source_target_pairs={{0,8},{8,16},{16,24},{24,32},{32,40},{40,48},{48,56},{56,64},{64,7... | collective-permute-start | bytes 393224 | tf_op jit(solution)/shard_map/ppermute | solution.py:15
  6.5 18.0 %collective-permute-start.1 = (f32[8,1,32,128]{3,2,1,0:T(8,128)}, f32[8,1,32,128]{3,2,1,0:T(8,128)S(1)}, u32[]{:S(2)}, u32[]{:S(2)}) collective-permute-start(f32[8,1,32,128]{3,2,1,0:T(8,128)} %get-tuple-element.77), channel_id=1, source_target_pairs={{8,0},{16,8},{24,16},{32,24},{40,32},{48,40},{56,48},{64,56},{72,6... | collective-permute-start | bytes 393224 | tf_op jit(solution)/shard_map/ppermute | solution.py:18
  9.3 47.6 %collective-permute-start.12 = (f32[3,1,32,128]{3,2,1,0:T(8,128)}, f32[3,1,32,128]{3,2,1,0:T(8,128)}, u32[]{:S(2)}, u32[]{:S(2)}) collective-permute-start(f32[3,1,32,128]{3,2,1,0:T(8,128)} %get-tuple-element.87), channel_id=1, source_target_pairs={{0,8},{8,16},{16,24},{24,32},{32,40},{40,48},{48,56},{56,64},{64,7... | collective-permute-start | bytes 147464 | tf_op jit(solution)/shard_map/ppermute | solution.py:15
  13.9 54.4 %collective-permute-start.13 = (f32[3,1,32,128]{3,2,1,0:T(8,128)}, f32[3,1,32,128]{3,2,1,0:T(8,128)}, u32[]{:S(2)}, u32[]{:S(2)}) collective-permute-start(f32[3,1,32,128]{3,2,1,0:T(8,128)} %get-tuple-element.86), channel_id=1, source_target_pairs={{8,0},{16,8},{24,16},{32,24},{40,32},{48,40},{56,48},{64,56},{72,6... | collective-permute-start | bytes 147464 | tf_op jit(solution)/shard_map/ppermute | solution.py:18
  24.3 7.2 %copy-start.12 = (f32[16]{0:T(128)S(1)}, f32[16]{0:T(128)}, u32[]{:S(2)}) copy-start(f32[16]{0:T(128)} %param.10) | copy-start | bytes 196
  24.6 7.4 %collective-permute-start.2 = (f32[8,18,1,128]{3,2,1,0:T(1,128)S(1)}, f32[8,18,1,128]{3,2,1,0:T(1,128)S(1)}, u32[]{:S(2)}, u32[]{:S(2)}) collective-permute-start(f32[8,18,1,128]{3,2,1,0:T(1,128)S(1)} %get-tuple-element.71), channel_id=1, source_target_pairs={{0,1},{1,2},{2,3},{3,4},{4,5},{5,6},{6,7},{8,9},{9,10},{10,11},{11... | collective-permute-start | bytes 221192 | tf_op jit(solution)/shard_map/ppermute | solution.py:15
  29.6 5.7 %collective-permute-start.3 = (f32[8,18,1,128]{3,2,1,0:T(1,128)S(1)}, f32[8,18,1,128]{3,2,1,0:T(1,128)S(1)}, u32[]{:S(2)}, u32[]{:S(2)}) collective-permute-start(f32[8,18,1,128]{3,2,1,0:T(1,128)S(1)} %get-tuple-element.72), channel_id=1, source_target_pairs={{1,0},{2,1},{3,2},{4,3},{5,4},{6,5},{7,6},{9,8},{10,9},{11,10},{12... | collective-permute-start | bytes 221192 | tf_op jit(solution)/shard_map/ppermute | solution.py:18
  35.9 1.0 copy-start.3
  40.0 6.5 %copy-start.11 = (s32[1,256]{1,0:T(1,128)S(1)}, s32[1,256]{1,0:T(1,128)}, u32[]{:S(2)}) copy-start(s32[1,256]{1,0:T(1,128)} %param.12) | copy-start | bytes 3076
  40.9 8.1 %collective-permute-start.4 = (f32[8,1,32,128]{3,2,1,0:T(8,128)}, f32[8,1,32,128]{3,2,1,0:T(8,128)S(1)}, u32[]{:S(2)}, u32[]{:S(2)}) collective-permute-start(f32[8,1,32,128]{3,2,1,0:T(8,128)} %get-tuple-element.75), channel_id=1, source_target_pairs={{0,8},{8,16},{16,24},{24,32},{32,40},{40,48},{48,56},{56,64},{64,7... | collective-permute-start | bytes 393224 | tf_op jit(solution)/shard_map/ppermute | solution.py:15
  45.2 5.7 %collective-permute-start.5 = (f32[8,1,32,128]{3,2,1,0:T(8,128)S(1)}, f32[8,1,32,128]{3,2,1,0:T(8,128)S(1)}, u32[]{:S(2)}, u32[]{:S(2)}) collective-permute-start(f32[8,1,32,128]{3,2,1,0:T(8,128)S(1)} %get-tuple-element.76), channel_id=1, source_target_pairs={{8,0},{16,8},{24,16},{32,24},{40,32},{48,40},{56,48},{64,56},{72,6... | collective-permute-start | bytes 393224 | tf_op jit(solution)/shard_map/ppermute | solution.py:18
  51.0 6.6 %collective-permute-start.6 = (f32[8,18,1,128]{3,2,1,0:T(1,128)S(1)}, f32[8,18,1,128]{3,2,1,0:T(1,128)S(1)}, u32[]{:S(2)}, u32[]{:S(2)}) collective-permute-start(f32[8,18,1,128]{3,2,1,0:T(1,128)S(1)} %get-tuple-element.69), channel_id=1, source_target_pairs={{0,1},{1,2},{2,3},{3,4},{4,5},{5,6},{6,7},{8,9},{9,10},{10,11},{11... | collective-permute-start | bytes 221192 | tf_op jit(solution)/shard_map/ppermute | solution.py:15
  54.9 5.7 %collective-permute-start.7 = (f32[8,18,1,128]{3,2,1,0:T(1,128)S(1)}, f32[8,18,1,128]{3,2,1,0:T(1,128)S(1)}, u32[]{:S(2)}, u32[]{:S(2)}) collective-permute-start(f32[8,18,1,128]{3,2,1,0:T(1,128)S(1)} %get-tuple-element.70), channel_id=1, source_target_pairs={{1,0},{2,1},{3,2},{4,3},{5,4},{6,5},{7,6},{9,8},{10,9},{11,10},{12... | collective-permute-start | bytes 221192 | tf_op jit(solution)/shard_map/ppermute | solution.py:18
  63.8 4.4 %copy-start.1 = (f32[3,8,32,128]{3,2,1,0:T(8,128)S(1)}, f32[3,8,32,128]{3,2,1,0:T(8,128)}, u32[]{:S(2)}) copy-start(f32[3,8,32,128]{3,2,1,0:T(8,128)} %param.13) | copy-start | bytes 1179652
  64.1 22.3 %copy-start = (f32[8,16,32,128]{3,2,1,0:T(8,128)}, f32[8,16,32,128]{3,2,1,0:T(8,128)S(1)}, u32[]{:S(2)}) copy-start(f32[8,16,32,128]{3,2,1,0:T(8,128)S(1)} %bitcast_dynamic-update-slice_fusion) | copy-start | bytes 6291460
  64.1 5.0 %collective-permute-start.8 = (f32[8,1,32,128]{3,2,1,0:T(8,128)S(1)}, f32[8,1,32,128]{3,2,1,0:T(8,128)S(1)}, u32[]{:S(2)}, u32[]{:S(2)}) collective-permute-start(f32[8,1,32,128]{3,2,1,0:T(8,128)S(1)} %get-tuple-element.73), channel_id=1, source_target_pairs={{0,8},{8,16},{16,24},{24,32},{32,40},{40,48},{48,56},{56,64},{64,7... | collective-permute-start | bytes 393224 | tf_op jit(solution)/shard_map/ppermute | solution.py:15
  67.0 8.1 %collective-permute-start.9 = (f32[8,1,32,128]{3,2,1,0:T(8,128)S(1)}, f32[8,1,32,128]{3,2,1,0:T(8,128)S(1)}, u32[]{:S(2)}, u32[]{:S(2)}) collective-permute-start(f32[8,1,32,128]{3,2,1,0:T(8,128)S(1)} %get-tuple-element.74), channel_id=1, source_target_pairs={{8,0},{16,8},{24,16},{32,24},{40,32},{48,40},{56,48},{64,56},{72,6... | collective-permute-start | bytes 393224 | tf_op jit(solution)/shard_map/ppermute | solution.py:18
  69.1 16.8 %copy-start.5 = (f32[3,10,32,128]{3,2,1,0:T(8,128)}, f32[3,10,32,128]{3,2,1,0:T(8,128)S(1)}, u32[]{:S(2)}) copy-start(f32[3,10,32,128]{3,2,1,0:T(8,128)S(1)} %constant_dynamic-update-slice_fusion.3) | copy-start | bytes 1474564
  75.2 10.7 %collective-permute-start.10 = (f32[8,18,1,128]{3,2,1,0:T(1,128)S(1)}, f32[8,18,1,128]{3,2,1,0:T(1,128)S(1)}, u32[]{:S(2)}, u32[]{:S(2)}) collective-permute-start(f32[8,18,1,128]{3,2,1,0:T(1,128)S(1)} %get-tuple-element.67), channel_id=1, source_target_pairs={{0,1},{1,2},{2,3},{3,4},{4,5},{5,6},{6,7},{8,9},{9,10},{10,11},{11... | collective-permute-start | bytes 221192 | tf_op jit(solution)/shard_map/ppermute | solution.py:15
  78.2 7.7 %collective-permute-start.11 = (f32[8,18,1,128]{3,2,1,0:T(1,128)S(1)}, f32[8,18,1,128]{3,2,1,0:T(1,128)S(1)}, u32[]{:S(2)}, u32[]{:S(2)}) collective-permute-start(f32[8,18,1,128]{3,2,1,0:T(1,128)S(1)} %get-tuple-element.68), channel_id=1, source_target_pairs={{1,0},{2,1},{3,2},{4,3},{5,4},{6,5},{7,6},{9,8},{10,9},{11,10},{12... | collective-permute-start | bytes 221192 | tf_op jit(solution)/shard_map/ppermute | solution.py:18
  80.1 29.3 %collective-permute-start.14 = (f32[3,10,1,128]{3,2,1,0:T(1,128)S(1)}, f32[3,10,1,128]{3,2,1,0:T(1,128)S(1)}, u32[]{:S(2)}, u32[]{:S(2)}) collective-permute-start(f32[3,10,1,128]{3,2,1,0:T(1,128)S(1)} %get-tuple-element.82), channel_id=1, source_target_pairs={{0,1},{1,2},{2,3},{3,4},{4,5},{5,6},{6,7},{8,9},{9,10},{10,11},{11... | collective-permute-start | bytes 46088 | tf_op jit(solution)/shard_map/ppermute | solution.py:15
  83.8 25.6 %collective-permute-start.15 = (f32[3,10,1,128]{3,2,1,0:T(1,128)S(1)}, f32[3,10,1,128]{3,2,1,0:T(1,128)S(1)}, u32[]{:S(2)}, u32[]{:S(2)}) collective-permute-start(f32[3,10,1,128]{3,2,1,0:T(1,128)S(1)} %get-tuple-element.83), channel_id=1, source_target_pairs={{1,0},{2,1},{3,2},{4,3},{5,4},{6,5},{7,6},{9,8},{10,9},{11,10},{12... | collective-permute-start | bytes 46088 | tf_op jit(solution)/shard_map/ppermute | solution.py:18
  86.6 0.8 copy-start.4
  89.0 1.8 %copy-start.7 = (s32[1024]{0:T(1024)S(1)}, s32[1024]{0:T(1024)}, u32[]{:S(2)}) copy-start(s32[1024]{0:T(1024)} %pad_clamp_fusion.1) | copy-start | bytes 12292
  89.7 19.7 %copy-start.9 = (s32[256,1]{0,1:T(1,128)S(1)}, s32[256,1]{0,1:T(1,128)}, u32[]{:S(2)}) copy-start(s32[256,1]{0,1:T(1,128)} %compare_select_fusion.2) | copy-start | bytes 3076
  89.7 19.7 %copy-start.6 = (f32[3,10,32,128]{3,2,1,0:T(8,128)S(1)}, f32[3,10,32,128]{3,2,1,0:T(8,128)}, u32[]{:S(2)}) copy-start(f32[3,10,32,128]{3,2,1,0:T(8,128)} %copy-done.5) | copy-start | bytes 1474564
  94.0 27.6 %all-to-all-start = ((bf16[3,128,4,128]{3,2,0,1:T(4,128)(2,1)}), bf16[3,128,4,128]{3,2,0,1:T(4,128)(2,1)S(1)}, u32[]{:S(2)}, u32[]{:S(2)}) async-start(bf16[3,128,4,128]{3,2,0,1:T(4,128)(2,1)} %copy_select_fusion), calls=%async_computation | async-start | bytes 786432 | tf_op jit(solution)/shard_map/all_to_all | solution.py:130
  109.4 13.4 %copy-start.13 = (pred[256]{0:T(512)(128)(4,1)S(1)}, pred[256]{0:T(512)(128)(4,1)}, u32[]{:S(2)}) copy-start(pred[256]{0:T(512)(128)(4,1)} %compare_and_fusion.1) | copy-start | bytes 772
  109.6 14.0 %copy-start.8 = (pred[8,32]{1,0:T(8,128)(4,1)S(1)}, pred[8,32]{1,0:T(8,128)(4,1)}, u32[]{:S(2)}) copy-start(pred[8,32]{1,0:T(8,128)(4,1)} %compare_and_fusion) | copy-start | bytes 772
where the time goes:
time: 127 us; the launch traced here: 125 us
  starting transfers between devices  59.5 us (47%)
  waiting for transfers between devices  26 us (20%)
  other arithmetic  23.8 us (19%)
  local copies, waits for them, and re-layouts  14.6 us (11%)
  between operations  1.55 us (1%)
    ppermute x8, starting transfers between devices, extended(): lax.ppermute(lax.slice_in_dim(block, block.shape[dim] - width, None, axis...  31.2 us
    all_to_all x1, starting transfers between devices, body(): lax.all_to_all(outgoing.reshape(3, peers, slots, depth), ('wide', 'narrow...  15.3 us
    ppermute x8, waiting for transfers between devices, extended(): lax.ppermute(lax.slice_in_dim(block, 0, width, axis=dim), axis, backward)  14 us
    ppermute x8, starting transfers between devices, extended(): lax.ppermute(lax.slice_in_dim(block, 0, width, axis=dim), axis, backward)  13 us
    all_to_all x1, waiting for transfers between devices, body(): lax.all_to_all(outgoing.reshape(3, peers, slots, depth), ('wide', 'narrow...  12 us
    unnamed x15, other arithmetic  6.92 us
    unnamed x34, local copies, waits for them, and re-layouts  3.7 us
    slice x2, local copies, waits for them, and re-layouts, extended(): lax.slice_in_dim(block, 0, width, axis=dim)  3.31 us
  transfers between devices with their start and end apart: 17, of which 5 were waited for; matrix products, arithmetic and copies ran while one was open for 25% of the time, Pallas kernels for 0%

commit v1 on v0

v1 whole, which is shorter than its diff:
```python
import functools

import jax
import jax.numpy as jnp
from jax import lax
from jax.experimental import pallas as pl
from jax.experimental.pallas import tpu as pltpu
from jax.sharding import PartitionSpec as P

DT = 0.25
VISC = 0.5
F32 = jnp.float32
BF16 = jnp.bfloat16
DEEP = 3
FLAT = 2
ROWS = 48
OFF = 8
MIB = 1 << 20


def strip(start, size, stride):
    return pl.ds(start, size, stride=stride)


def planes_of(span_x, span_y):
    return 8 * DEEP + 4 * FLAT


def prep_kernel(span_x, span_y, regions, rk, pot, src, lab, vel, dk, wlo, whi, nlo, nhi, vwlo, vwhi, vnlo, vnhi):
    depth = pot.shape[-1]

    def plane(x, carry):
        rows = pl.ds(pl.multiple_of(x * span_y, span_y), span_y)
        label = lab[rows, :]
        kappa = jnp.zeros((span_y, depth), F32)
        for r in range(regions):
            kappa = jnp.where(label == 2 * regions + r, rk[r], kappa)
        coil = label < regions
        for c in range(3):
            dk[c, rows, :] = jnp.where(coil, src[c, rows, :], 0.0)
        dk[3, rows, :] = kappa
        return carry

    lax.fori_loop(0, span_x, plane, 0)
    for c in range(8):
        for d in range(DEEP):
            wlo[c * DEEP + d] = pot[c, pl.ds(d * span_y, span_y), :]
            whi[c * DEEP + d] = pot[c, pl.ds((span_x - 1 - d) * span_y, span_y), :]
            nlo[c * DEEP + d] = pot[c, strip(d, span_x, span_y), :]
            nhi[c * DEEP + d] = pot[c, strip(span_y - 1 - d, span_x, span_y), :]
    for f in range(4):
        for d in range(FLAT):
            p = 8 * DEEP + f * FLAT + d
            wlo[p] = dk[f, pl.ds(d * span_y, span_y), :]
            whi[p] = dk[f, pl.ds((span_x - 1 - d) * span_y, span_y), :]
            nlo[p] = dk[f, strip(d, span_x, span_y), :]
            nhi[p] = dk[f, strip(span_y - 1 - d, span_x, span_y), :]
    les_x = vel.shape[1] // span_y
    for c in range(3):
        vwlo[c] = vel[c, pl.ds(0, span_y), :]
        vwhi[c] = vel[c, pl.ds((les_x - 1) * span_y, span_y), :]
        vnlo[c] = vel[c, strip(0, les_x, span_y), :]
        vnhi[c] = vel[c, strip(span_y - 1, les_x, span_y), :]


def corner_kernel(span_x, nlo, nhi, clo, chi):
    planes = nlo.shape[0]
    for d in range(FLAT):
        for side, ref in enumerate((nlo, nhi)):
            rows = pl.ds((d * 2 + side) * planes, planes)
            clo[rows, :] = ref[:, d, :]
            chi[rows, :] = ref[:, span_x - 1 - d, :]


def lanes(value):
    depth = value.shape[-1]
    lane = lax.broadcasted_iota(jnp.int32, value.shape, 1)
    ahead = jnp.where(lane == depth - 1, 0.0, pltpu.roll(value, depth - 1, 1))
    back = jnp.where(lane == 0, 0.0, pltpu.roll(value, 1, 1))
    return ahead, back


def sweep_tile(old, new, field, row):
    s6 = 6.0 * field[4, pl.ds(row, 8), :]
    kappa = field[3, pl.ds(row, 8), :]
    sk = kappa * field[4, pl.ds(row, 8), :]
    half = 0.5 * kappa
    total = []
    diff = []
    for c in range(8):
        xf = old[c, pl.ds(row + ROWS, 8), :]
        xb = old[c, pl.ds(row - ROWS, 8), :]
        yf = old[c, pl.ds(row + 1, 8), :]
        yb = old[c, pl.ds(row - 1, 8), :]
        zf, zb = lanes(old[c, pl.ds(row, 8), :])
        total.append((xf + xb) + (yf + yb) + (zf + zb))
        if c % 4 == 3:
            diff.append((xf - xb, yf - yb, zf - zb))
        else:
            diff.append(((xf - xb), (yf - yb), (zf - zb))[c % 4])
    for c in range(3):
        first = (field[c, pl.ds(row, 8), :] + total[c]) + half * diff[7][c]
        second = total[4 + c] - half * diff[3][c]
        new[c, pl.ds(row, 8), :] = s6 * first + sk * second
        new[4 + c, pl.ds(row, 8), :] = s6 * second - sk * first
    first = total[3] + half * (diff[4] + diff[5] + diff[6])
    second = total[7] - half * (diff[0] + diff[1] + diff[2])
    new[3, pl.ds(row, 8), :] = s6 * first + sk * second
    new[7, pl.ds(row, 8), :] = s6 * second - sk * first


def lorentz_tile(now, field, row):
    def grab(c, shift):
        return now[c, pl.ds(row + shift, 8), :]

    kappa = field[3, pl.ds(row, 8), :]

    def part(base):
        a = [grab(base + c, 0) for c in range(3)]
        azf, azb = lanes(a[0])
        bzf, bzb = lanes(a[1])
        curl = [
            (grab(base + 2, 1) - grab(base + 2, -1)) - (bzf - bzb),
            (azf - azb) - (grab(base + 2, ROWS) - grab(base + 2, -ROWS)),
            (grab(base + 1, ROWS) - grab(base + 1, -ROWS)) - (grab(base, 1) - grab(base, -1)),
        ]
        phi = grab(base + 3, 0)
        pzf, pzb = lanes(phi)
        grad = [
            grab(base + 3, ROWS) - grab(base + 3, -ROWS),
            grab(base + 3, 1) - grab(base + 3, -1),
            pzf - pzb,
        ]
        return curl, [a[c] + 0.5 * grad[c] for c in range(3)], a + [phi]

    real_b, field_re, values_re = part(0)
    imag_b, field_im, values_im = part(4)
    cur_re = [field[c, pl.ds(row, 8), :] + kappa * field_im[c] for c in range(3)]
    cur_im = [-kappa * field_re[c] for c in range(3)]
    force = []
    for c in range(3):
        n = (c + 1) % 3
        f = (c + 2) % 3
        value = (cur_re[n] * real_b[f] - cur_re[f] * real_b[n]) + (
            cur_im[n] * imag_b[f] - cur_im[f] * imag_b[n]
        )
        force.append(jnp.where(kappa > 0.0, 0.25 * value, 0.0))
    return force, values_re + values_im


def main_kernel(
    span_x, span_y, slots, flags, pot, dk, wlo, whi, nlo, nhi, clo, chi, hot, nxt, out, s0, s1, s2, field, force
):
    depth = pot.shape[-1]
    planes = wlo.shape[0]

    def at(x):
        return (x + DEEP) * ROWS + OFF

    def lay(x, carry):
        rows = pl.ds(pl.multiple_of(x * span_y, span_y), span_y)
        there = pl.ds(pl.multiple_of((x + DEEP) * ROWS + OFF, 8), span_y)
        for c in range(8):
            s0[c, there, :] = pot[c, rows, :]
        for f in range(4):
            field[f, there, :] = dk[f, rows, :]
        return carry

    lax.fori_loop(0, span_x, lay, 0)
    for c in range(12):
        deep = DEEP if c < 8 else FLAT
        ref, part = (s0, c) if c < 8 else (field, c - 8)
        for d in range(deep):
            p = c * DEEP + d if c < 8 else 8 * DEEP + part * FLAT + d
            ref[part, pl.ds(at(-1 - d), span_y), :] = wlo[p]
            ref[part, pl.ds(at(span_x + d), span_y), :] = whi[p]
            ref[part, strip(at(0) - 1 - d, span_x, ROWS), :] = nlo[p]
            ref[part, strip(at(0) + span_y + d, span_x, ROWS), :] = nhi[p]
            for e in range(deep - 1 - d):
                for source, x in ((clo, -1 - e), (chi, span_x + e)):
                    ref[part, pl.ds(at(x) - 1 - d, 1), :] = source[pl.ds(e * 2 * planes + p, 1), :]
                    ref[part, pl.ds(at(x) + span_y + d, 1), :] = source[pl.ds((e * 2 + 1) * planes + p, 1), :]

    line = lax.broadcasted_iota(jnp.int32, (8, depth), 0)

    def scale(i, carry):
        x = i - FLAT
        fx = jnp.where(x < 0, flags[0], jnp.where(x >= span_x, flags[1], 1.0))
        for t in range(5):
            row = at(x) - FLAT + 8 * t
            y = line + (8 * t - FLAT)
            fy = jnp.where(y < 0, flags[2], jnp.where(y >= span_y, flags[3], 1.0))
            kappa = field[3, pl.ds(row, 8), :]
            field[4, pl.ds(row, 8), :] = (fx * fy) / (36.0 + kappa * kappa)
        return carry

    lax.fori_loop(0, span_x + 2 * FLAT, scale, 0)

    def first(i, carry):
        for t in range(5):
            sweep_tile(s0, s1, field, at(i - 2) - 2 + 8 * t)
        return carry

    lax.fori_loop(0, span_x + 4, first, 0)

    def second(i, carry):
        for t in range(5):
            sweep_tile(s1, s2, field, at(i - 1) - 1 + 8 * t)
        return carry

    lax.fori_loop(0, span_x + 2, second, 0)

    def third(x, carry):
        for t in range(span_y // 8):
            f, values = lorentz_tile(s2, field, at(x) + 8 * t)
            rows = pl.ds(pl.multiple_of(x * span_y + 8 * t, 8), 8)
            for c in range(3):
                force[c, rows, :] = f[c]
            for c in range(8):
                nxt[c, rows, :] = values[c]
        return carry

    lax.fori_loop(0, span_x, third, 0)

    table = [force[c].astype(BF16) for c in range(3)]
    chunk = 256
    upper = lax.broadcasted_iota(jnp.int32, (chunk // 8, 8, depth), 1) < slots

    def pick(i, carry):
        h = hot[pl.ds(pl.multiple_of(i * chunk, chunk), chunk), :]
        got = [
            jnp.dot(h, table[c], preferred_element_type=F32).reshape(chunk // 8, 8, depth)
            for c in range(3)
        ]
        both = jnp.concatenate([jnp.where(upper, got[0], got[1]), got[2]], axis=1)
        out[pl.ds(i * (chunk // 8), chunk // 8)] = both.astype(BF16)
        return carry

    lax.fori_loop(0, hot.shape[0] // chunk, pick, 0)


def flow_kernel(les_x, span_y, vel, vwlo, vwhi, vnlo, vnhi, base, s0):
    def at(x):
        return (x + 1) * ROWS + OFF

    for c in range(3):
        for x in range(les_x):
            s0[c, pl.ds(at(x), span_y), :] = vel[c, pl.ds(x * span_y, span_y), :]
        s0[c, pl.ds(at(-1), span_y), :] = vwlo[c]
        s0[c, pl.ds(at(les_x), span_y), :] = vwhi[c]
        s0[c, strip(at(0) - 1, les_x, ROWS), :] = vnlo[c]
        s0[c, strip(at(0) + span_y, les_x, ROWS), :] = vnhi[c]

    def step(x, carry):
        for t in range(span_y // 8):
            row = at(x) + 8 * t
            middle = [s0[c, pl.ds(row, 8), :] for c in range(3)]
            for c in range(3):
                xf = s0[c, pl.ds(row + ROWS, 8), :]
                xb = s0[c, pl.ds(row - ROWS, 8), :]
                yf = s0[c, pl.ds(row + 1, 8), :]
                yb = s0[c, pl.ds(row - 1, 8), :]
                zf, zb = lanes(middle[c])
                carried = 0.5 * (middle[0] * (xf - xb) + middle[1] * (yf - yb) + middle[2] * (zf - zb))
                spread = (xf + xb) + (yf + yb) + (zf + zb) - 6.0 * middle[c]
                base[c, pl.ds(pl.multiple_of(x * span_y + 8 * t, 8), 8), :] = middle[c] + DT * (
                    VISC * spread - carried
                )
        return carry

    lax.fori_loop(0, les_x, step, 0)


def last_kernel(hot, got, base, les, nxt):
    rows = got.shape[0] * got.shape[1]
    values = got[...].reshape(rows, got.shape[2])
    push = jnp.dot(hot[...], values, preferred_element_type=F32).astype(BF16)
    les[...] = push
    nxt[...] = base[...] + DT * push.astype(F32)


def call(kernel, out, name, scratch=(), smem=0, count=1, limit=48):
    vmem = pl.BlockSpec(memory_space=pltpu.VMEM)
    specs = [pl.BlockSpec(memory_space=pltpu.SMEM)] * smem + [vmem] * (count - smem)
    return pl.pallas_call(
        kernel,
        out_shape=[jax.ShapeDtypeStruct(shape, kind) for shape, kind in out],
        in_specs=specs,
        out_specs=[vmem] * len(out),
        scratch_shapes=[pltpu.VMEM(shape, kind) for shape, kind in scratch],
        compiler_params=pltpu.CompilerParams(vmem_limit_bytes=limit * MIB),
        name=name,
    )


def swap(low, high, axis):
    count = lax.axis_size(axis)
    forward = [(i, i + 1) for i in range(count - 1)]
    backward = [(target, source) for source, target in forward]
    return lax.ppermute(high, axis, forward), lax.ppermute(low, axis, backward)


def body(potential, source_current, cell_label, region_kappa, send_lines, recv_slot, velocity):
    _, span_x, span_y, depth = potential.shape
    les_x = velocity.shape[1]
    peers, slots = send_lines.shape[1:]
    cells = span_x * span_y
    lines = les_x * span_y
    planes = planes_of(span_x, span_y)
    pot = potential.reshape(8, cells, depth)
    src = source_current.reshape(3, cells, depth)
    lab = cell_label.reshape(cells, depth)
    vel = velocity.reshape(3, lines, depth)

    wide = ((planes, span_y, depth), F32)
    narrow = ((planes, span_x, depth), F32)
    vw = ((3, span_y, depth), F32)
    vn = ((3, les_x, depth), F32)
    dk, wlo, whi, nlo, nhi, vwlo, vwhi, vnlo, vnhi = call(
        functools.partial(prep_kernel, span_x, span_y, region_kappa.shape[0]),
        [((4, cells, depth), F32), wide, wide, narrow, narrow, vw, vw, vn, vn],
        "prep", smem=1, count=5,
    )(region_kappa, pot, src, lab, vel)

    wlo, whi = swap(wlo, whi, "wide")
    nlo, nhi = swap(nlo, nhi, "narrow")
    corner = ((FLAT * 2 * planes, depth), F32)
    clo, chi = call(
        functools.partial(corner_kernel, span_x), [corner, corner], "corner", count=2
    )(nlo, nhi)
    clo, chi = swap(clo, chi, "wide")
    vwlo, vwhi = swap(vwlo, vwhi, "wide")
    vnlo, vnhi = swap(vnlo, vnhi, "narrow")

    sent = jnp.concatenate([send_lines[0], send_lines[0]], axis=1).reshape(-1)
    hot = (sent[:, None] == jnp.arange(cells, dtype=jnp.int32)[None, :]).astype(BF16)
    slot = recv_slot[0]
    place = (slot // slots) * 16 + slot % slots
    want = (place[None, :] + slots * jnp.arange(3, dtype=jnp.int32)[:, None]).reshape(-1)
    take = (want[:, None] == jnp.arange(peers * 16, dtype=jnp.int32)[None, :]).astype(BF16)

    w, n = lax.axis_index("wide"), lax.axis_index("narrow")
    flags = jnp.stack(
        [w > 0, w < lax.axis_size("wide") - 1, n > 0, n < lax.axis_size("narrow") - 1]
    ).astype(F32)
    pad = (span_x + 2 * DEEP) * ROWS
    potential_next, outgoing = call(
        functools.partial(main_kernel, span_x, span_y, slots),
        [((8, cells, depth), F32), ((peers, 16, depth), BF16)],
        "sweeps",
        scratch=[((8, pad, depth), F32)] * 3 + [((5, pad, depth), F32), ((3, cells, depth), F32)],
        smem=1, count=10,
    )(flags, pot, dk, wlo, whi, nlo, nhi, clo, chi, hot)

    incoming = lax.all_to_all(
        outgoing, ("wide", "narrow"), split_axis=0, concat_axis=0, tiled=True
    )
    (base,) = call(
        functools.partial(flow_kernel, les_x, span_y),
        [((3, lines, depth), F32)],
        "flow",
        scratch=[((3, (les_x + 2) * ROWS, depth), F32)],
        count=5,
    )(vel, vwlo, vwhi, vnlo, vnhi)
    les, velocity_next = call(
        last_kernel,
        [((3 * lines, depth), BF16), ((3 * lines, depth), F32)],
        "last", count=3,
    )(take, incoming, base.reshape(3 * lines, depth))
    block = (3, les_x, span_y, depth)
    return potential_next.reshape(potential.shape), les.reshape(block), velocity_next.reshape(block)


def solution(mesh):
    in_specs = (
        P(None, "wide", "narrow", None),
        P(None, "wide", "narrow", None),
        P("wide", "narrow", None),
        P(),
        P(("wide", "narrow"), None, None),
        P(("wide", "narrow"), None),
        P(None, "wide", "narrow", None),
    )
    out_specs = (
        P(None, "wide", "narrow", None),
        P(None, "wide", "narrow", None),
        P(None, "wide", "narrow", None),
    )
    return jax.shard_map(body, mesh=mesh, in_specs=in_specs, out_specs=out_specs, check_vma=False)
```

time: 127 us -> 84.9 us (0.67)
  other arithmetic: 23.8 us -> 0.99 us
  Pallas kernels: 0 us -> 21 us
  starting transfers between devices: 59.5 us -> 42.5 us
  waiting for transfers between devices: 26 us -> 13.2 us
  local copies, waits for them, and re-layouts: 14.6 us -> 5.69 us
    pallas_call x0 -> x5, Pallas kernels: none -> 21 us  [the longest x1 13.2 us: body(): call(functools.partial(main_kernel, span_x, span_y, slots), [((8, cells,...]
    ppermute x16 -> x10, starting transfers between devices: 44.2 us -> 28.4 us  [the longest x5 20.7 us: swap(): lax.ppermute(high, axis, forward)]
    ppermute x16 -> x10, waiting for transfers between devices: 14 us -> 2.95 us  [the longest x5 2.94 us: swap(): lax.ppermute(low, axis, backward)]
    unnamed x15 -> x0, other arithmetic: 6.92 us -> none
    select_n x7 -> x0, other arithmetic: 5.64 us -> none  [the longest x3 1.71 us: body(): jnp.take(incoming, recv_slot[0], axis=1)]
    slice x31 -> x0, local copies, waits for them, and re-layouts: 4.71 us -> none  [the longest x2 3.31 us: extended(): lax.slice_in_dim(block, 0, width, axis=dim)]
    another operation x9 -> x0, other arithmetic: 4.1 us -> none
    gather x2 -> x0, local copies, waits for them, and re-layouts: 3.07 us -> none  [the longest x1 2.08 us: body(): outgoing = jnp.take(flat, send_lines.reshape(-1), axis=1)]
  transfers between devices with their start and end apart: 17 -> 11, of which waited for: 5 -> 3; matrix products, arithmetic and copies ran while one was open for 25% -> 1% of each run, Pallas kernels for 0% -> 18%
where the time goes in v1:
time: 84.9 us; the launch traced here: 84.2 us
  starting transfers between devices  42.5 us (50%)
  Pallas kernels  21 us (25%)
  waiting for transfers between devices  13.2 us (16%)
  local copies, waits for them, and re-layouts  5.69 us (7%)
  other arithmetic  0.99 us (1%)
  between operations  0.87 us (1%)
    ppermute x5, starting transfers between devices, swap(): lax.ppermute(high, axis, forward)  20.7 us
    all_to_all x1, starting transfers between devices, body(): lax.all_to_all(outgoing, ('wide', 'narrow'), split_axis=0, concat_axis=0,...  14.1 us
    pallas_call x1, Pallas kernels, body(): call(functools.partial(main_kernel, span_x, span_y, slots), [((8, cells,...  13.2 us
    all_to_all x1, waiting for transfers between devices, body(): lax.all_to_all(outgoing, ('wide', 'narrow'), split_axis=0, concat_axis=0,...  10.2 us
    ppermute x5, starting transfers between devices, swap(): lax.ppermute(low, axis, backward)  7.71 us
    unnamed x18, local copies, waits for them, and re-layouts  5.49 us
    pallas_call x1, Pallas kernels, body(): call(functools.partial(prep_kernel, span_x, span_y, region_kappa.shape[0]...  3.21 us
    ppermute x5, waiting for transfers between devices, swap(): lax.ppermute(low, axis, backward)  2.94 us
  transfers between devices with their start and end apart: 11, of which 3 were waited for; matrix products, arithmetic and copies ran while one was open for 1% of the time, Pallas kernels for 18%

profile of v1, /device:TPU:1, one launch (start us, length us, event | category | flops | bytes accessed | tf_op | source)
XLA Modules:
  0.0 84.2 jit_solution(18012397576938957476)
XLA Ops:
  0.6 0.0 copy-start.8
  0.6 0.0 copy-start.7
  0.7 0.0 copy-start
  0.7 1.0 %copy-done = f32[3,8,32,128]{3,2,1,0:T(8,128)S(1)} copy-done((f32[3,8,32,128]{3,2,1,0:T(8,128)S(1)}, f32[3,8,32,128]{3,2,1,0:T(8,128)}, u32[]{:S(2)}) %copy-start) | copy-done | bytes 393240
  1.7 0.0 copy-start.4
  1.7 1.1 %copy-done.4 = f32[3,16,32,128]{3,2,1,0:T(8,128)S(1)} copy-done((f32[3,16,32,128]{3,2,1,0:T(8,128)S(1)}, f32[3,16,32,128]{3,2,1,0:T(8,128)}, u32[]{:S(2)}) %copy-start.4) | copy-done | bytes 786456
  2.8 0.9 %copy-done.5 = s32[16,32,128]{2,1,0:T(8,128)S(1)} copy-done((s32[16,32,128]{2,1,0:T(8,128)S(1)}, s32[16,32,128]{2,1,0:T(8,128)}, u32[]{:S(2)}) %copy-start.5) | copy-done | bytes 262168
  3.7 0.0 copy-start.6
  3.7 0.7 copy-done.6
  4.4 3.2 %prep.1 = (f32[4,512,128]{2,1,0:T(8,128)S(1)}, f32[32,32,128]{2,1,0:T(8,128)S(1)}, f32[32,32,128]{2,1,0:T(8,128)}, f32[32,16,128]{2,1,0:T(8,128)S(1)}, f32[32,16...) custom-call(f32[16]{0:T(128)S(1)} %copy-done.6, ...), custom_call_target="tpu_custom_call" | custom-call | tf_op jit(solution)/shard_map/prep/pallas_call | solution.py:319
  7.6 4.1 %collective-permute-start = (f32[32,32,128]{2,1,0:T(8,128)}, f32[32,32,128]{2,1,0:T(8,128)S(1)}, u32[]{:S(2)}, u32[]{:S(2)}) collective-permute-start(f32[32,32,128]{2,1,0:T(8,128)} %get-tuple-element.19), channel_id=1, source_target_pairs={{0,8},{8,16},{16,24},{24,32},{32,40},{40,48},{48,56},{56,64},{64,7... | collective-permute-start | bytes 1572872 | tf_op jit(solution)/shard_map/ppermute | solution.py:300
  11.7 1.3 %collective-permute-start.1 = (f32[32,32,128]{2,1,0:T(8,128)S(1)}, f32[32,32,128]{2,1,0:T(8,128)S(1)}, u32[]{:S(2)}, u32[]{:S(2)}) collective-permute-start(f32[32,32,128]{2,1,0:T(8,128)S(1)} %get-tuple-element.20), channel_id=1, source_target_pairs={{8,0},{16,8},{24,16},{32,24},{40,32},{48,40},{56,48},{64,56},{72,6... | collective-permute-start | bytes 1572872 | tf_op jit(solution)/shard_map/ppermute | solution.py:300
  13.0 4.4 %collective-permute-start.2 = (f32[32,16,128]{2,1,0:T(8,128)}, f32[32,16,128]{2,1,0:T(8,128)S(1)}, u32[]{:S(2)}, u32[]{:S(2)}) collective-permute-start(f32[32,16,128]{2,1,0:T(8,128)} %get-tuple-element.21), channel_id=1, source_target_pairs={{0,1},{1,2},{2,3},{3,4},{4,5},{5,6},{6,7},{8,9},{9,10},{10,11},{11... | collective-permute-start | bytes 786440 | tf_op jit(solution)/shard_map/ppermute | solution.py:300
  17.4 1.9 %collective-permute-start.3 = (f32[32,16,128]{2,1,0:T(8,128)S(1)}, f32[32,16,128]{2,1,0:T(8,128)S(1)}, u32[]{:S(2)}, u32[]{:S(2)}) collective-permute-start(f32[32,16,128]{2,1,0:T(8,128)S(1)} %get-tuple-element.22), channel_id=1, source_target_pairs={{1,0},{2,1},{3,2},{4,3},{5,4},{6,5},{7,6},{9,8},{10,9},{11,10},{12... | collective-permute-start | bytes 786440 | tf_op jit(solution)/shard_map/ppermute | solution.py:300
  19.3 4.9 %collective-permute-start.6 = (f32[3,32,128]{2,1,0:T(8,128)}, f32[3,32,128]{2,1,0:T(8,128)}, u32[]{:S(2)}, u32[]{:S(2)}) collective-permute-start(f32[3,32,128]{2,1,0:T(8,128)} %get-tuple-element.27), channel_id=1, source_target_pairs={{0,8},{8,16},{16,24},{24,32},{32,40},{40,48},{48,56},{56,64},{64,7... | collective-permute-start | bytes 147464 | tf_op jit(solution)/shard_map/ppermute | solution.py:300
  24.2 0.0 copy-done.8
  24.2 0.1 broadcast_add_fusion
  24.3 0.0 copy-done.7
  24.3 0.1 copy.10
  24.4 0.1 eq.30
  24.5 0.2 fusion.1.hot
  24.7 0.0 collective-permute-done.2.nlo
  24.8 0.6 collective-permute-done.3.nhi
  25.4 0.1 corner.1
  25.4 4.3 %collective-permute-start.4 = (f32[128,128]{1,0:T(8,128)S(1)}, f32[128,128]{1,0:T(8,128)S(1)}, u32[]{:S(2)}, u32[]{:S(2)}) collective-permute-start(f32[128,128]{1,0:T(8,128)S(1)} %get-tuple-element.23), channel_id=1, source_target_pairs={{0,8},{8,16},{16,24},{24,32},{32,40},{40,48},{48,56},{56,64},{64,7... | collective-permute-start | bytes 196616 | tf_op jit(solution)/shard_map/ppermute | solution.py:300
  29.7 1.3 %collective-permute-start.5 = (f32[128,128]{1,0:T(8,128)S(1)}, f32[128,128]{1,0:T(8,128)S(1)}, u32[]{:S(2)}, u32[]{:S(2)}) collective-permute-start(f32[128,128]{1,0:T(8,128)S(1)} %get-tuple-element.24), channel_id=1, source_target_pairs={{8,0},{16,8},{24,16},{32,24},{40,32},{48,40},{56,48},{64,56},{72,6... | collective-permute-start | bytes 196616 | tf_op jit(solution)/shard_map/ppermute | solution.py:300
  31.0 0.1 add_convert_fusion.flags
  31.1 0.0 collective-permute-done.4.clo
  31.1 1.3 %collective-permute-start.7 = (f32[3,32,128]{2,1,0:T(8,128)}, f32[3,32,128]{2,1,0:T(8,128)}, u32[]{:S(2)}, u32[]{:S(2)}) collective-permute-start(f32[3,32,128]{2,1,0:T(8,128)} %get-tuple-element.28), channel_id=1, source_target_pairs={{8,0},{16,8},{24,16},{32,24},{40,32},{48,40},{56,48},{64,56},{72,6... | collective-permute-start | bytes 147464 | tf_op jit(solution)/shard_map/ppermute | solution.py:300
  32.4 2.3 %collective-permute-done.5.chi = f32[128,128]{1,0:T(8,128)S(1)} collective-permute-done((f32[128,128]{1,0:T(8,128)S(1)}, f32[128,128]{1,0:T(8,128)S(1)}, u32[]{:S(2)}, u32[]{:S(2)}) %collective-permute-start.5) | collective-permute-done | bytes 65568 | tf_op jit(solution)/shard_map/ppermute | solution.py:300
  34.7 3.1 %collective-permute-start.8 = (f32[3,8,128]{2,1,0:T(8,128)}, f32[3,8,128]{2,1,0:T(8,128)S(1)}, u32[]{:S(2)}, u32[]{:S(2)}) collective-permute-start(f32[3,8,128]{2,1,0:T(8,128)} %get-tuple-element.29), channel_id=1, source_target_pairs={{0,1},{1,2},{2,3},{3,4},{4,5},{5,6},{6,7},{8,9},{9,10},{10,11},{11... | collective-permute-start | bytes 36872 | tf_op jit(solution)/shard_map/ppermute | solution.py:300
  37.8 0.0 collective-permute-done.wlo
  37.8 1.9 %collective-permute-start.9 = (f32[3,8,128]{2,1,0:T(8,128)}, f32[3,8,128]{2,1,0:T(8,128)}, u32[]{:S(2)}, u32[]{:S(2)}) collective-permute-start(f32[3,8,128]{2,1,0:T(8,128)} %get-tuple-element.30), channel_id=1, source_target_pairs={{1,0},{2,1},{3,2},{4,3},{5,4},{6,5},{7,6},{9,8},{10,9},{11,10},{12... | collective-permute-start | bytes 36872 | tf_op jit(solution)/shard_map/ppermute | solution.py:300
  39.7 0.0 collective-permute-done.1.whi
  39.8 13.2 %sweeps.1 = (f32[8,512,128]{2,1,0:T(8,128)}, bf16[128,16,128]{2,1,0:T(8,128)(2,1)}) custom-call(f32[4]{0:T(128)S(1)} %add_convert_fusion.flags, f32[8,512,128]{2,1,0:T(8,128)} %bitcast.20, f32[4,512,128]{2,1,0:T(8,128)S(1)} %get-tuple-element.18.dk, f32[32,32,128]{2,1,0:T(8,128)S(1)} %collective-permute-done.wlo, ...), custom_call_target="tpu_custom_call" | custom-call | tf_op jit(solution)/shard_map/sweeps/pallas_call | solution.py:347
  52.9 14.1 %all-to-all-start = ((bf16[128,16,128]{2,1,0:T(8,128)(2,1)}), bf16[128,16,128]{2,1,0:T(8,128)(2,1)}, u32[]{:S(2)}, u32[]{:S(2)}) async-start(bf16[128,16,128]{2,1,0:T(8,128)(2,1)} %get-tuple-element.26), calls=%async_computation | async-start | bytes 1048576 | tf_op jit(solution)/shard_map/all_to_all | solution.py:355
  67.1 0.6 fusion.hot
  67.7 0.0 collective-permute-done.8.vnlo
  67.7 0.0 collective-permute-done.9.vnhi
  67.7 0.0 collective-permute-done.6.vwlo
  67.7 0.0 collective-permute-done.7.vwhi
  67.7 0.0 copy-done.1
  67.7 1.7 %flow.1 = f32[3,256,128]{2,1,0:T(8,128)S(1)} custom-call(f32[3,256,128]{2,1,0:T(8,128)S(1)} %bitcast.15, f32[3,32,128]{2,1,0:T(8,128)} %collective-permute-done.6.vwlo, f32[3,32,128]{2,1,0:T(8,128)} %collective-permute-done.7.vwhi, f32[3,8,128]{2,1,0:T(8,128)S(1)} %collective-permute-done.8.vnlo, f32[3,8,128]{2,1,0:T(8,128)} %collective-permute-done.9.vnhi), custom_call_target="tpu_custom_call" | custom-call | tf_op jit(solution)/shard_map/flow/pallas_call | solution.py:358
  69.4 0.0 copy-start.2
  69.4 0.7 copy-done.2
  70.2 10.2 %all-to-all-done.got = bf16[128,16,128]{2,1,0:T(8,128)(2,1)} async-done(((bf16[128,16,128]{2,1,0:T(8,128)(2,1)}), bf16[128,16,128]{2,1,0:T(8,128)(2,1)}, u32[]{:S(2)}, u32[]{:S(2)}) %all-to-all-start) | async-done | bytes 524320 | tf_op jit(solution)/shard_map/all_to_all | solution.py:355
  80.4 1.0 %copy-done.3 = f32[3,256,128]{2,1,0:T(8,128)S(1)} copy-done((f32[3,256,128]{2,1,0:T(8,128)S(1)}, f32[3,256,128]{2,1,0:T(8,128)}, u32[]{:S(2)}) %copy-start.3) | copy-done | bytes 393240
  81.4 2.8 %last.1 = (bf16[768,128]{1,0:T(8,128)(2,1)}, f32[768,128]{1,0:T(8,128)}) custom-call(bf16[768,2048]{1,0:T(8,128)(2,1)S(1)} %fusion.hot, bf16[128,16,128]{2,1,0:T(8,128)(2,1)} %all-to-all-done.got, f32[768,128]{1,0:T(8,128)S(1)} %bitcast.16), custom_call_target="tpu_custom_call" | custom-call | tf_op jit(solution)/shard_map/last/pallas_call | solution.py:365
  (7 shorter events, 0.0 us)
Async XLA Ops:
  0.6 23.6 %copy-start.8 = (s32[1,256]{1,0:T(1,128)S(1)}, s32[1,256]{1,0:T(1,128)}, u32[]{:S(2)}) copy-start(s32[1,256]{1,0:T(1,128)} %param.12) | copy-start | bytes 3076
  0.6 23.6 %copy-start.7 = (s32[1,128,4]{1,2,0:T(4,128)S(1)}, s32[1,128,4]{1,2,0:T(4,128)}, u32[]{:S(2)}) copy-start(s32[1,128,4]{1,2,0:T(4,128)} %param.11) | copy-start | bytes 6148
  0.7 1.0 %copy-start = (f32[3,8,32,128]{3,2,1,0:T(8,128)S(1)}, f32[3,8,32,128]{3,2,1,0:T(8,128)}, u32[]{:S(2)}) copy-start(f32[3,8,32,128]{3,2,1,0:T(8,128)} %param.13) | copy-start | bytes 1179652
  1.7 1.1 %copy-start.4 = (f32[3,16,32,128]{3,2,1,0:T(8,128)S(1)}, f32[3,16,32,128]{3,2,1,0:T(8,128)}, u32[]{:S(2)}) copy-start(f32[3,16,32,128]{3,2,1,0:T(8,128)} %param.8) | copy-start | bytes 2359300
  2.8 0.9 %copy-start.5 = (s32[16,32,128]{2,1,0:T(8,128)S(1)}, s32[16,32,128]{2,1,0:T(8,128)}, u32[]{:S(2)}) copy-start(s32[16,32,128]{2,1,0:T(8,128)} %param.9) | copy-start | bytes 786436
  3.7 0.7 copy-start.6
  7.6 30.2 %collective-permute-start = (f32[32,32,128]{2,1,0:T(8,128)}, f32[32,32,128]{2,1,0:T(8,128)S(1)}, u32[]{:S(2)}, u32[]{:S(2)}) collective-permute-start(f32[32,32,128]{2,1,0:T(8,128)} %get-tuple-element.19), channel_id=1, source_target_pairs={{0,8},{8,16},{16,24},{24,32},{32,40},{40,48},{48,56},{56,64},{64,7... | collective-permute-start | bytes 1572872 | tf_op jit(solution)/shard_map/ppermute | solution.py:300
  11.7 28.1 %collective-permute-start.1 = (f32[32,32,128]{2,1,0:T(8,128)S(1)}, f32[32,32,128]{2,1,0:T(8,128)S(1)}, u32[]{:S(2)}, u32[]{:S(2)}) collective-permute-start(f32[32,32,128]{2,1,0:T(8,128)S(1)} %get-tuple-element.20), channel_id=1, source_target_pairs={{8,0},{16,8},{24,16},{32,24},{40,32},{48,40},{56,48},{64,56},{72,6... | collective-permute-start | bytes 1572872 | tf_op jit(solution)/shard_map/ppermute | solution.py:300
  13.0 11.8 %collective-permute-start.2 = (f32[32,16,128]{2,1,0:T(8,128)}, f32[32,16,128]{2,1,0:T(8,128)S(1)}, u32[]{:S(2)}, u32[]{:S(2)}) collective-permute-start(f32[32,16,128]{2,1,0:T(8,128)} %get-tuple-element.21), channel_id=1, source_target_pairs={{0,1},{1,2},{2,3},{3,4},{4,5},{5,6},{6,7},{8,9},{9,10},{10,11},{11... | collective-permute-start | bytes 786440 | tf_op jit(solution)/shard_map/ppermute | solution.py:300
  17.4 8.0 %collective-permute-start.3 = (f32[32,16,128]{2,1,0:T(8,128)S(1)}, f32[32,16,128]{2,1,0:T(8,128)S(1)}, u32[]{:S(2)}, u32[]{:S(2)}) collective-permute-start(f32[32,16,128]{2,1,0:T(8,128)S(1)} %get-tuple-element.22), channel_id=1, source_target_pairs={{1,0},{2,1},{3,2},{4,3},{5,4},{6,5},{7,6},{9,8},{10,9},{11,10},{12... | collective-permute-start | bytes 786440 | tf_op jit(solution)/shard_map/ppermute | solution.py:300
  19.3 48.4 %collective-permute-start.6 = (f32[3,32,128]{2,1,0:T(8,128)}, f32[3,32,128]{2,1,0:T(8,128)}, u32[]{:S(2)}, u32[]{:S(2)}) collective-permute-start(f32[3,32,128]{2,1,0:T(8,128)} %get-tuple-element.27), channel_id=1, source_target_pairs={{0,8},{8,16},{16,24},{24,32},{32,40},{40,48},{48,56},{56,64},{64,7... | collective-permute-start | bytes 147464 | tf_op jit(solution)/shard_map/ppermute | solution.py:300
  25.4 5.7 %collective-permute-start.4 = (f32[128,128]{1,0:T(8,128)S(1)}, f32[128,128]{1,0:T(8,128)S(1)}, u32[]{:S(2)}, u32[]{:S(2)}) collective-permute-start(f32[128,128]{1,0:T(8,128)S(1)} %get-tuple-element.23), channel_id=1, source_target_pairs={{0,8},{8,16},{16,24},{24,32},{32,40},{40,48},{48,56},{56,64},{64,7... | collective-permute-start | bytes 196616 | tf_op jit(solution)/shard_map/ppermute | solution.py:300
  29.7 5.0 %collective-permute-start.5 = (f32[128,128]{1,0:T(8,128)S(1)}, f32[128,128]{1,0:T(8,128)S(1)}, u32[]{:S(2)}, u32[]{:S(2)}) collective-permute-start(f32[128,128]{1,0:T(8,128)S(1)} %get-tuple-element.24), channel_id=1, source_target_pairs={{8,0},{16,8},{24,16},{32,24},{40,32},{48,40},{56,48},{64,56},{72,6... | collective-permute-start | bytes 196616 | tf_op jit(solution)/shard_map/ppermute | solution.py:300
  31.1 36.6 %collective-permute-start.7 = (f32[3,32,128]{2,1,0:T(8,128)}, f32[3,32,128]{2,1,0:T(8,128)}, u32[]{:S(2)}, u32[]{:S(2)}) collective-permute-start(f32[3,32,128]{2,1,0:T(8,128)} %get-tuple-element.28), channel_id=1, source_target_pairs={{8,0},{16,8},{24,16},{32,24},{40,32},{48,40},{56,48},{64,56},{72,6... | collective-permute-start | bytes 147464 | tf_op jit(solution)/shard_map/ppermute | solution.py:300
  34.7 33.0 %collective-permute-start.8 = (f32[3,8,128]{2,1,0:T(8,128)}, f32[3,8,128]{2,1,0:T(8,128)S(1)}, u32[]{:S(2)}, u32[]{:S(2)}) collective-permute-start(f32[3,8,128]{2,1,0:T(8,128)} %get-tuple-element.29), channel_id=1, source_target_pairs={{0,1},{1,2},{2,3},{3,4},{4,5},{5,6},{6,7},{8,9},{9,10},{10,11},{11... | collective-permute-start | bytes 36872 | tf_op jit(solution)/shard_map/ppermute | solution.py:300
  37.8 29.9 %collective-permute-start.9 = (f32[3,8,128]{2,1,0:T(8,128)}, f32[3,8,128]{2,1,0:T(8,128)}, u32[]{:S(2)}, u32[]{:S(2)}) collective-permute-start(f32[3,8,128]{2,1,0:T(8,128)} %get-tuple-element.30), channel_id=1, source_target_pairs={{1,0},{2,1},{3,2},{4,3},{5,4},{6,5},{7,6},{9,8},{10,9},{11,10},{12... | collective-permute-start | bytes 36872 | tf_op jit(solution)/shard_map/ppermute | solution.py:300
  52.9 14.8 %copy-start.1 = (f32[3,8,32,128]{3,2,1,0:T(8,128)S(1)}, f32[3,8,32,128]{3,2,1,0:T(8,128)}, u32[]{:S(2)}) copy-start(f32[3,8,32,128]{3,2,1,0:T(8,128)} %param.13) | copy-start | bytes 1179652
  52.9 27.5 %all-to-all-start = ((bf16[128,16,128]{2,1,0:T(8,128)(2,1)}), bf16[128,16,128]{2,1,0:T(8,128)(2,1)}, u32[]{:S(2)}, u32[]{:S(2)}) async-start(bf16[128,16,128]{2,1,0:T(8,128)(2,1)} %get-tuple-element.26), calls=%async_computation | async-start | bytes 1048576 | tf_op jit(solution)/shard_map/all_to_all | solution.py:355
  69.4 0.7 copy-start.2
  80.4 1.0 %copy-start.3 = (f32[3,256,128]{2,1,0:T(8,128)S(1)}, f32[3,256,128]{2,1,0:T(8,128)}, u32[]{:S(2)}) copy-start(f32[3,256,128]{2,1,0:T(8,128)} %copy-done.2) | copy-start | bytes 1179652

commit v2 on v1

v2 whole, which is shorter than its diff:
```python
import functools

import jax
import jax.numpy as jnp
from jax import lax
from jax.experimental import pallas as pl
from jax.experimental.pallas import tpu as pltpu
from jax.sharding import PartitionSpec as P

DT = 0.25
VISC = 0.5
F32 = jnp.float32
BF16 = jnp.bfloat16
DEEP = 3
FLAT = 2
ROWS = 40
OFF = 8
MIB = 1 << 20
LIMIT_IN = 48
LIMIT_OUT = 48


def strip(start, size, stride):
    return pl.ds(start, size, stride=stride)


def planes_of():
    return 8 * DEEP + 4 * FLAT + 3


def kappa_of(label, rk, regions):
    kappa = jnp.zeros(label.shape, F32)
    for r in range(regions):
        kappa = jnp.where(label == 2 * regions + r, rk[r], kappa)
    return kappa


class Copies:
    def __init__(self, sems):
        self.sems = sems
        self.count = 0

    def start(self, source, target):
        one = pltpu.make_async_copy(source, target, self.sems.at[self.count])
        one.start()
        self.count += 1
        return one


def faces_kernel(
    span_x, span_y, regions, rk, pot, src, lab, vel, wlo, whi, nlo, nhi, all_pot, all_src, all_lab, all_vel, sems
):
    les_x = vel.shape[1]
    flow = 8 * DEEP + 4 * FLAT
    copies = Copies(sems)
    waits = [
        copies.start(source, target)
        for source, target in ((lab, all_lab), (src, all_src), (vel, all_vel), (pot, all_pot))
    ]
    for one in waits[:2]:
        one.wait()
    for side, (wide, narrow) in enumerate(((wlo, nlo), (whi, nhi))):
        for d in range(FLAT):
            x = span_x - FLAT + d if side else d
            y = span_y - 1 - d if side else d
            label = all_lab[x]
            for c in range(3):
                wide[8 * DEEP + 4 * d + c] = jnp.where(label < regions, all_src[c, x], 0.0)
            wide[8 * DEEP + 4 * d + 3] = kappa_of(label, rk, regions)
            label = all_lab[:, y, :]
            for c in range(3):
                narrow[8 * DEEP + 4 * d + c] = jnp.where(label < regions, all_src[c, :, y, :], 0.0)
            narrow[8 * DEEP + 4 * d + 3] = kappa_of(label, rk, regions)
    waits[2].wait()
    for side, (wide, narrow) in enumerate(((wlo, nlo), (whi, nhi))):
        for c in range(3):
            wide[flow + c] = all_vel[c, side * (les_x - 1)]
            narrow[flow + c, pl.ds(0, les_x), :] = all_vel[c, :, side * (span_y - 1), :]
            narrow[flow + c, pl.ds(les_x, span_x - les_x), :] = jnp.zeros((span_x - les_x, vel.shape[3]), F32)
    waits[3].wait()
    for side, (wide, narrow) in enumerate(((wlo, nlo), (whi, nhi))):
        for d in range(DEEP):
            x = span_x - DEEP + d if side else d
            y = span_y - 1 - d if side else d
            for c in range(8):
                wide[8 * d + c] = all_pot[c, x]
                narrow[8 * d + c] = all_pot[c, :, y, :]


def corner_kernel(span_x, nlo, nhi, clo, chi):
    planes = 8 * DEEP + 4 * FLAT
    for d in range(FLAT):
        for side, ref in enumerate((nlo, nhi)):
            rows = pl.ds((d * 2 + side) * planes, planes)
            clo[rows, :] = ref[:planes, d, :]
            chi[rows, :] = ref[:planes, span_x - 1 - d, :]


def place(c, d):
    return 8 * d + c if c < 8 else 8 * DEEP + 4 * d + c - 8


def at(x):
    return (x + DEEP) * ROWS + OFF


def scale_plane(span_x, span_y, flags, field, x):
    line = lax.broadcasted_iota(jnp.int32, (8, field.shape[-1]), 0)
    fx = jnp.where(x < 0, flags[0], jnp.where(x >= span_x, flags[1], 1.0))
    for t in range(5):
        row = at(x) - FLAT + 8 * t
        y = line + (8 * t - FLAT)
        fy = jnp.where(y < 0, flags[2], jnp.where(y >= span_y, flags[3], 1.0))
        kappa = field[3, pl.ds(row, 8), :]
        field[4, pl.ds(row, 8), :] = (fx * fy) / (36.0 + kappa * kappa)


def sweep_plane(old, new, field, x, margin):
    for t in range(5):
        sweep_tile(old, new, field, at(x) - margin + 8 * t)


def over(low, high, do):
    def step(i, carry):
        do(i + low)
        return carry

    lax.fori_loop(0, high - low, step, 0)


def lanes(value):
    depth = value.shape[-1]
    lane = lax.broadcasted_iota(jnp.int32, value.shape, 1)
    ahead = jnp.where(lane == depth - 1, 0.0, pltpu.roll(value, depth - 1, 1))
    back = jnp.where(lane == 0, 0.0, pltpu.roll(value, 1, 1))
    return ahead, back


def sweep_tile(old, new, field, row):
    s6 = 6.0 * field[4, pl.ds(row, 8), :]
    kappa = field[3, pl.ds(row, 8), :]
    sk = kappa * field[4, pl.ds(row, 8), :]
    half = 0.5 * kappa
    total = []
    diff = []
    for c in range(8):
        xf = old[c, pl.ds(row + ROWS, 8), :]
        xb = old[c, pl.ds(row - ROWS, 8), :]
        yf = old[c, pl.ds(row + 1, 8), :]
        yb = old[c, pl.ds(row - 1, 8), :]
        zf, zb = lanes(old[c, pl.ds(row, 8), :])
        total.append((xf + xb) + (yf + yb) + (zf + zb))
        if c % 4 == 3:
            diff.append((xf - xb, yf - yb, zf - zb))
        else:
            diff.append(((xf - xb), (yf - yb), (zf - zb))[c % 4])
    for c in range(3):
        first = (field[c, pl.ds(row, 8), :] + total[c]) + half * diff[7][c]
        second = total[4 + c] - half * diff[3][c]
        new[c, pl.ds(row, 8), :] = s6 * first + sk * second
        new[4 + c, pl.ds(row, 8), :] = s6 * second - sk * first
    first = total[3] + half * (diff[4] + diff[5] + diff[6])
    second = total[7] - half * (diff[0] + diff[1] + diff[2])
    new[3, pl.ds(row, 8), :] = s6 * first + sk * second
    new[7, pl.ds(row, 8), :] = s6 * second - sk * first


def lorentz_tile(now, field, row):
    def grab(c, shift):
        return now[c, pl.ds(row + shift, 8), :]

    kappa = field[3, pl.ds(row, 8), :]

    def part(base):
        a = [grab(base + c, 0) for c in range(3)]
        azf, azb = lanes(a[0])
        bzf, bzb = lanes(a[1])
        curl = [
            (grab(base + 2, 1) - grab(base + 2, -1)) - (bzf - bzb),
            (azf - azb) - (grab(base + 2, ROWS) - grab(base + 2, -ROWS)),
            (grab(base + 1, ROWS) - grab(base + 1, -ROWS)) - (grab(base, 1) - grab(base, -1)),
        ]
        phi = grab(base + 3, 0)
        pzf, pzb = lanes(phi)
        grad = [
            grab(base + 3, ROWS) - grab(base + 3, -ROWS),
            grab(base + 3, 1) - grab(base + 3, -1),
            pzf - pzb,
        ]
        return curl, [a[c] + 0.5 * grad[c] for c in range(3)]

    real_b, field_re = part(0)
    imag_b, field_im = part(4)
    cur_re = [field[c, pl.ds(row, 8), :] + kappa * field_im[c] for c in range(3)]
    cur_im = [-kappa * field_re[c] for c in range(3)]
    force = []
    for c in range(3):
        n = (c + 1) % 3
        f = (c + 2) % 3
        value = (cur_re[n] * real_b[f] - cur_re[f] * real_b[n]) + (
            cur_im[n] * imag_b[f] - cur_im[f] * imag_b[n]
        )
        force.append(jnp.where(kappa > 0.0, 0.25 * value, 0.0))
    return force


def force_plane(now, field, force, span_y, x):
    for t in range(span_y // 8):
        f = lorentz_tile(now, field, at(x) + 8 * t)
        rows = pl.ds(pl.multiple_of(x * span_y + 8 * t, 8), 8)
        for c in range(3):
            force[c, rows, :] = f[c]


def stored(x):
    return pl.ds((x + DEEP) * ROWS, ROWS + OFF)


def kept(i):
    return pl.ds(i * (ROWS + OFF), ROWS + OFF)


def inner_kernel(
    span_x, span_y, regions, flags, rk, pot, src, lab, nlo, nhi,
    nxt, halves, nexts, fields, force, s0, s1, s2, field, some, tags, sems,
):
    copies = Copies(sems)
    early = [copies.start(lab, tags), copies.start(src, some)]
    late = [
        copies.start(pot.at[:, x], s0.at[:, pl.ds(at(x), span_y), :]) for x in range(span_x)
    ]
    for c in range(12):
        deep = DEEP if c < 8 else FLAT
        ref, part = (s0, c) if c < 8 else (field, c - 8)
        for d in range(deep):
            ref[part, strip(at(0) - 1 - d, span_x, ROWS), :] = nlo[place(c, d)]
            ref[part, strip(at(0) + span_y + d, span_x, ROWS), :] = nhi[place(c, d)]
    for one in early:
        one.wait()

    def lay(x):
        there = pl.ds(pl.multiple_of((x + DEEP) * ROWS + OFF, 8), span_y)
        label = tags[x]
        for c in range(3):
            field[c, there, :] = jnp.where(label < regions, some[c, x], 0.0)
        field[3, there, :] = kappa_of(label, rk, regions)

    over(0, span_x, lay)
    over(0, span_x, lambda x: scale_plane(span_x, span_y, flags, field, x))
    for one in late:
        one.wait()
    over(1, span_x - 1, lambda x: sweep_plane(s0, s1, field, x, 2))
    over(2, span_x - 2, lambda x: sweep_plane(s1, s2, field, x, 1))
    done = [
        copies.start(s2.at[:, pl.ds(at(x), span_y), :], nxt.at[:, x]) for x in range(2, span_x - 2)
    ]
    over(3, span_x - 3, lambda x: force_plane(s2, field, force, span_y, x))
    for c in range(8):
        for i, x in enumerate((1, 2, span_x - 3, span_x - 2)):
            halves[c, kept(i), :] = s1[c, stored(x), :]
        for i, x in enumerate((2, 3, span_x - 4, span_x - 3)):
            nexts[c, kept(i), :] = s2[c, stored(x), :]
    for c in range(5):
        for i, x in enumerate((0, 1, 2, span_x - 3, span_x - 2, span_x - 1)):
            fields[c, kept(i), :] = field[c, stored(x), :]
    for one in done:
        one.wait()


def outer_kernel(
    span_x, span_y, slots, flags, pot, wlo, whi, nlo, nhi, clo, chi, hot, halves, nexts, fields, some_force, old_nxt,
    nxt, out, s0, s1, s2, field, force, sent, sems, sent_sems,
):
    depth = pot.shape[-1]
    planes = 8 * DEEP + 4 * FLAT
    copies = Copies(sems)
    early = []
    late = []
    for d in range(FLAT):
        for ref, x in ((wlo, d - FLAT), (whi, span_x + d)):
            early.append(
                copies.start(ref.at[pl.ds(8 * DEEP + 4 * d, 4)], field.at[pl.ds(0, 4), pl.ds(at(x), span_y), :])
            )
    for d in range(DEEP):
        for ref, x in ((wlo, d - DEEP), (whi, span_x + d)):
            late.append(copies.start(ref.at[pl.ds(8 * d, 8)], s0.at[:, pl.ds(at(x), span_y), :]))
    for x in (0, 1, span_x - 2, span_x - 1):
        late.append(copies.start(pot.at[:, x], s0.at[:, pl.ds(at(x), span_y), :]))
    for c in range(8):
        for i, x in enumerate((1, 2, span_x - 3, span_x - 2)):
            s1[c, stored(x), :] = halves[c, kept(i), :]
        for i, x in enumerate((2, 3, span_x - 4, span_x - 3)):
            s2[c, stored(x), :] = nexts[c, kept(i), :]
    for c in range(3):
        rows = pl.ds(3 * span_y, (span_x - 6) * span_y)
        force[c, rows, :] = some_force[c, rows, :]
    for c in range(8):
        for d in range(DEEP):
            p = place(c, d)
            for x in (0, 1, span_x - 2, span_x - 1):
                s0[c, pl.ds(at(x) - 1 - d, 1), :] = nlo[p, pl.ds(x, 1), :]
                s0[c, pl.ds(at(x) + span_y + d, 1), :] = nhi[p, pl.ds(x, 1), :]
    for one in early:
        one.wait()
    for c in range(5):
        for i, x in enumerate((0, 1, 2, span_x - 3, span_x - 2, span_x - 1)):
            field[c, pl.ds(at(x) - 3, span_y + 6), :] = fields[c, pl.ds(i * (ROWS + OFF) + OFF - 3, span_y + 6), :]
    for c in range(12):
        deep = DEEP if c < 8 else FLAT
        ref, part = (s0, c) if c < 8 else (field, c - 8)
        for d in range(deep - 1):
            for e in range(deep - 1 - d):
                p = place(c, d)
                for source, x in ((clo, -1 - e), (chi, span_x + e)):
                    ref[part, pl.ds(at(x) - 1 - d, 1), :] = source[pl.ds(e * 2 * planes + p, 1), :]
                    ref[part, pl.ds(at(x) + span_y + d, 1), :] = source[pl.ds((e * 2 + 1) * planes + p, 1), :]

    def both(low, high, do):
        over(-high, -low, do)
        over(span_x + low, span_x + high, do)

    both(0, 2, lambda x: scale_plane(span_x, span_y, flags, field, x))
    for one in late:
        one.wait()
    both(-1, 2, lambda x: sweep_plane(s0, s1, field, x, 2))
    both(-2, 1, lambda x: sweep_plane(s1, s2, field, x, 1))
    done = [
        copies.start(s2.at[:, pl.ds(at(x), span_y), :], nxt.at[:, x])
        for x in (0, 1, span_x - 2, span_x - 1)
    ]
    both(-3, 0, lambda x: force_plane(s2, field, force, span_y, x))

    table = jnp.concatenate([force[c].astype(BF16) for c in range(3)], axis=1)
    chunk = 256
    upper = lax.broadcasted_iota(jnp.int32, (chunk // 8, 8, depth), 1) < slots
    for i in range(hot.shape[0] // chunk):
        h = hot[pl.ds(i * chunk, chunk), :]
        picked = jnp.dot(h, table, preferred_element_type=F32)
        got = [
            picked[:, c * depth : (c + 1) * depth].reshape(chunk // 8, 8, depth) for c in range(3)
        ]
        both_parts = jnp.concatenate([jnp.where(upper, got[0], got[1]), got[2]], axis=1)
        rows = pl.ds(i * (chunk // 8), chunk // 8)
        sent[rows] = both_parts.astype(BF16)
        one = pltpu.make_async_copy(sent.at[rows], out.at[rows], sent_sems.at[i])
        one.start()
        done.append(one)
    for one in done:
        one.wait()


def flow_kernel(les_x, span_y, vel, wlo, whi, nlo, nhi, base, s0):
    first = 8 * DEEP + 4 * FLAT
    for c in range(3):
        for x in range(les_x):
            s0[c, pl.ds((x + 1) * ROWS + OFF, span_y), :] = vel[c, pl.ds(x * span_y, span_y), :]
        s0[c, pl.ds(OFF, span_y), :] = wlo[first + c]
        s0[c, pl.ds((les_x + 1) * ROWS + OFF, span_y), :] = whi[first + c]
        s0[c, strip(ROWS + OFF - 1, les_x, ROWS), :] = nlo[first + c, pl.ds(0, les_x), :]
        s0[c, strip(ROWS + OFF + span_y, les_x, ROWS), :] = nhi[first + c, pl.ds(0, les_x), :]

    def step(x, carry):
        for t in range(span_y // 8):
            row = (x + 1) * ROWS + OFF + 8 * t
            middle = [s0[c, pl.ds(row, 8), :] for c in range(3)]
            for c in range(3):
                xf = s0[c, pl.ds(row + ROWS, 8), :]
                xb = s0[c, pl.ds(row - ROWS, 8), :]
                yf = s0[c, pl.ds(row + 1, 8), :]
                yb = s0[c, pl.ds(row - 1, 8), :]
                zf, zb = lanes(middle[c])
                carried = 0.5 * (middle[0] * (xf - xb) + middle[1] * (yf - yb) + middle[2] * (zf - zb))
                spread = (xf + xb) + (yf + yb) + (zf + zb) - 6.0 * middle[c]
                base[c, pl.ds(pl.multiple_of(x * span_y + 8 * t, 8), 8), :] = middle[c] + DT * (
                    VISC * spread - carried
                )
        return carry

    lax.fori_loop(0, les_x, step, 0)


def last_kernel(slots, column, got, base, les, nxt):
    lines = base.shape[1]
    depth = got.shape[2]
    wide = got[...].astype(F32)
    values = jnp.concatenate(
        [wide[:, 8 * h : 8 * h + 8, :].reshape(-1, depth).astype(BF16) for h in range(2)], axis=1
    )
    want = column[...]
    lane = lax.broadcasted_iota(jnp.int32, want.shape, 1)
    picked = []
    for half in range(2):
        take = jnp.concatenate(
            [
                jnp.where(want == lane + (depth * k - slots * half), 1.0, 0.0).astype(BF16)
                for k in range(values.shape[0] // depth)
            ],
            axis=1,
        )
        picked.append(jnp.dot(take, values, preferred_element_type=F32))
    for c in range(3):
        push = picked[c % 2][:, (c // 2) * depth : (c // 2 + 1) * depth].astype(BF16)
        les[c] = push
        nxt[c] = base[c] + DT * push.astype(F32)


def call(kernel, out, name, scratch=(), smem=0, count=1, hbm=(), hbm_out=(), alias=None, limit=16):
    vmem = pl.BlockSpec(memory_space=pltpu.VMEM)
    specs = [pl.BlockSpec(memory_space=pltpu.SMEM)] * smem + [vmem] * (count - smem)
    for i in hbm:
        specs[i] = pl.BlockSpec(memory_space=pltpu.HBM)
    return pl.pallas_call(
        kernel,
        out_shape=[jax.ShapeDtypeStruct(shape, kind) for shape, kind in out],
        in_specs=specs,
        out_specs=[
            pl.BlockSpec(memory_space=pltpu.HBM) if i in hbm_out else vmem for i in range(len(out))
        ],
        scratch_shapes=[pltpu.VMEM(*one) if isinstance(one, tuple) else one for one in scratch],
        input_output_aliases=alias or {},
        compiler_params=pltpu.CompilerParams(vmem_limit_bytes=limit * MIB),
        name=name,
    )


def swap(low, high, axis):
    count = lax.axis_size(axis)
    forward = [(i, i + 1) for i in range(count - 1)]
    backward = [(target, source) for source, target in forward]
    return lax.ppermute(high, axis, forward), lax.ppermute(low, axis, backward)


def body(potential, source_current, cell_label, region_kappa, send_lines, recv_slot, velocity):
    _, span_x, span_y, depth = potential.shape
    les_x = velocity.shape[1]
    peers, slots = send_lines.shape[1:]
    regions = region_kappa.shape[0]
    cells = span_x * span_y
    lines = les_x * span_y
    planes = planes_of()
    vel = velocity.reshape(3, lines, depth)

    wide = ((planes, span_y, depth), F32)
    narrow = ((planes, span_x, depth), F32)
    wlo, whi, nlo, nhi = call(
        functools.partial(faces_kernel, span_x, span_y, regions),
        [wide, wide, narrow, narrow],
        "faces",
        scratch=[
            (potential.shape, F32),
            (source_current.shape, F32),
            (cell_label.shape, jnp.int32),
            (velocity.shape, F32),
            pltpu.SemaphoreType.DMA((4,)),
        ],
        smem=1, count=5, hbm=(1, 2, 3, 4), limit=60,
    )(region_kappa, potential, source_current, cell_label, velocity)
    nlo, nhi = swap(nlo, nhi, "narrow")
    wlo, whi = swap(wlo, whi, "wide")

    corner = ((FLAT * 2 * (8 * DEEP + 4 * FLAT), depth), F32)
    clo, chi = call(
        functools.partial(corner_kernel, span_x), [corner, corner], "corner", count=2
    )(nlo, nhi)
    clo, chi = swap(clo, chi, "wide")

    pad = (span_x + 2 * DEEP) * ROWS + OFF
    padded = ((8, pad, depth), F32)
    fields = ((5, pad, depth), F32)
    w, n = lax.axis_index("wide"), lax.axis_index("narrow")
    flags = jnp.stack(
        [w > 0, w < lax.axis_size("wide") - 1, n > 0, n < lax.axis_size("narrow") - 1]
    ).astype(F32)
    keep = ROWS + OFF
    nxt, halves, nexts, edge_fields, force = call(
        functools.partial(inner_kernel, span_x, span_y, regions),
        [
            (potential.shape, F32),
            ((8, 4 * keep, depth), F32),
            ((8, 4 * keep, depth), F32),
            ((5, 6 * keep, depth), F32),
            ((3, cells, depth), F32),
        ],
        "inner",
        scratch=[
            padded,
            padded,
            padded,
            fields,
            ((3, span_x, span_y, depth), F32),
            ((span_x, span_y, depth), jnp.int32),
            pltpu.SemaphoreType.DMA((2 + 2 * span_x,)),
        ],
        smem=2, count=7, hbm=(2, 3, 4), hbm_out=(0,), limit=LIMIT_IN,
    )(flags, region_kappa, potential, source_current, cell_label, nlo, nhi)

    sent = jnp.concatenate([send_lines[0], send_lines[0]], axis=1).reshape(-1)
    hot = (sent[:, None] == jnp.arange(cells, dtype=jnp.int32)[None, :]).astype(BF16)
    potential_next, outgoing = call(
        functools.partial(outer_kernel, span_x, span_y, slots),
        [(potential.shape, F32), ((peers, 16, depth), BF16)],
        "outer",
        scratch=[
            padded,
            padded,
            padded,
            fields,
            ((3, cells, depth), F32),
            ((peers, 16, depth), BF16),
            pltpu.SemaphoreType.DMA((2 * FLAT + 2 * DEEP + 8,)),
            pltpu.SemaphoreType.DMA((hot.shape[0] // 256,)),
        ],
        smem=1, count=14, hbm=(1, 2, 3, 13), hbm_out=(0, 1), alias={13: 0}, limit=LIMIT_OUT,
    )(flags, potential, wlo, whi, nlo, nhi, clo, chi, hot, halves, nexts, edge_fields, force, nxt)

    incoming = lax.all_to_all(
        outgoing, ("wide", "narrow"), split_axis=0, concat_axis=0, tiled=True
    )
    slot = recv_slot[0]
    column = jnp.broadcast_to(((slot // slots) * 8 + slot % slots)[:, None], (lines, 128))
    (base,) = call(
        functools.partial(flow_kernel, les_x, span_y),
        [((3, lines, depth), F32)],
        "flow",
        scratch=[((3, (les_x + 2) * ROWS + OFF, depth), F32)],
        count=5,
    )(vel, wlo, whi, nlo, nhi)
    les, velocity_next = call(
        functools.partial(last_kernel, slots),
        [((3, lines, depth), BF16), ((3, lines, depth), F32)],
        "last", count=3,
    )(column, incoming, base)
    block = (3, les_x, span_y, depth)
    return potential_next, les.reshape(block), velocity_next.reshape(block)


def solution(mesh):
    in_specs = (
        P(None, "wide", "narrow", None),
        P(None, "wide", "narrow", None),
        P("wide", "narrow", None),
        P(),
        P(("wide", "narrow"), None, None),
        P(("wide", "narrow"), None),
        P(None, "wide", "narrow", None),
    )
    out_specs = (
        P(None, "wide", "narrow", None),
        P(None, "wide", "narrow", None),
        P(None, "wide", "narrow", None),
    )
    return jax.shard_map(body, mesh=mesh, in_specs=in_specs, out_specs=out_specs, check_vma=False)
```

time: 84.9 us -> 71.2 us (0.84)
  starting transfers between devices: 42.5 us -> 29.2 us
  local copies, waits for them, and re-layouts: 5.69 us -> 0.31 us
  waiting for transfers between devices: 13.2 us -> 17.9 us
    ppermute x5 -> x3, starting transfers between devices: 20.7 us -> 12.7 us  [swap(): lax.ppermute(high, axis, forward)]
    unnamed x18 -> x12, local copies, waits for them, and re-layouts: 5.49 us -> 0.03 us
    ppermute x5 -> x3, starting transfers between devices: 7.71 us -> 4.5 us  [swap(): lax.ppermute(low, axis, backward)]
    all_to_all x1, waiting for transfers between devices: 10.2 us -> 12.8 us  [body(): lax.all_to_all(outgoing, ('wide', 'narrow'), split_axis=0, concat_axis=0,...]
    all_to_all x1, starting transfers between devices: 14.1 us -> 12 us  [body(): lax.all_to_all(outgoing, ('wide', 'narrow'), split_axis=0, concat_axis=0,...]
    ppermute x5 -> x3, waiting for transfers between devices: 2.94 us -> 4.59 us  [swap(): lax.ppermute(low, axis, backward)]
    pallas_call x3 -> x4, Pallas kernels: 19.2 us -> 20.3 us  [the longest x1 8.09 us: body(): call(functools.partial(inner_kernel, span_x, span_y, regions), [(potentia...]
    convert_element_type x1, other arithmetic: 0.24 us -> 1.22 us  [body(): (sent[:, None] == jnp.arange(cells, dtype=jnp.int32)[None, :]).astype(BF16)]
  transfers between devices with their start and end apart: 11 -> 7, of which waited for: 3 -> 3; matrix products, arithmetic and copies ran while one was open for 1% -> 2% of each run, Pallas kernels for 18% -> 13%
where the time goes in v2:
time: 71.2 us; the launch traced here: 70.8 us
  starting transfers between devices  29.2 us (41%)
  Pallas kernels  21.2 us (30%)
  waiting for transfers between devices  17.9 us (25%)
  other arithmetic  1.33 us (2%)
  between operations  0.87 us (1%)
    all_to_all x1, waiting for transfers between devices, body(): lax.all_to_all(outgoing, ('wide', 'narrow'), split_axis=0, concat_axis=0,...  12.8 us
    ppermute x3, starting transfers between devices, swap(): lax.ppermute(high, axis, forward)  12.7 us
    all_to_all x1, starting transfers between devices, body(): lax.all_to_all(outgoing, ('wide', 'narrow'), split_axis=0, concat_axis=0,...  12 us
    pallas_call x1, Pallas kernels, body(): call(functools.partial(inner_kernel, span_x, span_y, regions), [(potentia...  8.09 us
    pallas_call x1, Pallas kernels, body(): call(functools.partial(outer_kernel, span_x, span_y, slots), [(potential....  6.81 us
    ppermute x3, waiting for transfers between devices, swap(): lax.ppermute(low, axis, backward)  4.59 us
    ppermute x3, starting transfers between devices, swap(): lax.ppermute(low, axis, backward)  4.5 us
    pallas_call x1, Pallas kernels, body(): call(functools.partial(faces_kernel, span_x, span_y, regions), [wide, wid...  4.08 us
  transfers between devices with their start and end apart: 7, of which 3 were waited for; matrix products, arithmetic and copies ran while one was open for 2% of the time, Pallas kernels for 13%

profile of v2, /device:TPU:1, one launch (start us, length us, event | category | flops | bytes accessed | tf_op | source)
XLA Modules:
  0.0 70.8 jit_solution(8907920676225627103)
XLA Ops:
  0.6 0.0 copy-start.3
  0.6 0.0 copy-start
  0.7 0.0 copy-start.2
  0.7 0.0 copy-start.4
  0.7 4.1 %faces.1 = (f32[35,32,128]{2,1,0:T(8,128)}, f32[35,32,128]{2,1,0:T(8,128)}, f32[35,16,128]{2,1,0:T(8,128)}, f32[35,16,128]{2,1,0:T(8,128)}) custom-call(f32[16]{0:T(128)} %rk.3, f32[8,16,32,128]{3,2,1,0:T(8,128)} %pot.5, f32[3,16,32,128]{3,2,1,0:T(8,128)} %src.3, s32[16,32,128]{2,1,0:T(8,128)} %lab.3, f32[3,8,32,128]{3,2,1,0:T(8,128)} %vel.1), custom_call_target="tpu_custom_call" | custom-call | tf_op jit(solution)/shard_map/faces/pallas_call | solution.py:445
  4.8 4.1 %collective-permute-start = (f32[35,32,128]{2,1,0:T(8,128)}, f32[35,32,128]{2,1,0:T(8,128)S(1)}, u32[]{:S(2)}, u32[]{:S(2)}) collective-permute-start(f32[35,32,128]{2,1,0:T(8,128)} %get-tuple-element.18), channel_id=1, source_target_pairs={{0,8},{8,16},{16,24},{24,32},{32,40},{40,48},{48,56},{56,64},{64,7... | collective-permute-start | bytes 1720328 | tf_op jit(solution)/shard_map/ppermute | solution.py:430
  8.8 1.3 %collective-permute-start.1 = (f32[35,32,128]{2,1,0:T(8,128)}, f32[35,32,128]{2,1,0:T(8,128)S(1)}, u32[]{:S(2)}, u32[]{:S(2)}) collective-permute-start(f32[35,32,128]{2,1,0:T(8,128)} %get-tuple-element.19), channel_id=1, source_target_pairs={{8,0},{16,8},{24,16},{32,24},{40,32},{48,40},{56,48},{64,56},{72,6... | collective-permute-start | bytes 1720328 | tf_op jit(solution)/shard_map/ppermute | solution.py:430
  10.1 4.4 %collective-permute-start.2 = (f32[35,16,128]{2,1,0:T(8,128)}, f32[35,16,128]{2,1,0:T(8,128)S(1)}, u32[]{:S(2)}, u32[]{:S(2)}) collective-permute-start(f32[35,16,128]{2,1,0:T(8,128)} %get-tuple-element.20), channel_id=1, source_target_pairs={{0,1},{1,2},{2,3},{3,4},{4,5},{5,6},{6,7},{8,9},{9,10},{10,11},{11... | collective-permute-start | bytes 860168 | tf_op jit(solution)/shard_map/ppermute | solution.py:430
  14.5 1.9 %collective-permute-start.3 = (f32[35,16,128]{2,1,0:T(8,128)}, f32[35,16,128]{2,1,0:T(8,128)S(1)}, u32[]{:S(2)}, u32[]{:S(2)}) collective-permute-start(f32[35,16,128]{2,1,0:T(8,128)} %get-tuple-element.21), channel_id=1, source_target_pairs={{1,0},{2,1},{3,2},{4,3},{5,4},{6,5},{7,6},{9,8},{10,9},{11,10},{12... | collective-permute-start | bytes 860168 | tf_op jit(solution)/shard_map/ppermute | solution.py:430
  16.5 0.0 copy-done.4
  16.5 0.1 copy.11
  16.6 0.1 eq.17
  16.7 1.2 %fusion.hot = bf16[1024,512]{1,0:T(8,128)(2,1)} fusion(s32[1024]{0:T(1024)S(1)} %eq.17), kind=kLoop, calls=%fused_computation.1 | loop fusion | flops 1048576 | bytes 1052672 | tf_op jit(solution)/shard_map/convert_element_type | solution.py:498
  17.9 0.5 collective-permute-done.2.nlo
  18.4 4.6 %collective-permute-done.3.nhi = f32[35,16,128]{2,1,0:T(8,128)S(1)} collective-permute-done((f32[35,16,128]{2,1,0:T(8,128)}, f32[35,16,128]{2,1,0:T(8,128)S(1)}, u32[]{:S(2)}, u32[]{:S(2)}) %collective-permute-start.3) | collective-permute-done | bytes 286752 | tf_op jit(solution)/shard_map/ppermute | solution.py:430
  23.0 0.1 corner.1
  23.1 4.3 %collective-permute-start.4 = (f32[128,128]{1,0:T(8,128)S(1)}, f32[128,128]{1,0:T(8,128)S(1)}, u32[]{:S(2)}, u32[]{:S(2)}) collective-permute-start(f32[128,128]{1,0:T(8,128)S(1)} %get-tuple-element.22), channel_id=1, source_target_pairs={{0,8},{8,16},{16,24},{24,32},{32,40},{40,48},{48,56},{56,64},{64,7... | collective-permute-start | bytes 196616 | tf_op jit(solution)/shard_map/ppermute | solution.py:430
  27.3 1.3 %collective-permute-start.5 = (f32[128,128]{1,0:T(8,128)S(1)}, f32[128,128]{1,0:T(8,128)S(1)}, u32[]{:S(2)}, u32[]{:S(2)}) collective-permute-start(f32[128,128]{1,0:T(8,128)S(1)} %get-tuple-element.23), channel_id=1, source_target_pairs={{8,0},{16,8},{24,16},{32,24},{40,32},{48,40},{56,48},{64,56},{72,6... | collective-permute-start | bytes 196616 | tf_op jit(solution)/shard_map/ppermute | solution.py:430
  28.6 0.1 add_convert_fusion.flags
  28.7 0.0 copy-done.3
  28.7 0.0 copy-done
  28.7 0.0 copy-done.2
  28.7 8.1 %inner.1 = (f32[8,16,32,128]{3,2,1,0:T(8,128)}, f32[8,192,128]{2,1,0:T(8,128)S(1)}, f32[8,192,128]{2,1,0:T(8,128)S(1)}, f32[5,288,128]{2,1,0:T(8,128)S(1)}, f32[3,512,128]{2,1,0:T(8,128)S(1)}) custom-call(f32[4]{0:T(128)S(1)} %add_convert_fusion.flags, f32[16]{0:T(128)S(1)} %copy-done.3, f32[8,16,32,128]{3,2,1,0:T(8,128)} %pot.5, ...), custom_call_target="tpu_custom_call" | custom-call | tf_op jit(solution)/shard_map/inner/pallas_call | solution.py:475
  36.8 0.0 collective-permute-done.4.clo
  36.8 0.0 collective-permute-done.5.chi
  36.9 0.0 collective-permute-done.wlo
  36.9 0.0 collective-permute-done.1.whi
  36.9 0.0 copy-start.5
  36.9 0.0 copy-start.1
  36.9 6.8 %outer.1 = (f32[8,16,32,128]{3,2,1,0:T(8,128)}, bf16[128,16,128]{2,1,0:T(8,128)(2,1)}) custom-call(f32[4]{0:T(128)S(1)} %add_convert_fusion.flags, f32[8,16,32,128]{3,2,1,0:T(8,128)} %pot.5, f32[35,32,128]{2,1,0:T(8,128)S(1)} %collective-permute-done.wlo, f32[35,32,128]{2,1,0:T(8,128)S(1)} %collective-permute-done.1.whi, ...), custom_call_target="tpu_custom_call", output_to_operand_aliasing={{0}: (13, {})} | custom-call | tf_op jit(solution)/shard_map/outer/pallas_call | solution.py:499
  43.7 12.0 %all-to-all-start = ((bf16[128,16,128]{2,1,0:T(8,128)(2,1)}), bf16[128,16,128]{2,1,0:T(8,128)(2,1)S(1)}, u32[]{:S(2)}, u32[]{:S(2)}) async-start(bf16[128,16,128]{2,1,0:T(8,128)(2,1)} %get-tuple-element.30), calls=%async_computation | async-start | bytes 1048576 | tf_op jit(solution)/shard_map/all_to_all | solution.py:516
  55.7 0.0 copy-done.5
  55.8 0.0 copy-done.1
  55.8 0.9 %flow.1.base = f32[3,256,128]{2,1,0:T(8,128)S(1)} custom-call(f32[3,256,128]{2,1,0:T(8,128)S(1)} %bitcast.9, f32[35,32,128]{2,1,0:T(8,128)S(1)} %collective-permute-done.wlo, f32[35,32,128]{2,1,0:T(8,128)S(1)} %collective-permute-done.1.whi, f32[35,16,128]{2,1,0:T(8,128)S(1)} %collective-permute-done.2.nlo, f32[35,16,128]{2,1,0:T(8,128)S(1)} %collective-permute-done.3.nhi), custom_call_target="tpu_custom_call" | custom-call | tf_op jit(solution)/shard_map/flow/pallas_call | solution.py:521
  56.6 12.8 %all-to-all-done.got = bf16[128,16,128]{2,1,0:T(8,128)(2,1)S(1)} async-done(((bf16[128,16,128]{2,1,0:T(8,128)(2,1)}), bf16[128,16,128]{2,1,0:T(8,128)(2,1)S(1)}, u32[]{:S(2)}, u32[]{:S(2)}) %all-to-all-start) | async-done | bytes 524320 | tf_op jit(solution)/shard_map/all_to_all | solution.py:516
  69.4 0.1 broadcast_in_dim.2.column
  69.5 1.3 %last.1 = (bf16[3,256,128]{2,1,0:T(8,128)(2,1)}, f32[3,256,128]{2,1,0:T(8,128)}) custom-call(s32[256,128]{1,0:T(8,128)S(1)} %broadcast_in_dim.2.column, bf16[128,16,128]{2,1,0:T(8,128)(2,1)S(1)} %all-to-all-done.got, f32[3,256,128]{2,1,0:T(8,128)S(1)} %flow.1.base), custom_call_target="tpu_custom_call" | custom-call | tf_op jit(solution)/shard_map/last/pallas_call | solution.py:528
  (2 shorter events, 0.0 us)
Async XLA Ops:
  0.6 28.1 %copy-start.3 = (f32[16]{0:T(128)S(1)}, f32[16]{0:T(128)}, u32[]{:S(2)}) copy-start(f32[16]{0:T(128)} %rk.3) | copy-start | bytes 196
  0.6 28.1 %copy-start = (f32[3,16,32,128]{3,2,1,0:T(8,128)S(1)}, f32[3,16,32,128]{3,2,1,0:T(8,128)}, u32[]{:S(2)}) copy-start(f32[3,16,32,128]{3,2,1,0:T(8,128)} %src.3) | copy-start | bytes 2359300
  0.7 28.1 %copy-start.2 = (s32[16,32,128]{2,1,0:T(8,128)S(1)}, s32[16,32,128]{2,1,0:T(8,128)}, u32[]{:S(2)}) copy-start(s32[16,32,128]{2,1,0:T(8,128)} %lab.3) | copy-start | bytes 786436
  0.7 15.8 %copy-start.4 = (s32[1,128,4]{1,2,0:T(4,128)S(1)}, s32[1,128,4]{1,2,0:T(4,128)}, u32[]{:S(2)}) copy-start(s32[1,128,4]{1,2,0:T(4,128)} %param.11) | copy-start | bytes 6148
  4.8 32.1 %collective-permute-start = (f32[35,32,128]{2,1,0:T(8,128)}, f32[35,32,128]{2,1,0:T(8,128)S(1)}, u32[]{:S(2)}, u32[]{:S(2)}) collective-permute-start(f32[35,32,128]{2,1,0:T(8,128)} %get-tuple-element.18), channel_id=1, source_target_pairs={{0,8},{8,16},{16,24},{24,32},{32,40},{40,48},{48,56},{56,64},{64,7... | collective-permute-start | bytes 1720328 | tf_op jit(solution)/shard_map/ppermute | solution.py:430
  8.8 28.0 %collective-permute-start.1 = (f32[35,32,128]{2,1,0:T(8,128)}, f32[35,32,128]{2,1,0:T(8,128)S(1)}, u32[]{:S(2)}, u32[]{:S(2)}) collective-permute-start(f32[35,32,128]{2,1,0:T(8,128)} %get-tuple-element.19), channel_id=1, source_target_pairs={{8,0},{16,8},{24,16},{32,24},{40,32},{48,40},{56,48},{64,56},{72,6... | collective-permute-start | bytes 1720328 | tf_op jit(solution)/shard_map/ppermute | solution.py:430
  10.1 8.3 %collective-permute-start.2 = (f32[35,16,128]{2,1,0:T(8,128)}, f32[35,16,128]{2,1,0:T(8,128)S(1)}, u32[]{:S(2)}, u32[]{:S(2)}) collective-permute-start(f32[35,16,128]{2,1,0:T(8,128)} %get-tuple-element.20), channel_id=1, source_target_pairs={{0,1},{1,2},{2,3},{3,4},{4,5},{5,6},{6,7},{8,9},{9,10},{10,11},{11... | collective-permute-start | bytes 860168 | tf_op jit(solution)/shard_map/ppermute | solution.py:430
  14.5 8.5 %collective-permute-start.3 = (f32[35,16,128]{2,1,0:T(8,128)}, f32[35,16,128]{2,1,0:T(8,128)S(1)}, u32[]{:S(2)}, u32[]{:S(2)}) collective-permute-start(f32[35,16,128]{2,1,0:T(8,128)} %get-tuple-element.21), channel_id=1, source_target_pairs={{1,0},{2,1},{3,2},{4,3},{5,4},{6,5},{7,6},{9,8},{10,9},{11,10},{12... | collective-permute-start | bytes 860168 | tf_op jit(solution)/shard_map/ppermute | solution.py:430
  23.1 13.8 %collective-permute-start.4 = (f32[128,128]{1,0:T(8,128)S(1)}, f32[128,128]{1,0:T(8,128)S(1)}, u32[]{:S(2)}, u32[]{:S(2)}) collective-permute-start(f32[128,128]{1,0:T(8,128)S(1)} %get-tuple-element.22), channel_id=1, source_target_pairs={{0,8},{8,16},{16,24},{24,32},{32,40},{40,48},{48,56},{56,64},{64,7... | collective-permute-start | bytes 196616 | tf_op jit(solution)/shard_map/ppermute | solution.py:430
  27.3 9.5 %collective-permute-start.5 = (f32[128,128]{1,0:T(8,128)S(1)}, f32[128,128]{1,0:T(8,128)S(1)}, u32[]{:S(2)}, u32[]{:S(2)}) collective-permute-start(f32[128,128]{1,0:T(8,128)S(1)} %get-tuple-element.23), channel_id=1, source_target_pairs={{8,0},{16,8},{24,16},{32,24},{40,32},{48,40},{56,48},{64,56},{72,6... | collective-permute-start | bytes 196616 | tf_op jit(solution)/shard_map/ppermute | solution.py:430
  36.9 18.9 %copy-start.5 = (s32[1,256]{1,0:T(1,128)S(1)}, s32[1,256]{1,0:T(1,128)}, u32[]{:S(2)}) copy-start(s32[1,256]{1,0:T(1,128)} %param.12) | copy-start | bytes 3076
  36.9 18.9 %copy-start.1 = (f32[3,8,32,128]{3,2,1,0:T(8,128)S(1)}, f32[3,8,32,128]{3,2,1,0:T(8,128)}, u32[]{:S(2)}) copy-start(f32[3,8,32,128]{3,2,1,0:T(8,128)} %vel.1) | copy-start | bytes 1179652
  43.7 25.7 %all-to-all-start = ((bf16[128,16,128]{2,1,0:T(8,128)(2,1)}), bf16[128,16,128]{2,1,0:T(8,128)(2,1)S(1)}, u32[]{:S(2)}, u32[]{:S(2)}) async-start(bf16[128,16,128]{2,1,0:T(8,128)(2,1)} %get-tuple-element.30), calls=%async_computation | async-start | bytes 1048576 | tf_op jit(solution)/shard_map/all_to_all | solution.py:516

commit v3 on v2

--- a/solution.py
+++ b/solution.py
@@ -233,8 +233,8 @@
         deep = DEEP if c < 8 else FLAT
         ref, part = (s0, c) if c < 8 else (field, c - 8)
         for d in range(deep):
-            ref[part, strip(at(0) - 1 - d, span_x, ROWS), :] = nlo[place(c, d)]
-            ref[part, strip(at(0) + span_y + d, span_x, ROWS), :] = nhi[place(c, d)]
+            ref[part, strip(at(0) - 1 - d, span_x, ROWS), :] = nlo[place(c, d)] * flags[2]
+            ref[part, strip(at(0) + span_y + d, span_x, ROWS), :] = nhi[place(c, d)] * flags[3]
     for one in early:
         one.wait()
 
@@ -298,8 +298,8 @@
         for d in range(DEEP):
             p = place(c, d)
             for x in (0, 1, span_x - 2, span_x - 1):
-                s0[c, pl.ds(at(x) - 1 - d, 1), :] = nlo[p, pl.ds(x, 1), :]
-                s0[c, pl.ds(at(x) + span_y + d, 1), :] = nhi[p, pl.ds(x, 1), :]
+                s0[c, pl.ds(at(x) - 1 - d, 1), :] = nlo[p, pl.ds(x, 1), :] * flags[2]
+                s0[c, pl.ds(at(x) + span_y + d, 1), :] = nhi[p, pl.ds(x, 1), :] * flags[3]
     for one in early:
         one.wait()
     for c in range(5):
@@ -312,8 +312,9 @@
             for e in range(deep - 1 - d):
                 p = place(c, d)
                 for source, x in ((clo, -1 - e), (chi, span_x + e)):
-                    ref[part, pl.ds(at(x) - 1 - d, 1), :] = source[pl.ds(e * 2 * planes + p, 1), :]
-                    ref[part, pl.ds(at(x) + span_y + d, 1), :] = source[pl.ds((e * 2 + 1) * planes + p, 1), :]
+                    low, high = (source[pl.ds((e * 2 + side) * planes + p, 1), :] for side in range(2))
+                    ref[part, pl.ds(at(x) - 1 - d, 1), :] = low * flags[2]
+                    ref[part, pl.ds(at(x) + span_y + d, 1), :] = high * flags[3]
 
     def both(low, high, do):
         over(-high, -low, do)
@@ -322,6 +323,14 @@
     both(0, 2, lambda x: scale_plane(span_x, span_y, flags, field, x))
     for one in late:
         one.wait()
+    for i, first in enumerate((-DEEP, span_x)):
+
+        @pl.when(flags[i] == 0.0)
+        def _():
+            for c in range(8):
+                for x in range(first, first + DEEP):
+                    s0[c, pl.ds(at(x) - DEEP, span_y + 2 * DEEP), :] = jnp.zeros((span_y + 2 * DEEP, depth), F32)
+
     both(-1, 2, lambda x: sweep_plane(s0, s1, field, x, 2))
     both(-2, 1, lambda x: sweep_plane(s1, s2, field, x, 1))
     done = [
@@ -349,15 +358,15 @@
         one.wait()
 
 
-def flow_kernel(les_x, span_y, vel, wlo, whi, nlo, nhi, base, s0):
+def flow_kernel(les_x, span_y, flags, vel, wlo, whi, nlo, nhi, base, s0):
     first = 8 * DEEP + 4 * FLAT
     for c in range(3):
         for x in range(les_x):
             s0[c, pl.ds((x + 1) * ROWS + OFF, span_y), :] = vel[c, pl.ds(x * span_y, span_y), :]
-        s0[c, pl.ds(OFF, span_y), :] = wlo[first + c]
-        s0[c, pl.ds((les_x + 1) * ROWS + OFF, span_y), :] = whi[first + c]
-        s0[c, strip(ROWS + OFF - 1, les_x, ROWS), :] = nlo[first + c, pl.ds(0, les_x), :]
-        s0[c, strip(ROWS + OFF + span_y, les_x, ROWS), :] = nhi[first + c, pl.ds(0, les_x), :]
+        s0[c, pl.ds(OFF, span_y), :] = wlo[first + c] * flags[0]
+        s0[c, pl.ds((les_x + 1) * ROWS + OFF, span_y), :] = whi[first + c] * flags[1]
+        s0[c, strip(ROWS + OFF - 1, les_x, ROWS), :] = nlo[first + c, pl.ds(0, les_x), :] * flags[2]
+        s0[c, strip(ROWS + OFF + span_y, les_x, ROWS), :] = nhi[first + c, pl.ds(0, les_x), :] * flags[3]
 
     def step(x, carry):
         for t in range(span_y // 8):
@@ -425,7 +434,7 @@
 
 def swap(low, high, axis):
     count = lax.axis_size(axis)
-    forward = [(i, i + 1) for i in range(count - 1)]
+    forward = [(i, (i + 1) % count) for i in range(count)]
     backward = [(target, source) for source, target in forward]
     return lax.ppermute(high, axis, forward), lax.ppermute(low, axis, backward)
 
@@ -523,8 +532,8 @@
         [((3, lines, depth), F32)],
         "flow",
         scratch=[((3, (les_x + 2) * ROWS + OFF, depth), F32)],
-        count=5,
-    )(vel, wlo, whi, nlo, nhi)
+        smem=1, count=6,
+    )(flags, vel, wlo, whi, nlo, nhi)
     les, velocity_next = call(
         functools.partial(last_kernel, slots),
         [((3, lines, depth), BF16), ((3, lines, depth), F32)],

time: 71.2 us -> 59.7 us (0.84)
  starting transfers between devices: 29.2 us -> 17.9 us
    ppermute x3, starting transfers between devices: 12.7 us -> 4.8 us  [swap(): lax.ppermute(high, axis, forward)]
    all_to_all x1, starting transfers between devices: 12 us -> 4.57 us  [body(): lax.all_to_all(outgoing, ('wide', 'narrow'), split_axis=0, concat_axis=0,...]
    ppermute x3, starting transfers between devices: 4.5 us -> 8.49 us  [swap(): lax.ppermute(low, axis, backward)]
    ppermute x3, waiting for transfers between devices: 0.5 us -> 2.46 us  [swap(): lax.ppermute(high, axis, forward)]
    ppermute x3, waiting for transfers between devices: 4.59 us -> 2.67 us  [swap(): lax.ppermute(low, axis, backward)]
  transfers between devices with their start and end apart: 7 -> 7, of which waited for: 3 -> 3; matrix products, arithmetic and copies ran while one was open for 2% -> 3% of each run, Pallas kernels for 13% -> 16%
where the time goes in v3:
time: 59.7 us; the launch traced here: 59.4 us
  Pallas kernels  21.8 us (37%)
  starting transfers between devices  17.9 us (30%)
  waiting for transfers between devices  17.4 us (29%)
  other arithmetic  1.32 us (2%)
  between operations  0.82 us (1%)
    all_to_all x1, waiting for transfers between devices, body(): lax.all_to_all(outgoing, ('wide', 'narrow'), split_axis=0, concat_axis=0,...  12.2 us
    ppermute x3, starting transfers between devices, swap(): lax.ppermute(low, axis, backward)  8.49 us
    pallas_call x1, Pallas kernels, body(): call(functools.partial(inner_kernel, span_x, span_y, regions), [(potentia...  8.09 us
    pallas_call x1, Pallas kernels, body(): call(functools.partial(outer_kernel, span_x, span_y, slots), [(potential....  6.85 us
    ppermute x3, starting transfers between devices, swap(): lax.ppermute(high, axis, forward)  4.8 us
    all_to_all x1, starting transfers between devices, body(): lax.all_to_all(outgoing, ('wide', 'narrow'), split_axis=0, concat_axis=0,...  4.57 us
    pallas_call x1, Pallas kernels, body(): call(functools.partial(faces_kernel, span_x, span_y, regions), [wide, wid...  4.08 us
    ppermute x3, waiting for transfers between devices, swap(): lax.ppermute(low, axis, backward)  2.67 us
  transfers between devices with their start and end apart: 7, of which 3 were waited for; matrix products, arithmetic and copies ran while one was open for 3% of the time, Pallas kernels for 16%

profile of v3, /device:TPU:1, one launch (start us, length us, event | category | flops | bytes accessed | tf_op | source)
XLA Modules:
  0.0 59.4 jit_solution(2282397255802474017)
XLA Ops:
  0.6 0.0 copy-start.3
  0.6 0.0 copy-start
  0.7 0.0 copy-start.2
  0.7 0.0 copy-start.4
  0.7 4.1 %faces.1 = (f32[35,32,128]{2,1,0:T(8,128)}, f32[35,32,128]{2,1,0:T(8,128)}, f32[35,16,128]{2,1,0:T(8,128)}, f32[35,16,128]{2,1,0:T(8,128)}) custom-call(f32[16]{0:T(128)} %rk.3, f32[8,16,32,128]{3,2,1,0:T(8,128)} %pot.5, f32[3,16,32,128]{3,2,1,0:T(8,128)} %src.3, s32[16,32,128]{2,1,0:T(8,128)} %lab.3, f32[3,8,32,128]{3,2,1,0:T(8,128)} %vel.1), custom_call_target="tpu_custom_call" | custom-call | tf_op jit(solution)/shard_map/faces/pallas_call | solution.py:454
  4.8 2.2 %collective-permute-start = (f32[35,32,128]{2,1,0:T(8,128)}, f32[35,32,128]{2,1,0:T(8,128)S(1)}, u32[]{:S(2)}, u32[]{:S(2)}) collective-permute-start(f32[35,32,128]{2,1,0:T(8,128)} %get-tuple-element.18), channel_id=1, source_target_pairs={{0,8},{8,16},{16,24},{24,32},{32,40},{40,48},{48,56},{56,64},{64,7... | collective-permute-start | bytes 1720328 | tf_op jit(solution)/shard_map/ppermute | solution.py:439
  7.0 3.7 %collective-permute-start.1 = (f32[35,32,128]{2,1,0:T(8,128)}, f32[35,32,128]{2,1,0:T(8,128)S(1)}, u32[]{:S(2)}, u32[]{:S(2)}) collective-permute-start(f32[35,32,128]{2,1,0:T(8,128)} %get-tuple-element.19), channel_id=1, source_target_pairs={{8,0},{16,8},{24,16},{32,24},{40,32},{48,40},{56,48},{64,56},{72,6... | collective-permute-start | bytes 1720328 | tf_op jit(solution)/shard_map/ppermute | solution.py:439
  10.7 2.5 %collective-permute-start.2 = (f32[35,16,128]{2,1,0:T(8,128)}, f32[35,16,128]{2,1,0:T(8,128)S(1)}, u32[]{:S(2)}, u32[]{:S(2)}) collective-permute-start(f32[35,16,128]{2,1,0:T(8,128)} %get-tuple-element.20), channel_id=1, source_target_pairs={{0,1},{1,2},{2,3},{3,4},{4,5},{5,6},{6,7},{7,0},{8,9},{9,10},{10,1... | collective-permute-start | bytes 860168 | tf_op jit(solution)/shard_map/ppermute | solution.py:439
  13.2 0.0 collective-permute-start.3
  13.2 0.0 copy-done.4
  13.2 0.1 copy.11
  13.3 0.1 eq.17
  13.4 1.2 %fusion.hot = bf16[1024,512]{1,0:T(8,128)(2,1)} fusion(s32[1024]{0:T(1024)S(1)} %eq.17), kind=kLoop, calls=%fused_computation.1 | loop fusion | flops 1048576 | bytes 1052672 | tf_op jit(solution)/shard_map/convert_element_type | solution.py:507
  14.7 2.5 %collective-permute-done.2.nlo = f32[35,16,128]{2,1,0:T(8,128)S(1)} collective-permute-done((f32[35,16,128]{2,1,0:T(8,128)}, f32[35,16,128]{2,1,0:T(8,128)S(1)}, u32[]{:S(2)}, u32[]{:S(2)}) %collective-permute-start.2) | collective-permute-done | bytes 286752 | tf_op jit(solution)/shard_map/ppermute | solution.py:439
  17.1 2.7 %collective-permute-done.3.nhi = f32[35,16,128]{2,1,0:T(8,128)S(1)} collective-permute-done((f32[35,16,128]{2,1,0:T(8,128)}, f32[35,16,128]{2,1,0:T(8,128)S(1)}, u32[]{:S(2)}, u32[]{:S(2)}) %collective-permute-start.3) | collective-permute-done | bytes 286752 | tf_op jit(solution)/shard_map/ppermute | solution.py:439
  19.8 0.1 corner.1
  19.8 0.1 collective-permute-start.4
  19.9 4.8 %collective-permute-start.5 = (f32[128,128]{1,0:T(8,128)S(1)}, f32[128,128]{1,0:T(8,128)S(1)}, u32[]{:S(2)}, u32[]{:S(2)}) collective-permute-start(f32[128,128]{1,0:T(8,128)S(1)} %get-tuple-element.23), channel_id=1, source_target_pairs={{8,0},{16,8},{24,16},{32,24},{40,32},{48,40},{56,48},{64,56},{72,6... | collective-permute-start | bytes 196616 | tf_op jit(solution)/shard_map/ppermute | solution.py:439
  24.7 0.1 add_convert_fusion.flags
  24.8 0.0 copy-done.3
  24.8 0.0 copy-done
  24.8 0.0 copy-done.2
  24.8 8.1 %inner.1 = (f32[8,16,32,128]{3,2,1,0:T(8,128)}, f32[8,192,128]{2,1,0:T(8,128)S(1)}, f32[8,192,128]{2,1,0:T(8,128)S(1)}, f32[5,288,128]{2,1,0:T(8,128)S(1)}, f32[3,512,128]{2,1,0:T(8,128)S(1)}) custom-call(f32[4]{0:T(128)S(1)} %add_convert_fusion.flags, f32[16]{0:T(128)S(1)} %copy-done.3, f32[8,16,32,128]{3,2,1,0:T(8,128)} %pot.5, ...), custom_call_target="tpu_custom_call" | custom-call | tf_op jit(solution)/shard_map/inner/pallas_call | solution.py:484
  32.9 0.0 collective-permute-done.4.clo
  32.9 0.0 collective-permute-done.5.chi
  32.9 0.0 collective-permute-done.wlo
  32.9 0.0 collective-permute-done.1.whi
  32.9 0.0 copy-start.5
  32.9 0.0 copy-start.1
  33.0 6.9 %outer.1 = (f32[8,16,32,128]{3,2,1,0:T(8,128)}, bf16[128,16,128]{2,1,0:T(8,128)(2,1)}) custom-call(f32[4]{0:T(128)S(1)} %add_convert_fusion.flags, f32[8,16,32,128]{3,2,1,0:T(8,128)} %pot.5, f32[35,32,128]{2,1,0:T(8,128)S(1)} %collective-permute-done.wlo, f32[35,32,128]{2,1,0:T(8,128)S(1)} %collective-permute-done.1.whi, ...), custom_call_target="tpu_custom_call", output_to_operand_aliasing={{0}: (13, {})} | custom-call | tf_op jit(solution)/shard_map/outer/pallas_call | solution.py:508
  39.8 4.6 %all-to-all-start = ((bf16[128,16,128]{2,1,0:T(8,128)(2,1)}), bf16[128,16,128]{2,1,0:T(8,128)(2,1)S(1)}, u32[]{:S(2)}, u32[]{:S(2)}) async-start(bf16[128,16,128]{2,1,0:T(8,128)(2,1)} %get-tuple-element.30), calls=%async_computation | async-start | bytes 1048576 | tf_op jit(solution)/shard_map/all_to_all | solution.py:525
  44.4 0.0 copy-done.5
  44.4 0.0 copy-done.1
  44.4 1.4 %flow.1.base = f32[3,256,128]{2,1,0:T(8,128)S(1)} custom-call(f32[4]{0:T(128)S(1)} %add_convert_fusion.flags, f32[3,256,128]{2,1,0:T(8,128)S(1)} %bitcast.9, f32[35,32,128]{2,1,0:T(8,128)S(1)} %collective-permute-done.wlo, f32[35,32,128]{2,1,0:T(8,128)S(1)} %collective-permute-done.1.whi, f32[35,16,128]{2,1,0:T(8,128)S(1)} %collective-permute-done.2.nlo, ...), custom_call_target="tpu_custom_call" | custom-call | tf_op jit(solution)/shard_map/flow/pallas_call | solution.py:530
  45.8 12.2 %all-to-all-done.got = bf16[128,16,128]{2,1,0:T(8,128)(2,1)S(1)} async-done(((bf16[128,16,128]{2,1,0:T(8,128)(2,1)}), bf16[128,16,128]{2,1,0:T(8,128)(2,1)S(1)}, u32[]{:S(2)}, u32[]{:S(2)}) %all-to-all-start) | async-done | bytes 524320 | tf_op jit(solution)/shard_map/all_to_all | solution.py:525
  58.1 0.1 broadcast_in_dim.2.column
  58.2 1.3 %last.1 = (bf16[3,256,128]{2,1,0:T(8,128)(2,1)}, f32[3,256,128]{2,1,0:T(8,128)}) custom-call(s32[256,128]{1,0:T(8,128)S(1)} %broadcast_in_dim.2.column, bf16[128,16,128]{2,1,0:T(8,128)(2,1)S(1)} %all-to-all-done.got, f32[3,256,128]{2,1,0:T(8,128)S(1)} %flow.1.base), custom_call_target="tpu_custom_call" | custom-call | tf_op jit(solution)/shard_map/last/pallas_call | solution.py:537
  (2 shorter events, 0.0 us)
Async XLA Ops:
  0.6 24.2 %copy-start.3 = (f32[16]{0:T(128)S(1)}, f32[16]{0:T(128)}, u32[]{:S(2)}) copy-start(f32[16]{0:T(128)} %rk.3) | copy-start | bytes 196
  0.6 24.1 %copy-start = (f32[3,16,32,128]{3,2,1,0:T(8,128)S(1)}, f32[3,16,32,128]{3,2,1,0:T(8,128)}, u32[]{:S(2)}) copy-start(f32[3,16,32,128]{3,2,1,0:T(8,128)} %src.3) | copy-start | bytes 2359300
  0.7 24.1 %copy-start.2 = (s32[16,32,128]{2,1,0:T(8,128)S(1)}, s32[16,32,128]{2,1,0:T(8,128)}, u32[]{:S(2)}) copy-start(s32[16,32,128]{2,1,0:T(8,128)} %lab.3) | copy-start | bytes 786436
  0.7 12.5 %copy-start.4 = (s32[1,128,4]{1,2,0:T(4,128)S(1)}, s32[1,128,4]{1,2,0:T(4,128)}, u32[]{:S(2)}) copy-start(s32[1,128,4]{1,2,0:T(4,128)} %param.11) | copy-start | bytes 6148
  4.8 28.2 %collective-permute-start = (f32[35,32,128]{2,1,0:T(8,128)}, f32[35,32,128]{2,1,0:T(8,128)S(1)}, u32[]{:S(2)}, u32[]{:S(2)}) collective-permute-start(f32[35,32,128]{2,1,0:T(8,128)} %get-tuple-element.18), channel_id=1, source_target_pairs={{0,8},{8,16},{16,24},{24,32},{32,40},{40,48},{48,56},{56,64},{64,7... | collective-permute-start | bytes 1720328 | tf_op jit(solution)/shard_map/ppermute | solution.py:439
  7.0 26.0 %collective-permute-start.1 = (f32[35,32,128]{2,1,0:T(8,128)}, f32[35,32,128]{2,1,0:T(8,128)S(1)}, u32[]{:S(2)}, u32[]{:S(2)}) collective-permute-start(f32[35,32,128]{2,1,0:T(8,128)} %get-tuple-element.19), channel_id=1, source_target_pairs={{8,0},{16,8},{24,16},{32,24},{40,32},{48,40},{56,48},{64,56},{72,6... | collective-permute-start | bytes 1720328 | tf_op jit(solution)/shard_map/ppermute | solution.py:439
  10.7 6.4 %collective-permute-start.2 = (f32[35,16,128]{2,1,0:T(8,128)}, f32[35,16,128]{2,1,0:T(8,128)S(1)}, u32[]{:S(2)}, u32[]{:S(2)}) collective-permute-start(f32[35,16,128]{2,1,0:T(8,128)} %get-tuple-element.20), channel_id=1, source_target_pairs={{0,1},{1,2},{2,3},{3,4},{4,5},{5,6},{6,7},{7,0},{8,9},{9,10},{10,1... | collective-permute-start | bytes 860168 | tf_op jit(solution)/shard_map/ppermute | solution.py:439
  13.2 6.6 %collective-permute-start.3 = (f32[35,16,128]{2,1,0:T(8,128)}, f32[35,16,128]{2,1,0:T(8,128)S(1)}, u32[]{:S(2)}, u32[]{:S(2)}) collective-permute-start(f32[35,16,128]{2,1,0:T(8,128)} %get-tuple-element.21), channel_id=1, source_target_pairs={{1,0},{2,1},{3,2},{4,3},{5,4},{6,5},{7,6},{0,7},{9,8},{10,9},{11,1... | collective-permute-start | bytes 860168 | tf_op jit(solution)/shard_map/ppermute | solution.py:439
  19.8 13.0 %collective-permute-start.4 = (f32[128,128]{1,0:T(8,128)S(1)}, f32[128,128]{1,0:T(8,128)S(1)}, u32[]{:S(2)}, u32[]{:S(2)}) collective-permute-start(f32[128,128]{1,0:T(8,128)S(1)} %get-tuple-element.22), channel_id=1, source_target_pairs={{0,8},{8,16},{16,24},{24,32},{32,40},{40,48},{48,56},{56,64},{64,7... | collective-permute-start | bytes 196616 | tf_op jit(solution)/shard_map/ppermute | solution.py:439
  19.9 13.0 %collective-permute-start.5 = (f32[128,128]{1,0:T(8,128)S(1)}, f32[128,128]{1,0:T(8,128)S(1)}, u32[]{:S(2)}, u32[]{:S(2)}) collective-permute-start(f32[128,128]{1,0:T(8,128)S(1)} %get-tuple-element.23), channel_id=1, source_target_pairs={{8,0},{16,8},{24,16},{32,24},{40,32},{48,40},{56,48},{64,56},{72,6... | collective-permute-start | bytes 196616 | tf_op jit(solution)/shard_map/ppermute | solution.py:439
  32.9 11.5 %copy-start.5 = (s32[1,256]{1,0:T(1,128)S(1)}, s32[1,256]{1,0:T(1,128)}, u32[]{:S(2)}) copy-start(s32[1,256]{1,0:T(1,128)} %param.12) | copy-start | bytes 3076
  32.9 11.5 %copy-start.1 = (f32[3,8,32,128]{3,2,1,0:T(8,128)S(1)}, f32[3,8,32,128]{3,2,1,0:T(8,128)}, u32[]{:S(2)}) copy-start(f32[3,8,32,128]{3,2,1,0:T(8,128)} %vel.1) | copy-start | bytes 1179652
  39.8 18.3 %all-to-all-start = ((bf16[128,16,128]{2,1,0:T(8,128)(2,1)}), bf16[128,16,128]{2,1,0:T(8,128)(2,1)S(1)}, u32[]{:S(2)}, u32[]{:S(2)}) async-start(bf16[128,16,128]{2,1,0:T(8,128)(2,1)} %get-tuple-element.30), calls=%async_computation | async-start | bytes 1048576 | tf_op jit(solution)/shard_map/all_to_all | solution.py:525

commit v4 on v3

--- a/solution.py
+++ b/solution.py
@@ -120,12 +120,12 @@
         sweep_tile(old, new, field, at(x) - margin + 8 * t)
 
 
-def over(low, high, do):
+def over(low, high, do, unroll=1):
     def step(i, carry):
         do(i + low)
         return carry
 
-    lax.fori_loop(0, high - low, step, 0)
+    lax.fori_loop(0, high - low, step, 0, unroll=unroll)
 
 
 def lanes(value):
@@ -249,12 +249,12 @@
     over(0, span_x, lambda x: scale_plane(span_x, span_y, flags, field, x))
     for one in late:
         one.wait()
-    over(1, span_x - 1, lambda x: sweep_plane(s0, s1, field, x, 2))
-    over(2, span_x - 2, lambda x: sweep_plane(s1, s2, field, x, 1))
+    over(1, span_x - 1, lambda x: sweep_plane(s0, s1, field, x, 2), 7)
+    over(2, span_x - 2, lambda x: sweep_plane(s1, s2, field, x, 1), 7)
     done = [
         copies.start(s2.at[:, pl.ds(at(x), span_y), :], nxt.at[:, x]) for x in range(2, span_x - 2)
     ]
-    over(3, span_x - 3, lambda x: force_plane(s2, field, force, span_y, x))
+    over(3, span_x - 3, lambda x: force_plane(s2, field, force, span_y, x), 5)
     for c in range(8):
         for i, x in enumerate((1, 2, span_x - 3, span_x - 2)):
             halves[c, kept(i), :] = s1[c, stored(x), :]
@@ -317,8 +317,8 @@
                     ref[part, pl.ds(at(x) + span_y + d, 1), :] = high * flags[3]
 
     def both(low, high, do):
-        over(-high, -low, do)
-        over(span_x + low, span_x + high, do)
+        over(-high, -low, do, 3)
+        over(span_x + low, span_x + high, do, 3)
 
     both(0, 2, lambda x: scale_plane(span_x, span_y, flags, field, x))
     for one in late:

time: 59.7 us -> 56.7 us (0.950)
  Pallas kernels: 21.8 us -> 18.7 us
    pallas_call x1, Pallas kernels: 8.09 us -> 6.43 us  [body(): call(functools.partial(inner_kernel, span_x, span_y, regions), [(potentia...]
    pallas_call x1, Pallas kernels: 6.85 us -> 5.48 us  [body(): call(functools.partial(outer_kernel, span_x, span_y, slots), [(potential....]
  transfers between devices with their start and end apart: 7 -> 7, of which waited for: 3 -> 3; matrix products, arithmetic and copies ran while one was open for 3% -> 3% of each run, Pallas kernels for 16% -> 14%
where the time goes in v4:
time: 56.7 us; the launch traced here: 56.4 us
  Pallas kernels  18.7 us (33%)
  starting transfers between devices  17.9 us (32%)
  waiting for transfers between devices  17.4 us (31%)
  other arithmetic  1.32 us (2%)
  between operations  0.82 us (1%)
    all_to_all x1, waiting for transfers between devices, body(): lax.all_to_all(outgoing, ('wide', 'narrow'), split_axis=0, concat_axis=0,...  12.2 us
    ppermute x3, starting transfers between devices, swap(): lax.ppermute(low, axis, backward)  8.49 us
    pallas_call x1, Pallas kernels, body(): call(functools.partial(inner_kernel, span_x, span_y, regions), [(potentia...  6.43 us
    pallas_call x1, Pallas kernels, body(): call(functools.partial(outer_kernel, span_x, span_y, slots), [(potential....  5.48 us
    ppermute x3, starting transfers between devices, swap(): lax.ppermute(high, axis, forward)  4.8 us
    all_to_all x1, starting transfers between devices, body(): lax.all_to_all(outgoing, ('wide', 'narrow'), split_axis=0, concat_axis=0,...  4.57 us
    pallas_call x1, Pallas kernels, body(): call(functools.partial(faces_kernel, span_x, span_y, regions), [wide, wid...  4.08 us
    ppermute x3, waiting for transfers between devices, swap(): lax.ppermute(low, axis, backward)  2.67 us
  transfers between devices with their start and end apart: 7, of which 3 were waited for; matrix products, arithmetic and copies ran while one was open for 3% of the time, Pallas kernels for 14%

profile of v4, /device:TPU:1, one launch (start us, length us, event | category | flops | bytes accessed | tf_op | source)
XLA Modules:
  0.0 56.4 jit_solution(8493443928377392721)
XLA Ops:
  0.6 0.0 copy-start.3
  0.6 0.0 copy-start
  0.7 0.0 copy-start.2
  0.7 0.0 copy-start.4
  0.7 4.1 %faces.1 = (f32[35,32,128]{2,1,0:T(8,128)}, f32[35,32,128]{2,1,0:T(8,128)}, f32[35,16,128]{2,1,0:T(8,128)}, f32[35,16,128]{2,1,0:T(8,128)}) custom-call(f32[16]{0:T(128)} %rk.3, f32[8,16,32,128]{3,2,1,0:T(8,128)} %pot.5, f32[3,16,32,128]{3,2,1,0:T(8,128)} %src.3, s32[16,32,128]{2,1,0:T(8,128)} %lab.3, f32[3,8,32,128]{3,2,1,0:T(8,128)} %vel.1), custom_call_target="tpu_custom_call" | custom-call | tf_op jit(solution)/shard_map/faces/pallas_call | solution.py:454
  4.8 2.2 %collective-permute-start = (f32[35,32,128]{2,1,0:T(8,128)}, f32[35,32,128]{2,1,0:T(8,128)S(1)}, u32[]{:S(2)}, u32[]{:S(2)}) collective-permute-start(f32[35,32,128]{2,1,0:T(8,128)} %get-tuple-element.18), channel_id=1, source_target_pairs={{0,8},{8,16},{16,24},{24,32},{32,40},{40,48},{48,56},{56,64},{64,7... | collective-permute-start | bytes 1720328 | tf_op jit(solution)/shard_map/ppermute | solution.py:439
  7.0 3.7 %collective-permute-start.1 = (f32[35,32,128]{2,1,0:T(8,128)}, f32[35,32,128]{2,1,0:T(8,128)S(1)}, u32[]{:S(2)}, u32[]{:S(2)}) collective-permute-start(f32[35,32,128]{2,1,0:T(8,128)} %get-tuple-element.19), channel_id=1, source_target_pairs={{8,0},{16,8},{24,16},{32,24},{40,32},{48,40},{56,48},{64,56},{72,6... | collective-permute-start | bytes 1720328 | tf_op jit(solution)/shard_map/ppermute | solution.py:439
  10.7 2.5 %collective-permute-start.2 = (f32[35,16,128]{2,1,0:T(8,128)}, f32[35,16,128]{2,1,0:T(8,128)S(1)}, u32[]{:S(2)}, u32[]{:S(2)}) collective-permute-start(f32[35,16,128]{2,1,0:T(8,128)} %get-tuple-element.20), channel_id=1, source_target_pairs={{0,1},{1,2},{2,3},{3,4},{4,5},{5,6},{6,7},{7,0},{8,9},{9,10},{10,1... | collective-permute-start | bytes 860168 | tf_op jit(solution)/shard_map/ppermute | solution.py:439
  13.2 0.0 collective-permute-start.3
  13.2 0.0 copy-done.4
  13.2 0.1 copy.11
  13.3 0.1 eq.17
  13.4 1.2 %fusion.hot = bf16[1024,512]{1,0:T(8,128)(2,1)} fusion(s32[1024]{0:T(1024)S(1)} %eq.17), kind=kLoop, calls=%fused_computation.1 | loop fusion | flops 1048576 | bytes 1052672 | tf_op jit(solution)/shard_map/convert_element_type | solution.py:507
  14.7 2.5 %collective-permute-done.2.nlo = f32[35,16,128]{2,1,0:T(8,128)S(1)} collective-permute-done((f32[35,16,128]{2,1,0:T(8,128)}, f32[35,16,128]{2,1,0:T(8,128)S(1)}, u32[]{:S(2)}, u32[]{:S(2)}) %collective-permute-start.2) | collective-permute-done | bytes 286752 | tf_op jit(solution)/shard_map/ppermute | solution.py:439
  17.1 2.7 %collective-permute-done.3.nhi = f32[35,16,128]{2,1,0:T(8,128)S(1)} collective-permute-done((f32[35,16,128]{2,1,0:T(8,128)}, f32[35,16,128]{2,1,0:T(8,128)S(1)}, u32[]{:S(2)}, u32[]{:S(2)}) %collective-permute-start.3) | collective-permute-done | bytes 286752 | tf_op jit(solution)/shard_map/ppermute | solution.py:439
  19.8 0.1 corner.1
  19.8 0.1 collective-permute-start.4
  19.9 4.8 %collective-permute-start.5 = (f32[128,128]{1,0:T(8,128)S(1)}, f32[128,128]{1,0:T(8,128)S(1)}, u32[]{:S(2)}, u32[]{:S(2)}) collective-permute-start(f32[128,128]{1,0:T(8,128)S(1)} %get-tuple-element.23), channel_id=1, source_target_pairs={{8,0},{16,8},{24,16},{32,24},{40,32},{48,40},{56,48},{64,56},{72,6... | collective-permute-start | bytes 196616 | tf_op jit(solution)/shard_map/ppermute | solution.py:439
  24.7 0.1 add_convert_fusion.flags
  24.8 0.0 copy-done.3
  24.8 0.0 copy-done
  24.8 0.0 copy-done.2
  24.8 6.4 %inner.1 = (f32[8,16,32,128]{3,2,1,0:T(8,128)}, f32[8,192,128]{2,1,0:T(8,128)S(1)}, f32[8,192,128]{2,1,0:T(8,128)S(1)}, f32[5,288,128]{2,1,0:T(8,128)S(1)}, f32[3,512,128]{2,1,0:T(8,128)S(1)}) custom-call(f32[4]{0:T(128)S(1)} %add_convert_fusion.flags, f32[16]{0:T(128)S(1)} %copy-done.3, f32[8,16,32,128]{3,2,1,0:T(8,128)} %pot.5, ...), custom_call_target="tpu_custom_call" | custom-call | tf_op jit(solution)/shard_map/inner/pallas_call | solution.py:484
  31.2 0.0 collective-permute-done.4.clo
  31.2 0.0 collective-permute-done.5.chi
  31.2 0.0 collective-permute-done.wlo
  31.3 0.0 collective-permute-done.1.whi
  31.3 0.0 copy-start.5
  31.3 0.0 copy-start.1
  31.3 5.5 %outer.1 = (f32[8,16,32,128]{3,2,1,0:T(8,128)}, bf16[128,16,128]{2,1,0:T(8,128)(2,1)}) custom-call(f32[4]{0:T(128)S(1)} %add_convert_fusion.flags, f32[8,16,32,128]{3,2,1,0:T(8,128)} %pot.5, f32[35,32,128]{2,1,0:T(8,128)S(1)} %collective-permute-done.wlo, f32[35,32,128]{2,1,0:T(8,128)S(1)} %collective-permute-done.1.whi, ...), custom_call_target="tpu_custom_call", output_to_operand_aliasing={{0}: (13, {})} | custom-call | tf_op jit(solution)/shard_map/outer/pallas_call | solution.py:508
  36.8 4.6 %all-to-all-start = ((bf16[128,16,128]{2,1,0:T(8,128)(2,1)}), bf16[128,16,128]{2,1,0:T(8,128)(2,1)S(1)}, u32[]{:S(2)}, u32[]{:S(2)}) async-start(bf16[128,16,128]{2,1,0:T(8,128)(2,1)} %get-tuple-element.30), calls=%async_computation | async-start | bytes 1048576 | tf_op jit(solution)/shard_map/all_to_all | solution.py:525
  41.4 0.0 copy-done.5
  41.4 0.0 copy-done.1
  41.4 1.4 %flow.1.base = f32[3,256,128]{2,1,0:T(8,128)S(1)} custom-call(f32[4]{0:T(128)S(1)} %add_convert_fusion.flags, f32[3,256,128]{2,1,0:T(8,128)S(1)} %bitcast.9, f32[35,32,128]{2,1,0:T(8,128)S(1)} %collective-permute-done.wlo, f32[35,32,128]{2,1,0:T(8,128)S(1)} %collective-permute-done.1.whi, f32[35,16,128]{2,1,0:T(8,128)S(1)} %collective-permute-done.2.nlo, ...), custom_call_target="tpu_custom_call" | custom-call | tf_op jit(solution)/shard_map/flow/pallas_call | solution.py:530
  42.8 12.2 %all-to-all-done.got = bf16[128,16,128]{2,1,0:T(8,128)(2,1)S(1)} async-done(((bf16[128,16,128]{2,1,0:T(8,128)(2,1)}), bf16[128,16,128]{2,1,0:T(8,128)(2,1)S(1)}, u32[]{:S(2)}, u32[]{:S(2)}) %all-to-all-start) | async-done | bytes 524320 | tf_op jit(solution)/shard_map/all_to_all | solution.py:525
  55.0 0.1 broadcast_in_dim.2.column
  55.1 1.3 %last.1 = (bf16[3,256,128]{2,1,0:T(8,128)(2,1)}, f32[3,256,128]{2,1,0:T(8,128)}) custom-call(s32[256,128]{1,0:T(8,128)S(1)} %broadcast_in_dim.2.column, bf16[128,16,128]{2,1,0:T(8,128)(2,1)S(1)} %all-to-all-done.got, f32[3,256,128]{2,1,0:T(8,128)S(1)} %flow.1.base), custom_call_target="tpu_custom_call" | custom-call | tf_op jit(solution)/shard_map/last/pallas_call | solution.py:537
  (2 shorter events, 0.0 us)
Async XLA Ops:
  0.6 24.2 %copy-start.3 = (f32[16]{0:T(128)S(1)}, f32[16]{0:T(128)}, u32[]{:S(2)}) copy-start(f32[16]{0:T(128)} %rk.3) | copy-start | bytes 196
  0.6 24.1 %copy-start = (f32[3,16,32,128]{3,2,1,0:T(8,128)S(1)}, f32[3,16,32,128]{3,2,1,0:T(8,128)}, u32[]{:S(2)}) copy-start(f32[3,16,32,128]{3,2,1,0:T(8,128)} %src.3) | copy-start | bytes 2359300
  0.7 24.1 %copy-start.2 = (s32[16,32,128]{2,1,0:T(8,128)S(1)}, s32[16,32,128]{2,1,0:T(8,128)}, u32[]{:S(2)}) copy-start(s32[16,32,128]{2,1,0:T(8,128)} %lab.3) | copy-start | bytes 786436
  0.7 12.5 %copy-start.4 = (s32[1,128,4]{1,2,0:T(4,128)S(1)}, s32[1,128,4]{1,2,0:T(4,128)}, u32[]{:S(2)}) copy-start(s32[1,128,4]{1,2,0:T(4,128)} %param.11) | copy-start | bytes 6148
  4.8 26.5 %collective-permute-start = (f32[35,32,128]{2,1,0:T(8,128)}, f32[35,32,128]{2,1,0:T(8,128)S(1)}, u32[]{:S(2)}, u32[]{:S(2)}) collective-permute-start(f32[35,32,128]{2,1,0:T(8,128)} %get-tuple-element.18), channel_id=1, source_target_pairs={{0,8},{8,16},{16,24},{24,32},{32,40},{40,48},{48,56},{56,64},{64,7... | collective-permute-start | bytes 1720328 | tf_op jit(solution)/shard_map/ppermute | solution.py:439
  7.0 24.3 %collective-permute-start.1 = (f32[35,32,128]{2,1,0:T(8,128)}, f32[35,32,128]{2,1,0:T(8,128)S(1)}, u32[]{:S(2)}, u32[]{:S(2)}) collective-permute-start(f32[35,32,128]{2,1,0:T(8,128)} %get-tuple-element.19), channel_id=1, source_target_pairs={{8,0},{16,8},{24,16},{32,24},{40,32},{48,40},{56,48},{64,56},{72,6... | collective-permute-start | bytes 1720328 | tf_op jit(solution)/shard_map/ppermute | solution.py:439
  10.7 6.4 %collective-permute-start.2 = (f32[35,16,128]{2,1,0:T(8,128)}, f32[35,16,128]{2,1,0:T(8,128)S(1)}, u32[]{:S(2)}, u32[]{:S(2)}) collective-permute-start(f32[35,16,128]{2,1,0:T(8,128)} %get-tuple-element.20), channel_id=1, source_target_pairs={{0,1},{1,2},{2,3},{3,4},{4,5},{5,6},{6,7},{7,0},{8,9},{9,10},{10,1... | collective-permute-start | bytes 860168 | tf_op jit(solution)/shard_map/ppermute | solution.py:439
  13.2 6.6 %collective-permute-start.3 = (f32[35,16,128]{2,1,0:T(8,128)}, f32[35,16,128]{2,1,0:T(8,128)S(1)}, u32[]{:S(2)}, u32[]{:S(2)}) collective-permute-start(f32[35,16,128]{2,1,0:T(8,128)} %get-tuple-element.21), channel_id=1, source_target_pairs={{1,0},{2,1},{3,2},{4,3},{5,4},{6,5},{7,6},{0,7},{9,8},{10,9},{11,1... | collective-permute-start | bytes 860168 | tf_op jit(solution)/shard_map/ppermute | solution.py:439
  19.8 11.4 %collective-permute-start.4 = (f32[128,128]{1,0:T(8,128)S(1)}, f32[128,128]{1,0:T(8,128)S(1)}, u32[]{:S(2)}, u32[]{:S(2)}) collective-permute-start(f32[128,128]{1,0:T(8,128)S(1)} %get-tuple-element.22), channel_id=1, source_target_pairs={{0,8},{8,16},{16,24},{24,32},{32,40},{40,48},{48,56},{56,64},{64,7... | collective-permute-start | bytes 196616 | tf_op jit(solution)/shard_map/ppermute | solution.py:439
  19.9 11.3 %collective-permute-start.5 = (f32[128,128]{1,0:T(8,128)S(1)}, f32[128,128]{1,0:T(8,128)S(1)}, u32[]{:S(2)}, u32[]{:S(2)}) collective-permute-start(f32[128,128]{1,0:T(8,128)S(1)} %get-tuple-element.23), channel_id=1, source_target_pairs={{8,0},{16,8},{24,16},{32,24},{40,32},{48,40},{56,48},{64,56},{72,6... | collective-permute-start | bytes 196616 | tf_op jit(solution)/shard_map/ppermute | solution.py:439
  31.3 10.1 %copy-start.5 = (s32[1,256]{1,0:T(1,128)S(1)}, s32[1,256]{1,0:T(1,128)}, u32[]{:S(2)}) copy-start(s32[1,256]{1,0:T(1,128)} %param.12) | copy-start | bytes 3076
  31.3 10.1 %copy-start.1 = (f32[3,8,32,128]{3,2,1,0:T(8,128)S(1)}, f32[3,8,32,128]{3,2,1,0:T(8,128)}, u32[]{:S(2)}) copy-start(f32[3,8,32,128]{3,2,1,0:T(8,128)} %vel.1) | copy-start | bytes 1179652
  36.8 18.3 %all-to-all-start = ((bf16[128,16,128]{2,1,0:T(8,128)(2,1)}), bf16[128,16,128]{2,1,0:T(8,128)(2,1)S(1)}, u32[]{:S(2)}, u32[]{:S(2)}) async-start(bf16[128,16,128]{2,1,0:T(8,128)(2,1)} %get-tuple-element.30), calls=%async_computation | async-start | bytes 1048576 | tf_op jit(solution)/shard_map/all_to_all | solution.py:525

commit v5 on v4

--- a/solution.py
+++ b/solution.py
@@ -268,8 +268,8 @@
 
 
 def outer_kernel(
-    span_x, span_y, slots, flags, pot, wlo, whi, nlo, nhi, clo, chi, hot, halves, nexts, fields, some_force, old_nxt,
-    nxt, out, s0, s1, s2, field, force, sent, sems, sent_sems,
+    span_x, span_y, slots, flags, pot, wlo, whi, nlo, nhi, clo, chi, hot_far, halves, nexts, fields, some_force, old_nxt,
+    nxt, out, s0, s1, s2, field, force, sent, hot, sems, sent_sems,
 ):
     depth = pot.shape[-1]
     planes = 8 * DEEP + 4 * FLAT
@@ -286,6 +286,7 @@
             late.append(copies.start(ref.at[pl.ds(8 * d, 8)], s0.at[:, pl.ds(at(x), span_y), :]))
     for x in (0, 1, span_x - 2, span_x - 1):
         late.append(copies.start(pot.at[:, x], s0.at[:, pl.ds(at(x), span_y), :]))
+    picks = copies.start(hot_far, hot)
     for c in range(8):
         for i, x in enumerate((1, 2, span_x - 3, span_x - 2)):
             s1[c, stored(x), :] = halves[c, kept(i), :]
@@ -339,6 +340,7 @@
     ]
     both(-3, 0, lambda x: force_plane(s2, field, force, span_y, x))
 
+    picks.wait()
     table = jnp.concatenate([force[c].astype(BF16) for c in range(3)], axis=1)
     chunk = 256
     upper = lax.broadcasted_iota(jnp.int32, (chunk // 8, 8, depth), 1) < slots
@@ -516,10 +518,11 @@
             fields,
             ((3, cells, depth), F32),
             ((peers, 16, depth), BF16),
-            pltpu.SemaphoreType.DMA((2 * FLAT + 2 * DEEP + 8,)),
+            (hot.shape, BF16),
+            pltpu.SemaphoreType.DMA((2 * FLAT + 2 * DEEP + 9,)),
             pltpu.SemaphoreType.DMA((hot.shape[0] // 256,)),
         ],
-        smem=1, count=14, hbm=(1, 2, 3, 13), hbm_out=(0, 1), alias={13: 0}, limit=LIMIT_OUT,
+        smem=1, count=14, hbm=(1, 2, 3, 8, 13), hbm_out=(0, 1), alias={13: 0}, limit=LIMIT_OUT,
     )(flags, potential, wlo, whi, nlo, nhi, clo, chi, hot, halves, nexts, edge_fields, force, nxt)
 
     incoming = lax.all_to_all(

time: 56.7 us -> 56 us (0.988)
  Pallas kernels: 18.7 us -> 18.1 us
    pallas_call x1, Pallas kernels: 5.48 us -> 4.85 us  [body(): call(functools.partial(outer_kernel, span_x, span_y, slots), [(potential....]
where the time goes in v5:
time: 56 us; the launch traced here: 55.8 us
  Pallas kernels  18.1 us (32%)
  starting transfers between devices  17.9 us (32%)
  waiting for transfers between devices  17.4 us (31%)
  other arithmetic  1.32 us (2%)
  between operations  0.82 us (1%)
    all_to_all x1, waiting for transfers between devices, body(): lax.all_to_all(outgoing, ('wide', 'narrow'), split_axis=0, concat_axis=0,...  12.2 us
    ppermute x3, starting transfers between devices, swap(): lax.ppermute(low, axis, backward)  8.49 us
    pallas_call x1, Pallas kernels, body(): call(functools.partial(inner_kernel, span_x, span_y, regions), [(potentia...  6.43 us
    pallas_call x1, Pallas kernels, body(): call(functools.partial(outer_kernel, span_x, span_y, slots), [(potential....  4.85 us
    ppermute x3, starting transfers between devices, swap(): lax.ppermute(high, axis, forward)  4.8 us
    all_to_all x1, starting transfers between devices, body(): lax.all_to_all(outgoing, ('wide', 'narrow'), split_axis=0, concat_axis=0,...  4.57 us
    pallas_call x1, Pallas kernels, body(): call(functools.partial(faces_kernel, span_x, span_y, regions), [wide, wid...  4.08 us
    ppermute x3, waiting for transfers between devices, swap(): lax.ppermute(low, axis, backward)  2.67 us
  transfers between devices with their start and end apart: 7, of which 3 were waited for; matrix products, arithmetic and copies ran while one was open for 3% of the time, Pallas kernels for 14%

profile of v5, /device:TPU:1, one launch (start us, length us, event | category | flops | bytes accessed | tf_op | source)
XLA Modules:
  0.0 55.8 jit_solution(15583837829530991612)
XLA Ops:
  0.6 0.0 copy-start.3
  0.6 0.0 copy-start
  0.7 0.0 copy-start.2
  0.7 0.0 copy-start.4
  0.7 4.1 %faces.1 = (f32[35,32,128]{2,1,0:T(8,128)}, f32[35,32,128]{2,1,0:T(8,128)}, f32[35,16,128]{2,1,0:T(8,128)}, f32[35,16,128]{2,1,0:T(8,128)}) custom-call(f32[16]{0:T(128)} %rk.3, f32[8,16,32,128]{3,2,1,0:T(8,128)} %pot.5, f32[3,16,32,128]{3,2,1,0:T(8,128)} %src.3, s32[16,32,128]{2,1,0:T(8,128)} %lab.3, f32[3,8,32,128]{3,2,1,0:T(8,128)} %vel.1), custom_call_target="tpu_custom_call" | custom-call | tf_op jit(solution)/shard_map/faces/pallas_call | solution.py:456
  4.8 2.2 %collective-permute-start = (f32[35,32,128]{2,1,0:T(8,128)}, f32[35,32,128]{2,1,0:T(8,128)S(1)}, u32[]{:S(2)}, u32[]{:S(2)}) collective-permute-start(f32[35,32,128]{2,1,0:T(8,128)} %get-tuple-element.18), channel_id=1, source_target_pairs={{0,8},{8,16},{16,24},{24,32},{32,40},{40,48},{48,56},{56,64},{64,7... | collective-permute-start | bytes 1720328 | tf_op jit(solution)/shard_map/ppermute | solution.py:441
  7.0 3.7 %collective-permute-start.1 = (f32[35,32,128]{2,1,0:T(8,128)}, f32[35,32,128]{2,1,0:T(8,128)S(1)}, u32[]{:S(2)}, u32[]{:S(2)}) collective-permute-start(f32[35,32,128]{2,1,0:T(8,128)} %get-tuple-element.19), channel_id=1, source_target_pairs={{8,0},{16,8},{24,16},{32,24},{40,32},{48,40},{56,48},{64,56},{72,6... | collective-permute-start | bytes 1720328 | tf_op jit(solution)/shard_map/ppermute | solution.py:441
  10.7 2.5 %collective-permute-start.2 = (f32[35,16,128]{2,1,0:T(8,128)}, f32[35,16,128]{2,1,0:T(8,128)S(1)}, u32[]{:S(2)}, u32[]{:S(2)}) collective-permute-start(f32[35,16,128]{2,1,0:T(8,128)} %get-tuple-element.20), channel_id=1, source_target_pairs={{0,1},{1,2},{2,3},{3,4},{4,5},{5,6},{6,7},{7,0},{8,9},{9,10},{10,1... | collective-permute-start | bytes 860168 | tf_op jit(solution)/shard_map/ppermute | solution.py:441
  13.2 0.0 collective-permute-start.3
  13.2 0.0 copy-done.4
  13.2 0.1 copy.11
  13.3 0.1 eq.17
  13.4 1.2 %fusion.hot_far = bf16[1024,512]{1,0:T(8,128)(2,1)} fusion(s32[1024]{0:T(1024)S(1)} %eq.17), kind=kLoop, calls=%fused_computation.1 | loop fusion | flops 1048576 | bytes 1052672 | tf_op jit(solution)/shard_map/convert_element_type | solution.py:509
  14.7 2.5 %collective-permute-done.2.nlo = f32[35,16,128]{2,1,0:T(8,128)S(1)} collective-permute-done((f32[35,16,128]{2,1,0:T(8,128)}, f32[35,16,128]{2,1,0:T(8,128)S(1)}, u32[]{:S(2)}, u32[]{:S(2)}) %collective-permute-start.2) | collective-permute-done | bytes 286752 | tf_op jit(solution)/shard_map/ppermute | solution.py:441
  17.1 2.7 %collective-permute-done.3.nhi = f32[35,16,128]{2,1,0:T(8,128)S(1)} collective-permute-done((f32[35,16,128]{2,1,0:T(8,128)}, f32[35,16,128]{2,1,0:T(8,128)S(1)}, u32[]{:S(2)}, u32[]{:S(2)}) %collective-permute-start.3) | collective-permute-done | bytes 286752 | tf_op jit(solution)/shard_map/ppermute | solution.py:441
  19.8 0.1 corner.1
  19.8 0.1 collective-permute-start.4
  19.9 4.8 %collective-permute-start.5 = (f32[128,128]{1,0:T(8,128)S(1)}, f32[128,128]{1,0:T(8,128)S(1)}, u32[]{:S(2)}, u32[]{:S(2)}) collective-permute-start(f32[128,128]{1,0:T(8,128)S(1)} %get-tuple-element.23), channel_id=1, source_target_pairs={{8,0},{16,8},{24,16},{32,24},{40,32},{48,40},{56,48},{64,56},{72,6... | collective-permute-start | bytes 196616 | tf_op jit(solution)/shard_map/ppermute | solution.py:441
  24.7 0.1 add_convert_fusion.flags
  24.8 0.0 copy-done.3
  24.8 0.0 copy-done
  24.8 0.0 copy-done.2
  24.8 6.4 %inner.1 = (f32[8,16,32,128]{3,2,1,0:T(8,128)}, f32[8,192,128]{2,1,0:T(8,128)S(1)}, f32[8,192,128]{2,1,0:T(8,128)S(1)}, f32[5,288,128]{2,1,0:T(8,128)S(1)}, f32[3,512,128]{2,1,0:T(8,128)S(1)}) custom-call(f32[4]{0:T(128)S(1)} %add_convert_fusion.flags, f32[16]{0:T(128)S(1)} %copy-done.3, f32[8,16,32,128]{3,2,1,0:T(8,128)} %pot.5, ...), custom_call_target="tpu_custom_call" | custom-call | tf_op jit(solution)/shard_map/inner/pallas_call | solution.py:486
  31.2 0.0 collective-permute-done.4.clo
  31.2 0.0 collective-permute-done.5.chi
  31.2 0.0 collective-permute-done.wlo
  31.3 0.0 collective-permute-done.1.whi
  31.3 0.0 copy-start.5
  31.3 0.0 copy-start.1
  31.3 4.8 %outer.1 = (f32[8,16,32,128]{3,2,1,0:T(8,128)}, bf16[128,16,128]{2,1,0:T(8,128)(2,1)}) custom-call(f32[4]{0:T(128)S(1)} %add_convert_fusion.flags, f32[8,16,32,128]{3,2,1,0:T(8,128)} %pot.5, f32[35,32,128]{2,1,0:T(8,128)S(1)} %collective-permute-done.wlo, f32[35,32,128]{2,1,0:T(8,128)S(1)} %collective-permute-done.1.whi, ...), custom_call_target="tpu_custom_call", output_to_operand_aliasing={{0}: (13, {})} | custom-call | tf_op jit(solution)/shard_map/outer/pallas_call | solution.py:510
  36.1 4.6 %all-to-all-start = ((bf16[128,16,128]{2,1,0:T(8,128)(2,1)}), bf16[128,16,128]{2,1,0:T(8,128)(2,1)S(1)}, u32[]{:S(2)}, u32[]{:S(2)}) async-start(bf16[128,16,128]{2,1,0:T(8,128)(2,1)} %get-tuple-element.30), calls=%async_computation | async-start | bytes 1048576 | tf_op jit(solution)/shard_map/all_to_all | solution.py:528
  40.7 0.0 copy-done.5
  40.8 0.0 copy-done.1
  40.8 1.4 %flow.1.base = f32[3,256,128]{2,1,0:T(8,128)S(1)} custom-call(f32[4]{0:T(128)S(1)} %add_convert_fusion.flags, f32[3,256,128]{2,1,0:T(8,128)S(1)} %bitcast.9, f32[35,32,128]{2,1,0:T(8,128)S(1)} %collective-permute-done.wlo, f32[35,32,128]{2,1,0:T(8,128)S(1)} %collective-permute-done.1.whi, f32[35,16,128]{2,1,0:T(8,128)S(1)} %collective-permute-done.2.nlo, ...), custom_call_target="tpu_custom_call" | custom-call | tf_op jit(solution)/shard_map/flow/pallas_call | solution.py:533
  42.2 12.2 %all-to-all-done.got = bf16[128,16,128]{2,1,0:T(8,128)(2,1)S(1)} async-done(((bf16[128,16,128]{2,1,0:T(8,128)(2,1)}), bf16[128,16,128]{2,1,0:T(8,128)(2,1)S(1)}, u32[]{:S(2)}, u32[]{:S(2)}) %all-to-all-start) | async-done | bytes 524320 | tf_op jit(solution)/shard_map/all_to_all | solution.py:528
  54.4 0.1 broadcast_in_dim.2.column
  54.5 1.3 %last.1 = (bf16[3,256,128]{2,1,0:T(8,128)(2,1)}, f32[3,256,128]{2,1,0:T(8,128)}) custom-call(s32[256,128]{1,0:T(8,128)S(1)} %broadcast_in_dim.2.column, bf16[128,16,128]{2,1,0:T(8,128)(2,1)S(1)} %all-to-all-done.got, f32[3,256,128]{2,1,0:T(8,128)S(1)} %flow.1.base), custom_call_target="tpu_custom_call" | custom-call | tf_op jit(solution)/shard_map/last/pallas_call | solution.py:540
  (2 shorter events, 0.0 us)
Async XLA Ops:
  0.6 24.2 %copy-start.3 = (f32[16]{0:T(128)S(1)}, f32[16]{0:T(128)}, u32[]{:S(2)}) copy-start(f32[16]{0:T(128)} %rk.3) | copy-start | bytes 196
  0.6 24.1 %copy-start = (f32[3,16,32,128]{3,2,1,0:T(8,128)S(1)}, f32[3,16,32,128]{3,2,1,0:T(8,128)}, u32[]{:S(2)}) copy-start(f32[3,16,32,128]{3,2,1,0:T(8,128)} %src.3) | copy-start | bytes 2359300
  0.7 24.1 %copy-start.2 = (s32[16,32,128]{2,1,0:T(8,128)S(1)}, s32[16,32,128]{2,1,0:T(8,128)}, u32[]{:S(2)}) copy-start(s32[16,32,128]{2,1,0:T(8,128)} %lab.3) | copy-start | bytes 786436
  0.7 12.5 %copy-start.4 = (s32[1,128,4]{1,2,0:T(4,128)S(1)}, s32[1,128,4]{1,2,0:T(4,128)}, u32[]{:S(2)}) copy-start(s32[1,128,4]{1,2,0:T(4,128)} %param.11) | copy-start | bytes 6148
  4.8 26.5 %collective-permute-start = (f32[35,32,128]{2,1,0:T(8,128)}, f32[35,32,128]{2,1,0:T(8,128)S(1)}, u32[]{:S(2)}, u32[]{:S(2)}) collective-permute-start(f32[35,32,128]{2,1,0:T(8,128)} %get-tuple-element.18), channel_id=1, source_target_pairs={{0,8},{8,16},{16,24},{24,32},{32,40},{40,48},{48,56},{56,64},{64,7... | collective-permute-start | bytes 1720328 | tf_op jit(solution)/shard_map/ppermute | solution.py:441
  7.0 24.3 %collective-permute-start.1 = (f32[35,32,128]{2,1,0:T(8,128)}, f32[35,32,128]{2,1,0:T(8,128)S(1)}, u32[]{:S(2)}, u32[]{:S(2)}) collective-permute-start(f32[35,32,128]{2,1,0:T(8,128)} %get-tuple-element.19), channel_id=1, source_target_pairs={{8,0},{16,8},{24,16},{32,24},{40,32},{48,40},{56,48},{64,56},{72,6... | collective-permute-start | bytes 1720328 | tf_op jit(solution)/shard_map/ppermute | solution.py:441
  10.7 6.4 %collective-permute-start.2 = (f32[35,16,128]{2,1,0:T(8,128)}, f32[35,16,128]{2,1,0:T(8,128)S(1)}, u32[]{:S(2)}, u32[]{:S(2)}) collective-permute-start(f32[35,16,128]{2,1,0:T(8,128)} %get-tuple-element.20), channel_id=1, source_target_pairs={{0,1},{1,2},{2,3},{3,4},{4,5},{5,6},{6,7},{7,0},{8,9},{9,10},{10,1... | collective-permute-start | bytes 860168 | tf_op jit(solution)/shard_map/ppermute | solution.py:441
  13.2 6.6 %collective-permute-start.3 = (f32[35,16,128]{2,1,0:T(8,128)}, f32[35,16,128]{2,1,0:T(8,128)S(1)}, u32[]{:S(2)}, u32[]{:S(2)}) collective-permute-start(f32[35,16,128]{2,1,0:T(8,128)} %get-tuple-element.21), channel_id=1, source_target_pairs={{1,0},{2,1},{3,2},{4,3},{5,4},{6,5},{7,6},{0,7},{9,8},{10,9},{11,1... | collective-permute-start | bytes 860168 | tf_op jit(solution)/shard_map/ppermute | solution.py:441
  19.8 11.4 %collective-permute-start.4 = (f32[128,128]{1,0:T(8,128)S(1)}, f32[128,128]{1,0:T(8,128)S(1)}, u32[]{:S(2)}, u32[]{:S(2)}) collective-permute-start(f32[128,128]{1,0:T(8,128)S(1)} %get-tuple-element.22), channel_id=1, source_target_pairs={{0,8},{8,16},{16,24},{24,32},{32,40},{40,48},{48,56},{56,64},{64,7... | collective-permute-start | bytes 196616 | tf_op jit(solution)/shard_map/ppermute | solution.py:441
  19.9 11.3 %collective-permute-start.5 = (f32[128,128]{1,0:T(8,128)S(1)}, f32[128,128]{1,0:T(8,128)S(1)}, u32[]{:S(2)}, u32[]{:S(2)}) collective-permute-start(f32[128,128]{1,0:T(8,128)S(1)} %get-tuple-element.23), channel_id=1, source_target_pairs={{8,0},{16,8},{24,16},{32,24},{40,32},{48,40},{56,48},{64,56},{72,6... | collective-permute-start | bytes 196616 | tf_op jit(solution)/shard_map/ppermute | solution.py:441
  31.3 9.5 %copy-start.5 = (s32[1,256]{1,0:T(1,128)S(1)}, s32[1,256]{1,0:T(1,128)}, u32[]{:S(2)}) copy-start(s32[1,256]{1,0:T(1,128)} %param.12) | copy-start | bytes 3076
  31.3 9.5 %copy-start.1 = (f32[3,8,32,128]{3,2,1,0:T(8,128)S(1)}, f32[3,8,32,128]{3,2,1,0:T(8,128)}, u32[]{:S(2)}) copy-start(f32[3,8,32,128]{3,2,1,0:T(8,128)} %vel.1) | copy-start | bytes 1179652
  36.1 18.3 %all-to-all-start = ((bf16[128,16,128]{2,1,0:T(8,128)(2,1)}), bf16[128,16,128]{2,1,0:T(8,128)(2,1)S(1)}, u32[]{:S(2)}, u32[]{:S(2)}) async-start(bf16[128,16,128]{2,1,0:T(8,128)(2,1)} %get-tuple-element.30), calls=%async_computation | async-start | bytes 1048576 | tf_op jit(solution)/shard_map/all_to_all | solution.py:528

commit v6 on v5

--- a/solution.py
+++ b/solution.py
@@ -88,12 +88,16 @@
 
 
 def corner_kernel(span_x, nlo, nhi, clo, chi):
-    planes = 8 * DEEP + 4 * FLAT
-    for d in range(FLAT):
-        for side, ref in enumerate((nlo, nhi)):
-            rows = pl.ds((d * 2 + side) * planes, planes)
-            clo[rows, :] = ref[:planes, d, :]
-            chi[rows, :] = ref[:planes, span_x - 1 - d, :]
+    flat = 8 * DEEP
+    for side, ref in enumerate((nlo, nhi)):
+        for out, x, beyond in ((clo, 0, 1), (chi, span_x - 1, span_x - 2)):
+            out[pl.ds(32 * side, 16), :] = ref[:16, x, :]
+            out[pl.ds(32 * side + 16, 8), :] = ref[:8, beyond, :]
+            out[pl.ds(32 * side + 24, 8), :] = ref[flat : flat + 8, x, :]
+
+
+def corner_row(side, c, d, e):
+    return 32 * side + (24 + c - 8 if c >= 8 else 8 * d + c if e == 0 else 16 + c)
 
 
 def place(c, d):
@@ -313,7 +317,7 @@
             for e in range(deep - 1 - d):
                 p = place(c, d)
                 for source, x in ((clo, -1 - e), (chi, span_x + e)):
-                    low, high = (source[pl.ds((e * 2 + side) * planes + p, 1), :] for side in range(2))
+                    low, high = (source[pl.ds(corner_row(side, c, d, e), 1), :] for side in range(2))
                     ref[part, pl.ds(at(x) - 1 - d, 1), :] = low * flags[2]
                     ref[part, pl.ds(at(x) + span_y + d, 1), :] = high * flags[3]
 
@@ -469,7 +473,7 @@
     nlo, nhi = swap(nlo, nhi, "narrow")
     wlo, whi = swap(wlo, whi, "wide")
 
-    corner = ((FLAT * 2 * (8 * DEEP + 4 * FLAT), depth), F32)
+    corner = ((64, depth), F32)
     clo, chi = call(
         functools.partial(corner_kernel, span_x), [corner, corner], "corner", count=2
     )(nlo, nhi)

time: 56 us -> 56 us (level)
  no operation moved by 1% of the time
where the time goes in v6:
time: 56 us; the launch traced here: 55.7 us
  Pallas kernels  18.1 us (32%)
  starting transfers between devices  17.9 us (32%)
  waiting for transfers between devices  17.4 us (31%)
  other arithmetic  1.32 us (2%)
  between operations  0.82 us (1%)
    all_to_all x1, waiting for transfers between devices, body(): lax.all_to_all(outgoing, ('wide', 'narrow'), split_axis=0, concat_axis=0,...  12.2 us
    ppermute x3, starting transfers between devices, swap(): lax.ppermute(low, axis, backward)  8.49 us
    pallas_call x1, Pallas kernels, body(): call(functools.partial(inner_kernel, span_x, span_y, regions), [(potentia...  6.43 us
    pallas_call x1, Pallas kernels, body(): call(functools.partial(outer_kernel, span_x, span_y, slots), [(potential....  4.85 us
    ppermute x3, starting transfers between devices, swap(): lax.ppermute(high, axis, forward)  4.8 us
    all_to_all x1, starting transfers between devices, body(): lax.all_to_all(outgoing, ('wide', 'narrow'), split_axis=0, concat_axis=0,...  4.57 us
    pallas_call x1, Pallas kernels, body(): call(functools.partial(faces_kernel, span_x, span_y, regions), [wide, wid...  4.08 us
    ppermute x3, waiting for transfers between devices, swap(): lax.ppermute(low, axis, backward)  2.67 us
  transfers between devices with their start and end apart: 7, of which 3 were waited for; matrix products, arithmetic and copies ran while one was open for 3% of the time, Pallas kernels for 14%

profile of v6, /device:TPU:1, one launch (start us, length us, event | category | flops | bytes accessed | tf_op | source)
XLA Modules:
  0.0 55.7 jit_solution(8238106214693039)
XLA Ops:
  0.6 0.0 copy-start.3
  0.6 0.0 copy-start
  0.7 0.0 copy-start.2
  0.7 0.0 copy-start.4
  0.7 4.1 %faces.1 = (f32[35,32,128]{2,1,0:T(8,128)}, f32[35,32,128]{2,1,0:T(8,128)}, f32[35,16,128]{2,1,0:T(8,128)}, f32[35,16,128]{2,1,0:T(8,128)}) custom-call(f32[16]{0:T(128)} %rk.3, f32[8,16,32,128]{3,2,1,0:T(8,128)} %pot.5, f32[3,16,32,128]{3,2,1,0:T(8,128)} %src.3, s32[16,32,128]{2,1,0:T(8,128)} %lab.3, f32[3,8,32,128]{3,2,1,0:T(8,128)} %vel.1), custom_call_target="tpu_custom_call" | custom-call | tf_op jit(solution)/shard_map/faces/pallas_call | solution.py:460
  4.8 2.2 %collective-permute-start = (f32[35,32,128]{2,1,0:T(8,128)}, f32[35,32,128]{2,1,0:T(8,128)S(1)}, u32[]{:S(2)}, u32[]{:S(2)}) collective-permute-start(f32[35,32,128]{2,1,0:T(8,128)} %get-tuple-element.18), channel_id=1, source_target_pairs={{0,8},{8,16},{16,24},{24,32},{32,40},{40,48},{48,56},{56,64},{64,7... | collective-permute-start | bytes 1720328 | tf_op jit(solution)/shard_map/ppermute | solution.py:445
  7.0 3.7 %collective-permute-start.1 = (f32[35,32,128]{2,1,0:T(8,128)}, f32[35,32,128]{2,1,0:T(8,128)S(1)}, u32[]{:S(2)}, u32[]{:S(2)}) collective-permute-start(f32[35,32,128]{2,1,0:T(8,128)} %get-tuple-element.19), channel_id=1, source_target_pairs={{8,0},{16,8},{24,16},{32,24},{40,32},{48,40},{56,48},{64,56},{72,6... | collective-permute-start | bytes 1720328 | tf_op jit(solution)/shard_map/ppermute | solution.py:445
  10.7 2.5 %collective-permute-start.2 = (f32[35,16,128]{2,1,0:T(8,128)}, f32[35,16,128]{2,1,0:T(8,128)S(1)}, u32[]{:S(2)}, u32[]{:S(2)}) collective-permute-start(f32[35,16,128]{2,1,0:T(8,128)} %get-tuple-element.20), channel_id=1, source_target_pairs={{0,1},{1,2},{2,3},{3,4},{4,5},{5,6},{6,7},{7,0},{8,9},{9,10},{10,1... | collective-permute-start | bytes 860168 | tf_op jit(solution)/shard_map/ppermute | solution.py:445
  13.2 0.0 collective-permute-start.3
  13.2 0.0 copy-done.4
  13.2 0.1 copy.11
  13.3 0.1 eq.17
  13.4 1.2 %fusion.hot_far = bf16[1024,512]{1,0:T(8,128)(2,1)} fusion(s32[1024]{0:T(1024)S(1)} %eq.17), kind=kLoop, calls=%fused_computation.1 | loop fusion | flops 1048576 | bytes 1052672 | tf_op jit(solution)/shard_map/convert_element_type | solution.py:513
  14.7 2.5 %collective-permute-done.2.nlo = f32[35,16,128]{2,1,0:T(8,128)S(1)} collective-permute-done((f32[35,16,128]{2,1,0:T(8,128)}, f32[35,16,128]{2,1,0:T(8,128)S(1)}, u32[]{:S(2)}, u32[]{:S(2)}) %collective-permute-start.2) | collective-permute-done | bytes 286752 | tf_op jit(solution)/shard_map/ppermute | solution.py:445
  17.1 2.7 %collective-permute-done.3.nhi = f32[35,16,128]{2,1,0:T(8,128)S(1)} collective-permute-done((f32[35,16,128]{2,1,0:T(8,128)}, f32[35,16,128]{2,1,0:T(8,128)S(1)}, u32[]{:S(2)}, u32[]{:S(2)}) %collective-permute-start.3) | collective-permute-done | bytes 286752 | tf_op jit(solution)/shard_map/ppermute | solution.py:445
  19.8 0.1 collective-permute-start.4
  19.9 4.8 %collective-permute-start.5 = (f32[64,128]{1,0:T(8,128)S(1)}, f32[64,128]{1,0:T(8,128)S(1)}, u32[]{:S(2)}, u32[]{:S(2)}) collective-permute-start(f32[64,128]{1,0:T(8,128)S(1)} %get-tuple-element.23), channel_id=1, source_target_pairs={{8,0},{16,8},{24,16},{32,24},{40,32},{48,40},{56,48},{64,56},{72,6... | collective-permute-start | bytes 98312 | tf_op jit(solution)/shard_map/ppermute | solution.py:445
  24.7 0.1 add_convert_fusion.flags
  24.7 0.0 copy-done.3
  24.8 0.0 copy-done
  24.8 0.0 copy-done.2
  24.8 6.4 %inner.1 = (f32[8,16,32,128]{3,2,1,0:T(8,128)}, f32[8,192,128]{2,1,0:T(8,128)S(1)}, f32[8,192,128]{2,1,0:T(8,128)S(1)}, f32[5,288,128]{2,1,0:T(8,128)S(1)}, f32[3,512,128]{2,1,0:T(8,128)S(1)}) custom-call(f32[4]{0:T(128)S(1)} %add_convert_fusion.flags, f32[16]{0:T(128)S(1)} %copy-done.3, f32[8,16,32,128]{3,2,1,0:T(8,128)} %pot.5, ...), custom_call_target="tpu_custom_call" | custom-call | tf_op jit(solution)/shard_map/inner/pallas_call | solution.py:490
  31.2 0.0 collective-permute-done.4.clo
  31.2 0.0 collective-permute-done.5.chi
  31.2 0.0 collective-permute-done.wlo
  31.2 0.0 collective-permute-done.1.whi
  31.2 0.0 copy-start.5
  31.2 0.0 copy-start.1
  31.3 4.8 %outer.1 = (f32[8,16,32,128]{3,2,1,0:T(8,128)}, bf16[128,16,128]{2,1,0:T(8,128)(2,1)}) custom-call(f32[4]{0:T(128)S(1)} %add_convert_fusion.flags, f32[8,16,32,128]{3,2,1,0:T(8,128)} %pot.5, f32[35,32,128]{2,1,0:T(8,128)S(1)} %collective-permute-done.wlo, f32[35,32,128]{2,1,0:T(8,128)S(1)} %collective-permute-done.1.whi, ...), custom_call_target="tpu_custom_call", output_to_operand_aliasing={{0}: (13, {})} | custom-call | tf_op jit(solution)/shard_map/outer/pallas_call | solution.py:514
  36.1 4.6 %all-to-all-start = ((bf16[128,16,128]{2,1,0:T(8,128)(2,1)}), bf16[128,16,128]{2,1,0:T(8,128)(2,1)S(1)}, u32[]{:S(2)}, u32[]{:S(2)}) async-start(bf16[128,16,128]{2,1,0:T(8,128)(2,1)} %get-tuple-element.30), calls=%async_computation | async-start | bytes 1048576 | tf_op jit(solution)/shard_map/all_to_all | solution.py:532
  40.7 0.0 copy-done.5
  40.7 0.0 copy-done.1
  40.7 1.4 %flow.1.base = f32[3,256,128]{2,1,0:T(8,128)S(1)} custom-call(f32[4]{0:T(128)S(1)} %add_convert_fusion.flags, f32[3,256,128]{2,1,0:T(8,128)S(1)} %bitcast.9, f32[35,32,128]{2,1,0:T(8,128)S(1)} %collective-permute-done.wlo, f32[35,32,128]{2,1,0:T(8,128)S(1)} %collective-permute-done.1.whi, f32[35,16,128]{2,1,0:T(8,128)S(1)} %collective-permute-done.2.nlo, ...), custom_call_target="tpu_custom_call" | custom-call | tf_op jit(solution)/shard_map/flow/pallas_call | solution.py:537
  42.1 12.2 %all-to-all-done.got = bf16[128,16,128]{2,1,0:T(8,128)(2,1)S(1)} async-done(((bf16[128,16,128]{2,1,0:T(8,128)(2,1)}), bf16[128,16,128]{2,1,0:T(8,128)(2,1)S(1)}, u32[]{:S(2)}, u32[]{:S(2)}) %all-to-all-start) | async-done | bytes 524320 | tf_op jit(solution)/shard_map/all_to_all | solution.py:532
  54.4 0.1 broadcast_in_dim.2.column
  54.5 1.3 %last.1 = (bf16[3,256,128]{2,1,0:T(8,128)(2,1)}, f32[3,256,128]{2,1,0:T(8,128)}) custom-call(s32[256,128]{1,0:T(8,128)S(1)} %broadcast_in_dim.2.column, bf16[128,16,128]{2,1,0:T(8,128)(2,1)S(1)} %all-to-all-done.got, f32[3,256,128]{2,1,0:T(8,128)S(1)} %flow.1.base), custom_call_target="tpu_custom_call" | custom-call | tf_op jit(solution)/shard_map/last/pallas_call | solution.py:544
  (3 shorter events, 0.1 us)
Async XLA Ops:
  0.6 24.1 %copy-start.3 = (f32[16]{0:T(128)S(1)}, f32[16]{0:T(128)}, u32[]{:S(2)}) copy-start(f32[16]{0:T(128)} %rk.3) | copy-start | bytes 196
  0.6 24.1 %copy-start = (f32[3,16,32,128]{3,2,1,0:T(8,128)S(1)}, f32[3,16,32,128]{3,2,1,0:T(8,128)}, u32[]{:S(2)}) copy-start(f32[3,16,32,128]{3,2,1,0:T(8,128)} %src.3) | copy-start | bytes 2359300
  0.7 24.1 %copy-start.2 = (s32[16,32,128]{2,1,0:T(8,128)S(1)}, s32[16,32,128]{2,1,0:T(8,128)}, u32[]{:S(2)}) copy-start(s32[16,32,128]{2,1,0:T(8,128)} %lab.3) | copy-start | bytes 786436
  0.7 12.5 %copy-start.4 = (s32[1,128,4]{1,2,0:T(4,128)S(1)}, s32[1,128,4]{1,2,0:T(4,128)}, u32[]{:S(2)}) copy-start(s32[1,128,4]{1,2,0:T(4,128)} %param.11) | copy-start | bytes 6148
  4.8 26.5 %collective-permute-start = (f32[35,32,128]{2,1,0:T(8,128)}, f32[35,32,128]{2,1,0:T(8,128)S(1)}, u32[]{:S(2)}, u32[]{:S(2)}) collective-permute-start(f32[35,32,128]{2,1,0:T(8,128)} %get-tuple-element.18), channel_id=1, source_target_pairs={{0,8},{8,16},{16,24},{24,32},{32,40},{40,48},{48,56},{56,64},{64,7... | collective-permute-start | bytes 1720328 | tf_op jit(solution)/shard_map/ppermute | solution.py:445
  7.0 24.3 %collective-permute-start.1 = (f32[35,32,128]{2,1,0:T(8,128)}, f32[35,32,128]{2,1,0:T(8,128)S(1)}, u32[]{:S(2)}, u32[]{:S(2)}) collective-permute-start(f32[35,32,128]{2,1,0:T(8,128)} %get-tuple-element.19), channel_id=1, source_target_pairs={{8,0},{16,8},{24,16},{32,24},{40,32},{48,40},{56,48},{64,56},{72,6... | collective-permute-start | bytes 1720328 | tf_op jit(solution)/shard_map/ppermute | solution.py:445
  10.7 6.4 %collective-permute-start.2 = (f32[35,16,128]{2,1,0:T(8,128)}, f32[35,16,128]{2,1,0:T(8,128)S(1)}, u32[]{:S(2)}, u32[]{:S(2)}) collective-permute-start(f32[35,16,128]{2,1,0:T(8,128)} %get-tuple-element.20), channel_id=1, source_target_pairs={{0,1},{1,2},{2,3},{3,4},{4,5},{5,6},{6,7},{7,0},{8,9},{9,10},{10,1... | collective-permute-start | bytes 860168 | tf_op jit(solution)/shard_map/ppermute | solution.py:445
  13.2 6.6 %collective-permute-start.3 = (f32[35,16,128]{2,1,0:T(8,128)}, f32[35,16,128]{2,1,0:T(8,128)S(1)}, u32[]{:S(2)}, u32[]{:S(2)}) collective-permute-start(f32[35,16,128]{2,1,0:T(8,128)} %get-tuple-element.21), channel_id=1, source_target_pairs={{1,0},{2,1},{3,2},{4,3},{5,4},{6,5},{7,6},{0,7},{9,8},{10,9},{11,1... | collective-permute-start | bytes 860168 | tf_op jit(solution)/shard_map/ppermute | solution.py:445
  19.8 11.4 %collective-permute-start.4 = (f32[64,128]{1,0:T(8,128)S(1)}, f32[64,128]{1,0:T(8,128)S(1)}, u32[]{:S(2)}, u32[]{:S(2)}) collective-permute-start(f32[64,128]{1,0:T(8,128)S(1)} %get-tuple-element.22), channel_id=1, source_target_pairs={{0,8},{8,16},{16,24},{24,32},{32,40},{40,48},{48,56},{56,64},{64,7... | collective-permute-start | bytes 98312 | tf_op jit(solution)/shard_map/ppermute | solution.py:445
  19.9 11.3 %collective-permute-start.5 = (f32[64,128]{1,0:T(8,128)S(1)}, f32[64,128]{1,0:T(8,128)S(1)}, u32[]{:S(2)}, u32[]{:S(2)}) collective-permute-start(f32[64,128]{1,0:T(8,128)S(1)} %get-tuple-element.23), channel_id=1, source_target_pairs={{8,0},{16,8},{24,16},{32,24},{40,32},{48,40},{56,48},{64,56},{72,6... | collective-permute-start | bytes 98312 | tf_op jit(solution)/shard_map/ppermute | solution.py:445
  31.2 9.5 %copy-start.5 = (s32[1,256]{1,0:T(1,128)S(1)}, s32[1,256]{1,0:T(1,128)}, u32[]{:S(2)}) copy-start(s32[1,256]{1,0:T(1,128)} %param.12) | copy-start | bytes 3076
  31.2 9.5 %copy-start.1 = (f32[3,8,32,128]{3,2,1,0:T(8,128)S(1)}, f32[3,8,32,128]{3,2,1,0:T(8,128)}, u32[]{:S(2)}) copy-start(f32[3,8,32,128]{3,2,1,0:T(8,128)} %vel.1) | copy-start | bytes 1179652
  36.1 18.3 %all-to-all-start = ((bf16[128,16,128]{2,1,0:T(8,128)(2,1)}), bf16[128,16,128]{2,1,0:T(8,128)(2,1)S(1)}, u32[]{:S(2)}, u32[]{:S(2)}) async-start(bf16[128,16,128]{2,1,0:T(8,128)(2,1)} %get-tuple-element.30), calls=%async_computation | async-start | bytes 1048576 | tf_op jit(solution)/shard_map/all_to_all | solution.py:532

commit v7 on v6

--- a/solution.py
+++ b/solution.py
@@ -403,18 +403,23 @@
     )
     want = column[...]
     lane = lax.broadcasted_iota(jnp.int32, want.shape, 1)
-    picked = []
-    for half in range(2):
-        take = jnp.concatenate(
-            [
-                jnp.where(want == lane + (depth * k - slots * half), 1.0, 0.0).astype(BF16)
-                for k in range(values.shape[0] // depth)
-            ],
-            axis=1,
-        )
-        picked.append(jnp.dot(take, values, preferred_element_type=F32))
+    take = jnp.concatenate(
+        [
+            jnp.concatenate(
+                [
+                    jnp.where(want == lane + (depth * k - slots * half), 1.0, 0.0).astype(BF16)
+                    for k in range(values.shape[0] // depth)
+                ],
+                axis=1,
+            )
+            for half in range(2)
+        ],
+        axis=0,
+    )
+    picked = jnp.dot(take, values, preferred_element_type=F32)
     for c in range(3):
-        push = picked[c % 2][:, (c // 2) * depth : (c // 2 + 1) * depth].astype(BF16)
+        part = picked[(c % 2) * lines : (c % 2 + 1) * lines, (c // 2) * depth : (c // 2 + 1) * depth]
+        push = part.astype(BF16)
         les[c] = push
         nxt[c] = base[c] + DT * push.astype(F32)
 

time: 56 us -> 56 us (level)
  no operation moved by 1% of the time
where the time goes in v7:
time: 56 us; the launch traced here: 55.7 us
  Pallas kernels  18.1 us (32%)
  starting transfers between devices  17.9 us (32%)
  waiting for transfers between devices  17.4 us (31%)
  other arithmetic  1.32 us (2%)
  between operations  0.82 us (1%)
    all_to_all x1, waiting for transfers between devices, body(): lax.all_to_all(outgoing, ('wide', 'narrow'), split_axis=0, concat_axis=0,...  12.2 us
    ppermute x3, starting transfers between devices, swap(): lax.ppermute(low, axis, backward)  8.49 us
    pallas_call x1, Pallas kernels, body(): call(functools.partial(inner_kernel, span_x, span_y, regions), [(potentia...  6.43 us
    pallas_call x1, Pallas kernels, body(): call(functools.partial(outer_kernel, span_x, span_y, slots), [(potential....  4.85 us
    ppermute x3, starting transfers between devices, swap(): lax.ppermute(high, axis, forward)  4.8 us
    all_to_all x1, starting transfers between devices, body(): lax.all_to_all(outgoing, ('wide', 'narrow'), split_axis=0, concat_axis=0,...  4.57 us
    pallas_call x1, Pallas kernels, body(): call(functools.partial(faces_kernel, span_x, span_y, regions), [wide, wid...  4.08 us
    ppermute x3, waiting for transfers between devices, swap(): lax.ppermute(low, axis, backward)  2.67 us
  transfers between devices with their start and end apart: 7, of which 3 were waited for; matrix products, arithmetic and copies ran while one was open for 3% of the time, Pallas kernels for 14%

profile of v7, /device:TPU:1, one launch (start us, length us, event | category | flops | bytes accessed | tf_op | source)
XLA Modules:
  0.0 55.7 jit_solution(3190713300844466707)
XLA Ops:
  0.6 0.0 copy-start.3
  0.6 0.0 copy-start
  0.7 0.0 copy-start.2
  0.7 0.0 copy-start.4
  0.7 4.1 %faces.1 = (f32[35,32,128]{2,1,0:T(8,128)}, f32[35,32,128]{2,1,0:T(8,128)}, f32[35,16,128]{2,1,0:T(8,128)}, f32[35,16,128]{2,1,0:T(8,128)}) custom-call(f32[16]{0:T(128)} %rk.3, f32[8,16,32,128]{3,2,1,0:T(8,128)} %pot.5, f32[3,16,32,128]{3,2,1,0:T(8,128)} %src.3, s32[16,32,128]{2,1,0:T(8,128)} %lab.3, f32[3,8,32,128]{3,2,1,0:T(8,128)} %vel.1), custom_call_target="tpu_custom_call" | custom-call | tf_op jit(solution)/shard_map/faces/pallas_call | solution.py:465
  4.8 2.2 %collective-permute-start = (f32[35,32,128]{2,1,0:T(8,128)}, f32[35,32,128]{2,1,0:T(8,128)S(1)}, u32[]{:S(2)}, u32[]{:S(2)}) collective-permute-start(f32[35,32,128]{2,1,0:T(8,128)} %get-tuple-element.18), channel_id=1, source_target_pairs={{0,8},{8,16},{16,24},{24,32},{32,40},{40,48},{48,56},{56,64},{64,7... | collective-permute-start | bytes 1720328 | tf_op jit(solution)/shard_map/ppermute | solution.py:450
  7.0 3.7 %collective-permute-start.1 = (f32[35,32,128]{2,1,0:T(8,128)}, f32[35,32,128]{2,1,0:T(8,128)S(1)}, u32[]{:S(2)}, u32[]{:S(2)}) collective-permute-start(f32[35,32,128]{2,1,0:T(8,128)} %get-tuple-element.19), channel_id=1, source_target_pairs={{8,0},{16,8},{24,16},{32,24},{40,32},{48,40},{56,48},{64,56},{72,6... | collective-permute-start | bytes 1720328 | tf_op jit(solution)/shard_map/ppermute | solution.py:450
  10.7 2.5 %collective-permute-start.2 = (f32[35,16,128]{2,1,0:T(8,128)}, f32[35,16,128]{2,1,0:T(8,128)S(1)}, u32[]{:S(2)}, u32[]{:S(2)}) collective-permute-start(f32[35,16,128]{2,1,0:T(8,128)} %get-tuple-element.20), channel_id=1, source_target_pairs={{0,1},{1,2},{2,3},{3,4},{4,5},{5,6},{6,7},{7,0},{8,9},{9,10},{10,1... | collective-permute-start | bytes 860168 | tf_op jit(solution)/shard_map/ppermute | solution.py:450
  13.2 0.0 collective-permute-start.3
  13.2 0.0 copy-done.4
  13.2 0.1 copy.11
  13.3 0.1 eq.17
  13.4 1.2 %fusion.hot_far = bf16[1024,512]{1,0:T(8,128)(2,1)} fusion(s32[1024]{0:T(1024)S(1)} %eq.17), kind=kLoop, calls=%fused_computation.1 | loop fusion | flops 1048576 | bytes 1052672 | tf_op jit(solution)/shard_map/convert_element_type | solution.py:518
  14.7 2.5 %collective-permute-done.2.nlo = f32[35,16,128]{2,1,0:T(8,128)S(1)} collective-permute-done((f32[35,16,128]{2,1,0:T(8,128)}, f32[35,16,128]{2,1,0:T(8,128)S(1)}, u32[]{:S(2)}, u32[]{:S(2)}) %collective-permute-start.2) | collective-permute-done | bytes 286752 | tf_op jit(solution)/shard_map/ppermute | solution.py:450
  17.1 2.7 %collective-permute-done.3.nhi = f32[35,16,128]{2,1,0:T(8,128)S(1)} collective-permute-done((f32[35,16,128]{2,1,0:T(8,128)}, f32[35,16,128]{2,1,0:T(8,128)S(1)}, u32[]{:S(2)}, u32[]{:S(2)}) %collective-permute-start.3) | collective-permute-done | bytes 286752 | tf_op jit(solution)/shard_map/ppermute | solution.py:450
  19.8 0.1 collective-permute-start.4
  19.9 4.8 %collective-permute-start.5 = (f32[64,128]{1,0:T(8,128)S(1)}, f32[64,128]{1,0:T(8,128)S(1)}, u32[]{:S(2)}, u32[]{:S(2)}) collective-permute-start(f32[64,128]{1,0:T(8,128)S(1)} %get-tuple-element.23), channel_id=1, source_target_pairs={{8,0},{16,8},{24,16},{32,24},{40,32},{48,40},{56,48},{64,56},{72,6... | collective-permute-start | bytes 98312 | tf_op jit(solution)/shard_map/ppermute | solution.py:450
  24.7 0.1 add_convert_fusion.flags
  24.7 0.0 copy-done.3
  24.8 0.0 copy-done
  24.8 0.0 copy-done.2
  24.8 6.4 %inner.1 = (f32[8,16,32,128]{3,2,1,0:T(8,128)}, f32[8,192,128]{2,1,0:T(8,128)S(1)}, f32[8,192,128]{2,1,0:T(8,128)S(1)}, f32[5,288,128]{2,1,0:T(8,128)S(1)}, f32[3,512,128]{2,1,0:T(8,128)S(1)}) custom-call(f32[4]{0:T(128)S(1)} %add_convert_fusion.flags, f32[16]{0:T(128)S(1)} %copy-done.3, f32[8,16,32,128]{3,2,1,0:T(8,128)} %pot.5, ...), custom_call_target="tpu_custom_call" | custom-call | tf_op jit(solution)/shard_map/inner/pallas_call | solution.py:495
  31.2 0.0 collective-permute-done.4.clo
  31.2 0.0 collective-permute-done.5.chi
  31.2 0.0 collective-permute-done.wlo
  31.2 0.0 collective-permute-done.1.whi
  31.2 0.0 copy-start.5
  31.2 0.0 copy-start.1
  31.3 4.8 %outer.1 = (f32[8,16,32,128]{3,2,1,0:T(8,128)}, bf16[128,16,128]{2,1,0:T(8,128)(2,1)}) custom-call(f32[4]{0:T(128)S(1)} %add_convert_fusion.flags, f32[8,16,32,128]{3,2,1,0:T(8,128)} %pot.5, f32[35,32,128]{2,1,0:T(8,128)S(1)} %collective-permute-done.wlo, f32[35,32,128]{2,1,0:T(8,128)S(1)} %collective-permute-done.1.whi, ...), custom_call_target="tpu_custom_call", output_to_operand_aliasing={{0}: (13, {})} | custom-call | tf_op jit(solution)/shard_map/outer/pallas_call | solution.py:519
  36.1 4.6 %all-to-all-start = ((bf16[128,16,128]{2,1,0:T(8,128)(2,1)}), bf16[128,16,128]{2,1,0:T(8,128)(2,1)S(1)}, u32[]{:S(2)}, u32[]{:S(2)}) async-start(bf16[128,16,128]{2,1,0:T(8,128)(2,1)} %get-tuple-element.30), calls=%async_computation | async-start | bytes 1048576 | tf_op jit(solution)/shard_map/all_to_all | solution.py:537
  40.7 0.0 copy-done.5
  40.7 0.0 copy-done.1
  40.7 1.4 %flow.1.base = f32[3,256,128]{2,1,0:T(8,128)S(1)} custom-call(f32[4]{0:T(128)S(1)} %add_convert_fusion.flags, f32[3,256,128]{2,1,0:T(8,128)S(1)} %bitcast.9, f32[35,32,128]{2,1,0:T(8,128)S(1)} %collective-permute-done.wlo, f32[35,32,128]{2,1,0:T(8,128)S(1)} %collective-permute-done.1.whi, f32[35,16,128]{2,1,0:T(8,128)S(1)} %collective-permute-done.2.nlo, ...), custom_call_target="tpu_custom_call" | custom-call | tf_op jit(solution)/shard_map/flow/pallas_call | solution.py:542
  42.1 12.2 %all-to-all-done.got = bf16[128,16,128]{2,1,0:T(8,128)(2,1)S(1)} async-done(((bf16[128,16,128]{2,1,0:T(8,128)(2,1)}), bf16[128,16,128]{2,1,0:T(8,128)(2,1)S(1)}, u32[]{:S(2)}, u32[]{:S(2)}) %all-to-all-start) | async-done | bytes 524320 | tf_op jit(solution)/shard_map/all_to_all | solution.py:537
  54.4 0.1 broadcast_in_dim.2.column
  54.5 1.3 %last.1 = (bf16[3,256,128]{2,1,0:T(8,128)(2,1)}, f32[3,256,128]{2,1,0:T(8,128)}) custom-call(s32[256,128]{1,0:T(8,128)S(1)} %broadcast_in_dim.2.column, bf16[128,16,128]{2,1,0:T(8,128)(2,1)S(1)} %all-to-all-done.got, f32[3,256,128]{2,1,0:T(8,128)S(1)} %flow.1.base), custom_call_target="tpu_custom_call" | custom-call | tf_op jit(solution)/shard_map/last/pallas_call | solution.py:549
  (3 shorter events, 0.1 us)
Async XLA Ops:
  0.6 24.1 %copy-start.3 = (f32[16]{0:T(128)S(1)}, f32[16]{0:T(128)}, u32[]{:S(2)}) copy-start(f32[16]{0:T(128)} %rk.3) | copy-start | bytes 196
  0.6 24.1 %copy-start = (f32[3,16,32,128]{3,2,1,0:T(8,128)S(1)}, f32[3,16,32,128]{3,2,1,0:T(8,128)}, u32[]{:S(2)}) copy-start(f32[3,16,32,128]{3,2,1,0:T(8,128)} %src.3) | copy-start | bytes 2359300
  0.7 24.1 %copy-start.2 = (s32[16,32,128]{2,1,0:T(8,128)S(1)}, s32[16,32,128]{2,1,0:T(8,128)}, u32[]{:S(2)}) copy-start(s32[16,32,128]{2,1,0:T(8,128)} %lab.3) | copy-start | bytes 786436
  0.7 12.5 %copy-start.4 = (s32[1,128,4]{1,2,0:T(4,128)S(1)}, s32[1,128,4]{1,2,0:T(4,128)}, u32[]{:S(2)}) copy-start(s32[1,128,4]{1,2,0:T(4,128)} %param.11) | copy-start | bytes 6148
  4.8 26.5 %collective-permute-start = (f32[35,32,128]{2,1,0:T(8,128)}, f32[35,32,128]{2,1,0:T(8,128)S(1)}, u32[]{:S(2)}, u32[]{:S(2)}) collective-permute-start(f32[35,32,128]{2,1,0:T(8,128)} %get-tuple-element.18), channel_id=1, source_target_pairs={{0,8},{8,16},{16,24},{24,32},{32,40},{40,48},{48,56},{56,64},{64,7... | collective-permute-start | bytes 1720328 | tf_op jit(solution)/shard_map/ppermute | solution.py:450
  7.0 24.3 %collective-permute-start.1 = (f32[35,32,128]{2,1,0:T(8,128)}, f32[35,32,128]{2,1,0:T(8,128)S(1)}, u32[]{:S(2)}, u32[]{:S(2)}) collective-permute-start(f32[35,32,128]{2,1,0:T(8,128)} %get-tuple-element.19), channel_id=1, source_target_pairs={{8,0},{16,8},{24,16},{32,24},{40,32},{48,40},{56,48},{64,56},{72,6... | collective-permute-start | bytes 1720328 | tf_op jit(solution)/shard_map/ppermute | solution.py:450
  10.7 6.4 %collective-permute-start.2 = (f32[35,16,128]{2,1,0:T(8,128)}, f32[35,16,128]{2,1,0:T(8,128)S(1)}, u32[]{:S(2)}, u32[]{:S(2)}) collective-permute-start(f32[35,16,128]{2,1,0:T(8,128)} %get-tuple-element.20), channel_id=1, source_target_pairs={{0,1},{1,2},{2,3},{3,4},{4,5},{5,6},{6,7},{7,0},{8,9},{9,10},{10,1... | collective-permute-start | bytes 860168 | tf_op jit(solution)/shard_map/ppermute | solution.py:450
  13.2 6.6 %collective-permute-start.3 = (f32[35,16,128]{2,1,0:T(8,128)}, f32[35,16,128]{2,1,0:T(8,128)S(1)}, u32[]{:S(2)}, u32[]{:S(2)}) collective-permute-start(f32[35,16,128]{2,1,0:T(8,128)} %get-tuple-element.21), channel_id=1, source_target_pairs={{1,0},{2,1},{3,2},{4,3},{5,4},{6,5},{7,6},{0,7},{9,8},{10,9},{11,1... | collective-permute-start | bytes 860168 | tf_op jit(solution)/shard_map/ppermute | solution.py:450
  19.8 11.4 %collective-permute-start.4 = (f32[64,128]{1,0:T(8,128)S(1)}, f32[64,128]{1,0:T(8,128)S(1)}, u32[]{:S(2)}, u32[]{:S(2)}) collective-permute-start(f32[64,128]{1,0:T(8,128)S(1)} %get-tuple-element.22), channel_id=1, source_target_pairs={{0,8},{8,16},{16,24},{24,32},{32,40},{40,48},{48,56},{56,64},{64,7... | collective-permute-start | bytes 98312 | tf_op jit(solution)/shard_map/ppermute | solution.py:450
  19.9 11.3 %collective-permute-start.5 = (f32[64,128]{1,0:T(8,128)S(1)}, f32[64,128]{1,0:T(8,128)S(1)}, u32[]{:S(2)}, u32[]{:S(2)}) collective-permute-start(f32[64,128]{1,0:T(8,128)S(1)} %get-tuple-element.23), channel_id=1, source_target_pairs={{8,0},{16,8},{24,16},{32,24},{40,32},{48,40},{56,48},{64,56},{72,6... | collective-permute-start | bytes 98312 | tf_op jit(solution)/shard_map/ppermute | solution.py:450
  31.2 9.5 %copy-start.5 = (s32[1,256]{1,0:T(1,128)S(1)}, s32[1,256]{1,0:T(1,128)}, u32[]{:S(2)}) copy-start(s32[1,256]{1,0:T(1,128)} %param.12) | copy-start | bytes 3076
  31.2 9.5 %copy-start.1 = (f32[3,8,32,128]{3,2,1,0:T(8,128)S(1)}, f32[3,8,32,128]{3,2,1,0:T(8,128)}, u32[]{:S(2)}) copy-start(f32[3,8,32,128]{3,2,1,0:T(8,128)} %vel.1) | copy-start | bytes 1179652
  36.1 18.3 %all-to-all-start = ((bf16[128,16,128]{2,1,0:T(8,128)(2,1)}), bf16[128,16,128]{2,1,0:T(8,128)(2,1)S(1)}, u32[]{:S(2)}, u32[]{:S(2)}) async-start(bf16[128,16,128]{2,1,0:T(8,128)(2,1)} %get-tuple-element.30), calls=%async_computation | async-start | bytes 1048576 | tf_op jit(solution)/shard_map/all_to_all | solution.py:537
